TPU v7x, 256 devices: a whole 4x4x8 slice. The times are simulated.
256 devices in a mesh: col: 4 (over y), row: 64 (over x, z, core).
Axes of the slice: x: 4, y: 4, z: 8, core: 2. Of those that a mesh axis runs over, the one named last changes fastest.
Arguments:
- factor_blocks: bfloat16 [320, 17, 512, 512], P('row', None, None, 'col'), may hold values from -0.25 to 0.25
- block_scales: float32 [320, 17], P('row'), may hold values from 0.1 to 0.3
- dep_column: int32 [320, 17], P('row'), may hold values from 0 to 383, as said below
- dep_count: int32 [320], P('row'), may hold values from 1 to 17, as said below
- diag_inverse: bfloat16 [384, 512, 512], P('row', 'col'), may hold values from -0.25 to 0.25
- right_side: float32 [384, 512, 256], P('row', 'col'), may hold values from -6 to 6
Outputs:
- solution: bfloat16 [384, 512, 256], P('row', 'col')
Inputs may be any that keep to these rules, and one draw needn't show every extreme that they name: `dep_column`: A live entry (slot below dep_count of its row) names supernode shard * 6 + level with a level below its own row's level and a shard at most 4 away from the row's shard; the live entries of a row are distinct; entries past the count name the row's own shard at level 0 and are unused. `dep_count`: at least one, at most the number of possible supernodes within reach; some supernode uses all 17 slots.
All inputs are finite; a program needn't handle non-finite values.
Results may differ from a plain program's by a relative error of at most 0.0054.
Values may be sent and summed in bfloat16 or wider, within the bound.
No kernel may reach another device: no remote copies, remote signals or barrier semaphores. Data moves between devices by JAX's collectives and lax.ppermute only.
A program may use at most 128 MiB of HBM per device.

v0:
```python
import jax
import jax.numpy as jnp
from jax import lax
from jax.sharding import PartitionSpec as P

REACH = 4


def shifted(value, axis, steps):
    count = lax.axis_size(axis)
    initial, last = (max(0, -steps), min(count, count - steps))
    return lax.ppermute(value, axis, [(source, source + steps) for source in range(initial, last)])


def row_products(
    running_init,
    dep_row,
    stored,
    anchor,
    factor_blocks,
    block_scales,
    dep_column,
    dep_count,
    level_count,
):
    live_count = dep_count[dep_row]

    def add_slot(slot_index, running):
        column = dep_column[dep_row, slot_index]
        x_piece = stored[column % level_count, column // level_count - anchor]
        product = jnp.dot(
            factor_blocks[dep_row, slot_index], x_piece, preferred_element_type=jnp.float32
        )
        return running + block_scales[dep_row, slot_index] * product

    return lax.fori_loop(0, live_count, add_slot, running_init)


def per_device(factor_blocks, block_scales, dep_column, dep_count, diag_inverse, right_side):
    level_count = diag_inverse.shape[0]
    row_share = diag_inverse.shape[1]
    block_rows = diag_inverse.shape[2]
    rhs_width = right_side.shape[2]
    own_shard = lax.axis_index("row")
    own_col = lax.axis_index("col")
    stored = jnp.zeros((level_count, 2 * REACH + 1, row_share, rhs_width), jnp.bfloat16)
    anchor = own_shard - REACH
    empty = jnp.zeros((block_rows, rhs_width), jnp.float32)
    outputs = []
    for level_index in range(level_count):
        if level_index == 0:
            partial_value = empty
        else:
            partial_value = row_products(
                empty,
                level_index - 1,
                stored,
                anchor,
                factor_blocks,
                block_scales,
                dep_column,
                dep_count,
                level_count,
            )
        inverse_rows = diag_inverse[level_index]
        placed = lax.dynamic_update_slice(empty, right_side[level_index], (own_col * row_share, 0))
        reduced = lax.psum(partial_value - placed, "col")
        product = jnp.dot(
            inverse_rows.astype(jnp.float32), reduced, precision=lax.Precision.HIGHEST
        )
        solved = (-product).astype(jnp.bfloat16)
        outputs.append(solved)
        if level_index + 1 < level_count:
            stored = stored.at[level_index, REACH].set(solved)
            for offset in range(-REACH, REACH + 1):
                if offset != 0:
                    arrived = shifted(solved, "row", -offset)
                    stored = stored.at[level_index, offset + REACH].set(arrived)
    return jnp.stack(outputs, axis=0)


def solution(mesh):
    in_specs = (
        P("row", None, None, "col"),
        P("row", None),
        P("row", None),
        P("row"),
        P("row", "col", None),
        P("row", "col", None),
    )
    out_specs = P("row", "col", None)
    return jax.shard_map(
        per_device, mesh=mesh, in_specs=in_specs, out_specs=out_specs, check_vma=False
    )
```

profile of v0, /device:TPU:1, one launch (start us, length us, event | category | flops | bytes accessed | tf_op | source)
XLA Modules:
  0.0 1080.3 jit_solution(14872057060059243905)
XLA Ops:
  18.8 41.0 %all-reduce.7.cloned.1.call-done = f32[512,256]{1,0:T(8,128)} async-done(((f32[512,256]{1,0:T(8,128)}), f32[512,256]{1,0:T(8,128)}) %all-reduce.7.cloned.1.call-update) | async-done | bytes 524304 | tf_op jit(solution)/shard_map/psum | solution.py:67
  61.5 4.0 collective-permute-start
  65.5 8.2 collective-permute-start.1
  73.7 2.3 collective-permute-start.2
  78.1 2.2 collective-permute-start.4
  101.6 35.4 %while.105 = (s32[]{:T(128)}, f32[512,256]{1,0:T(8,128)S(1)}, s32[]{:T(128)}, f32[5,17]{1,0:T(8,128)S(1)}, bf16[5,17,512,128]{3,2,1,0:T(8,128)(2,1)}, /*index=5*...) while((s32[]{:T(128)}, f32[512,256]{1,0:T(8,128)S(1)}, ...), condition=%wide.region_9.0_spmd, body=%wide.region_8.0_spmd.sunk | while | flops 33816600 | bytes 1246102 | solution.py:36
  138.0 79.9 %all-reduce.9.cloned.1.call-done = f32[512,256]{1,0:T(8,128)} async-done(((f32[512,256]{1,0:T(8,128)}), f32[512,256]{1,0:T(8,128)}) %all-reduce.9.cloned.1.call-update) | async-done | bytes 524304 | tf_op jit(solution)/shard_map/psum | solution.py:67
  219.6 4.0 collective-permute-start.8
  224.2 8.2 collective-permute-start.9
  232.4 2.3 collective-permute-start.10
  234.7 2.1 collective-permute-start.11
  236.8 2.2 collective-permute-start.12
  251.8 92.1 %while.106 = (s32[]{:T(128)}, f32[512,256]{1,0:T(8,128)S(1)}, s32[]{:T(128)}, f32[5,17]{1,0:T(8,128)S(1)}, bf16[5,17,512,128]{3,2,1,0:T(8,128)(2,1)}, /*index=5*...) while((s32[]{:T(128)}, f32[512,256]{1,0:T(8,128)S(1)}, ...), condition=%wide.region_12.13_spmd, body=%wide.region_11.12_spmd.sunk | while | flops 33816600 | bytes 1246102 | solution.py:36
  344.9 86.4 %all-reduce.11.cloned.1.call-done = f32[512,256]{1,0:T(8,128)} async-done(((f32[512,256]{1,0:T(8,128)}), f32[512,256]{1,0:T(8,128)}) %all-reduce.11.cloned.1.call-update) | async-done | bytes 524304 | tf_op jit(solution)/shard_map/psum | solution.py:67
  432.9 4.0 collective-permute-start.16
  437.6 8.2 collective-permute-start.17
  445.8 2.3 collective-permute-start.18
  450.2 2.2 collective-permute-start.20
  465.2 108.1 %while.107 = (s32[]{:T(128)}, f32[512,256]{1,0:T(8,128)S(1)}, s32[]{:T(128)}, f32[5,17]{1,0:T(8,128)S(1)}, bf16[5,17,512,128]{3,2,1,0:T(8,128)(2,1)}, /*index=5*...) while((s32[]{:T(128)}, f32[512,256]{1,0:T(8,128)S(1)}, ...), condition=%wide.region_15.16_spmd, body=%wide.region_14.15_spmd.sunk | while | flops 33816600 | bytes 1246102 | solution.py:36
  574.3 71.0 %all-reduce.13.cloned.1.call-done = f32[512,256]{1,0:T(8,128)} async-done(((f32[512,256]{1,0:T(8,128)}), f32[512,256]{1,0:T(8,128)}) %all-reduce.13.cloned.1.call-update) | async-done | bytes 524304 | tf_op jit(solution)/shard_map/psum | solution.py:67
  647.0 4.0 collective-permute-start.24
  651.6 8.2 collective-permute-start.25
  659.8 2.3 collective-permute-start.26
  664.2 2.2 collective-permute-start.28
  679.2 106.2 %while.108 = (s32[]{:T(128)}, f32[512,256]{1,0:T(8,128)S(1)}, s32[]{:T(128)}, f32[5,17]{1,0:T(8,128)S(1)}, bf16[5,17,512,128]{3,2,1,0:T(8,128)(2,1)}, /*index=5*...) while((s32[]{:T(128)}, f32[512,256]{1,0:T(8,128)S(1)}, ...), condition=%wide.region_18.19_spmd, body=%wide.region_17.18_spmd.sunk | while | flops 33816600 | bytes 1246102 | solution.py:36
  786.4 70.8 %all-reduce.15.cloned.1.call-done = f32[512,256]{1,0:T(8,128)} async-done(((f32[512,256]{1,0:T(8,128)}), f32[512,256]{1,0:T(8,128)}) %all-reduce.15.cloned.1.call-update) | async-done | bytes 524304 | tf_op jit(solution)/shard_map/psum | solution.py:67
  858.8 4.0 collective-permute-start.32
  863.4 8.2 collective-permute-start.33
  871.6 2.3 collective-permute-start.34
  876.1 2.2 collective-permute-start.36
  891.0 115.1 %while.109 = (s32[]{:T(128)}, f32[512,256]{1,0:T(8,128)S(1)}, s32[]{:T(128)}, f32[5,17]{1,0:T(8,128)S(1)}, bf16[5,17,512,128]{3,2,1,0:T(8,128)(2,1)}, /*index=5*...) while((s32[]{:T(128)}, f32[512,256]{1,0:T(8,128)S(1)}, ...), condition=%wide.region_21.22_spmd, body=%wide.region_20.21_spmd.sunk | while | flops 33816600 | bytes 1246102 | solution.py:36
  1007.0 63.8 %all-reduce.17.cloned.1.call-done = f32[512,256]{1,0:T(8,128)} async-done(((f32[512,256]{1,0:T(8,128)}), f32[512,256]{1,0:T(8,128)}) %all-reduce.17.cloned.1.call-update) | async-done | bytes 524304 | tf_op jit(solution)/shard_map/psum | solution.py:67
  (353 shorter events, 297.3 us)
Async XLA Ops:
  6.5 53.3 %all-reduce.7.cloned.1.call-start = ((), (), s32[]{:S(2)}) async-start(), calls=%async_computation | async-start | bytes 1048576 | tf_op jit(solution)/shard_map/psum | solution.py:67
  8.4 209.5 %all-reduce.9.cloned.1.call-start = ((), (), s32[]{:S(2)}) async-start(), calls=%async_computation.1 | async-start | bytes 1048576 | tf_op jit(solution)/shard_map/psum | solution.py:67
  61.5 21.6 %collective-permute-start = (bf16[128,256]{0,1:T(8,128)(2,1)S(1)}, bf16[128,256]{0,1:T(8,128)(2,1)S(1)}, u32[]{:S(2)}, u32[]{:S(2)}) collective-permute-start(bf16[128,256]{0,1:T(8,128)(2,1)S(1)} %bitcast.315), channel_id=1, source_target_pairs={{0,4},{1,5},{2,6},{3,7},{4,8},{5,9},{6,10},{7,11},{8,12},{9,13},{1... | collective-permute-start | bytes 196616 | tf_op jit(solution)/shard_map/ppermute | solution.py:12
  65.5 18.9 %collective-permute-start.1 = (bf16[128,256]{0,1:T(8,128)(2,1)S(1)}, bf16[128,256]{0,1:T(8,128)(2,1)S(1)}, u32[]{:S(2)}, u32[]{:S(2)}) collective-permute-start(bf16[128,256]{0,1:T(8,128)(2,1)S(1)} %bitcast.316), channel_id=1, source_target_pairs={{0,3},{1,4},{2,5},{3,6},{4,7},{5,8},{6,9},{7,10},{8,11},{9,12},{10... | collective-permute-start | bytes 196616 | tf_op jit(solution)/shard_map/ppermute | solution.py:12
  73.7 13.3 %collective-permute-start.2 = (bf16[128,256]{0,1:T(8,128)(2,1)S(1)}, bf16[128,256]{0,1:T(8,128)(2,1)S(1)}, u32[]{:S(2)}, u32[]{:S(2)}) collective-permute-start(bf16[128,256]{0,1:T(8,128)(2,1)S(1)} %bitcast.317), channel_id=1, source_target_pairs={{0,2},{1,3},{2,4},{3,5},{4,6},{5,7},{6,8},{7,9},{8,10},{9,11},{10,... | collective-permute-start | bytes 196616 | tf_op jit(solution)/shard_map/ppermute | solution.py:12
  76.0 14.3 %collective-permute-start.3 = (bf16[128,256]{0,1:T(8,128)(2,1)S(1)}, bf16[128,256]{0,1:T(8,128)(2,1)S(1)}, u32[]{:S(2)}, u32[]{:S(2)}) collective-permute-start(bf16[128,256]{0,1:T(8,128)(2,1)S(1)} %bitcast.318), channel_id=1, source_target_pairs={{0,1},{1,2},{2,3},{3,4},{4,5},{5,6},{6,7},{7,8},{8,9},{9,10},{10,1... | collective-permute-start | bytes 196616 | tf_op jit(solution)/shard_map/ppermute | solution.py:12
  78.1 14.1 %collective-permute-start.4 = (bf16[128,256]{0,1:T(8,128)(2,1)S(1)}, bf16[128,256]{0,1:T(8,128)(2,1)S(1)}, u32[]{:S(2)}, u32[]{:S(2)}) collective-permute-start(bf16[128,256]{0,1:T(8,128)(2,1)S(1)} %bitcast.319), channel_id=1, source_target_pairs={{1,0},{2,1},{3,2},{4,3},{5,4},{6,5},{7,6},{8,7},{9,8},{10,9},{11,1... | collective-permute-start | bytes 196616 | tf_op jit(solution)/shard_map/ppermute | solution.py:12
  83.1 11.1 %collective-permute-start.5 = (bf16[128,256]{0,1:T(8,128)(2,1)S(1)}, bf16[128,256]{0,1:T(8,128)(2,1)S(1)}, u32[]{:S(2)}, u32[]{:S(2)}) collective-permute-start(bf16[128,256]{0,1:T(8,128)(2,1)S(1)} %bitcast.320), channel_id=1, source_target_pairs={{2,0},{3,1},{4,2},{5,3},{6,4},{7,5},{8,6},{9,7},{10,8},{11,9},{12,... | collective-permute-start | bytes 196616 | tf_op jit(solution)/shard_map/ppermute | solution.py:12
  84.5 11.6 %collective-permute-start.6 = (bf16[128,256]{0,1:T(8,128)(2,1)S(1)}, bf16[128,256]{0,1:T(8,128)(2,1)S(1)}, u32[]{:S(2)}, u32[]{:S(2)}) collective-permute-start(bf16[128,256]{0,1:T(8,128)(2,1)S(1)} %bitcast.321), channel_id=1, source_target_pairs={{3,0},{4,1},{5,2},{6,3},{7,4},{8,5},{9,6},{10,7},{11,8},{12,9},{13... | collective-permute-start | bytes 196616 | tf_op jit(solution)/shard_map/ppermute | solution.py:12
  87.0 10.8 %collective-permute-start.7 = (bf16[128,256]{0,1:T(8,128)(2,1)S(1)}, bf16[128,256]{0,1:T(8,128)(2,1)S(1)}, u32[]{:S(2)}, u32[]{:S(2)}) collective-permute-start(bf16[128,256]{0,1:T(8,128)(2,1)S(1)} %bitcast.322), channel_id=1, source_target_pairs={{4,0},{5,1},{6,2},{7,3},{8,4},{9,5},{10,6},{11,7},{12,8},{13,9},{1... | collective-permute-start | bytes 196616 | tf_op jit(solution)/shard_map/ppermute | solution.py:12
  137.9 293.4 %all-reduce.11.cloned.1.call-start = ((), (), s32[]{:S(2)}) async-start(), calls=%async_computation.2 | async-start | bytes 1048576 | tf_op jit(solution)/shard_map/psum | solution.py:67
  219.6 19.5 %collective-permute-start.8 = (bf16[128,256]{0,1:T(8,128)(2,1)S(1)}, bf16[128,256]{0,1:T(8,128)(2,1)S(1)}, u32[]{:S(2)}, u32[]{:S(2)}) collective-permute-start(bf16[128,256]{0,1:T(8,128)(2,1)S(1)} %bitcast.323), channel_id=1, source_target_pairs={{0,4},{1,5},{2,6},{3,7},{4,8},{5,9},{6,10},{7,11},{8,12},{9,13},{1... | collective-permute-start | bytes 196616 | tf_op jit(solution)/shard_map/ppermute | solution.py:12
  224.2 16.8 %collective-permute-start.9 = (bf16[128,256]{0,1:T(8,128)(2,1)S(1)}, bf16[128,256]{0,1:T(8,128)(2,1)S(1)}, u32[]{:S(2)}, u32[]{:S(2)}) collective-permute-start(bf16[128,256]{0,1:T(8,128)(2,1)S(1)} %bitcast.324), channel_id=1, source_target_pairs={{0,3},{1,4},{2,5},{3,6},{4,7},{5,8},{6,9},{7,10},{8,11},{9,12},{10... | collective-permute-start | bytes 196616 | tf_op jit(solution)/shard_map/ppermute | solution.py:12
  232.4 10.5 collective-permute-start.10
  234.7 10.1 collective-permute-start.11
  344.8 300.5 %all-reduce.13.cloned.1.call-start = ((), (), s32[]{:S(2)}) async-start(), calls=%async_computation.3 | async-start | bytes 1048576 | tf_op jit(solution)/shard_map/psum | solution.py:67
  432.9 19.5 %collective-permute-start.16 = (bf16[128,256]{0,1:T(8,128)(2,1)S(1)}, bf16[128,256]{0,1:T(8,128)(2,1)S(1)}, u32[]{:S(2)}, u32[]{:S(2)}) collective-permute-start(bf16[128,256]{0,1:T(8,128)(2,1)S(1)} %bitcast.331), channel_id=1, source_target_pairs={{0,4},{1,5},{2,6},{3,7},{4,8},{5,9},{6,10},{7,11},{8,12},{9,13},{1... | collective-permute-start | bytes 196616 | tf_op jit(solution)/shard_map/ppermute | solution.py:12
  437.6 16.8 %collective-permute-start.17 = (bf16[128,256]{0,1:T(8,128)(2,1)S(1)}, bf16[128,256]{0,1:T(8,128)(2,1)S(1)}, u32[]{:S(2)}, u32[]{:S(2)}) collective-permute-start(bf16[128,256]{0,1:T(8,128)(2,1)S(1)} %bitcast.332), channel_id=1, source_target_pairs={{0,3},{1,4},{2,5},{3,6},{4,7},{5,8},{6,9},{7,10},{8,11},{9,12},{10... | collective-permute-start | bytes 196616 | tf_op jit(solution)/shard_map/ppermute | solution.py:12
  445.8 10.5 collective-permute-start.18
  448.1 10.1 collective-permute-start.19
  450.2 8.6 collective-permute-start.20
  574.2 283.0 %all-reduce.15.cloned.1.call-start = ((), (), s32[]{:S(2)}) async-start(), calls=%async_computation.4 | async-start | bytes 1048576 | tf_op jit(solution)/shard_map/psum | solution.py:67
  647.0 19.5 %collective-permute-start.24 = (bf16[128,256]{0,1:T(8,128)(2,1)S(1)}, bf16[128,256]{0,1:T(8,128)(2,1)S(1)}, u32[]{:S(2)}, u32[]{:S(2)}) collective-permute-start(bf16[128,256]{0,1:T(8,128)(2,1)S(1)} %bitcast.339), channel_id=1, source_target_pairs={{0,4},{1,5},{2,6},{3,7},{4,8},{5,9},{6,10},{7,11},{8,12},{9,13},{1... | collective-permute-start | bytes 196616 | tf_op jit(solution)/shard_map/ppermute | solution.py:12
  651.6 16.8 %collective-permute-start.25 = (bf16[128,256]{0,1:T(8,128)(2,1)S(1)}, bf16[128,256]{0,1:T(8,128)(2,1)S(1)}, u32[]{:S(2)}, u32[]{:S(2)}) collective-permute-start(bf16[128,256]{0,1:T(8,128)(2,1)S(1)} %bitcast.340), channel_id=1, source_target_pairs={{0,3},{1,4},{2,5},{3,6},{4,7},{5,8},{6,9},{7,10},{8,11},{9,12},{10... | collective-permute-start | bytes 196616 | tf_op jit(solution)/shard_map/ppermute | solution.py:12
  659.8 10.5 collective-permute-start.26
  662.1 10.1 collective-permute-start.27
  786.2 284.6 %all-reduce.17.cloned.1.call-start = ((), (), s32[]{:S(2)}) async-start(), calls=%async_computation.5 | async-start | bytes 1048576 | tf_op jit(solution)/shard_map/psum | solution.py:67
  858.8 19.5 %collective-permute-start.32 = (bf16[128,256]{0,1:T(8,128)(2,1)S(1)}, bf16[128,256]{0,1:T(8,128)(2,1)S(1)}, u32[]{:S(2)}, u32[]{:S(2)}) collective-permute-start(bf16[128,256]{0,1:T(8,128)(2,1)S(1)} %bitcast.347), channel_id=1, source_target_pairs={{0,4},{1,5},{2,6},{3,7},{4,8},{5,9},{6,10},{7,11},{8,12},{9,13},{1... | collective-permute-start | bytes 196616 | tf_op jit(solution)/shard_map/ppermute | solution.py:12
  863.4 16.8 %collective-permute-start.33 = (bf16[128,256]{0,1:T(8,128)(2,1)S(1)}, bf16[128,256]{0,1:T(8,128)(2,1)S(1)}, u32[]{:S(2)}, u32[]{:S(2)}) collective-permute-start(bf16[128,256]{0,1:T(8,128)(2,1)S(1)} %bitcast.348), channel_id=1, source_target_pairs={{0,3},{1,4},{2,5},{3,6},{4,7},{5,8},{6,9},{7,10},{8,11},{9,12},{10... | collective-permute-start | bytes 196616 | tf_op jit(solution)/shard_map/ppermute | solution.py:12
  871.6 10.5 collective-permute-start.34
  873.9 10.1 collective-permute-start.35
  876.1 8.6 collective-permute-start.36
  (19 other events, 430.1 us)
Sparse Core Ops, SparseCore 0:
  9.7 50.1 all-reduce.6
  138.0 79.8 all-reduce.8
  344.9 86.3 all-reduce.10
  574.3 70.9 all-reduce.12
  786.4 70.7 all-reduce.14
  1007.1 63.6 all-reduce.16
where the time goes:
time: 1090 us; the launch traced here: 1080 us
  waiting for transfers between devices  428 us (39%)
  loops' own time  270 us (25%)
  matrix products  119 us (11%)
  starting transfers between devices  114 us (10%)
  local copies, waits for them, and re-layouts  74.8 us (7%)
  other arithmetic  60.6 us (6%)
  between operations  14.2 us (1%)
    psum x6, waiting for transfers between devices, per_device(): reduced = lax.psum(partial_value - placed, 'col')  413 us
    another operation x5, loops' own time, row_products(): return lax.fori_loop(0, live_count, add_slot, running_init)  270 us
    ppermute x40, starting transfers between devices, shifted(): lax.ppermute(value, axis, [(source, source + steps) for source in range(i...  113 us
    dot_general x60, matrix products, add_slot(): jnp.dot(factor_blocks[dep_row, slot_index], x_piece, preferred_element_ty...  109 us
    rem x60, other arithmetic, add_slot(): x_piece = stored[column % level_count, column // level_count - anchor]  39.2 us
    dynamic_slice x60, local copies, waits for them, and re-layouts, add_slot(): return running + block_scales[dep_row, slot_index] * product  38.7 us
  transfers between devices with their start and end apart: 46, of which 14 were waited for; matrix products, arithmetic and copies ran while one was open for 4% of the time, Pallas kernels for 0%

commit v1 on v0

v1 whole, which is shorter than its diff:
```python
import functools

import jax
import jax.numpy as jnp
from jax import lax
from jax.experimental import pallas as pl
from jax.experimental.pallas import tpu as pltpu
from jax.sharding import PartitionSpec as P

VMEM = pl.BlockSpec(memory_space=pltpu.VMEM)
SMEM = pl.BlockSpec(memory_space=pltpu.SMEM)
MIB = 2**20


def row_moves(count, delta):
    pairs = []
    for target in range(count):
        step = 2 * delta if target % 2 == 0 else -2 * delta
        pairs.append(((target + step) % count, target))
    return pairs


def swap_moves(count):
    return [(source, source ^ 1) for source in range(count)]


def col_moves(cols, rows, flip):
    pairs = []
    for col in range(cols):
        for row in range(rows):
            partner = col ^ 1 if (row % 2) ^ flip == 0 else cols - 1 - col
            pairs.append((col * rows + row, partner * rows + row))
    return pairs


def turn_moves(cols, rows, turn):
    pairs = []
    for col in range(cols):
        for row in range(rows):
            target = (col + (turn if row % 2 == 0 else -turn)) % cols
            pairs.append((col * rows + row, target * rows + row))
    return pairs


def split(value):
    high = value.astype(jnp.bfloat16)
    return high, (value - high.astype(jnp.float32)).astype(jnp.bfloat16)


def product(left, right):
    return jnp.dot(left, right, preferred_element_type=jnp.float32)


def exact_product(left, right):
    high, low = split(right)
    return product(left, high) + product(left, low)


def first_kernel(meta_ref, diag_ref, own_ref, *refs):
    out_ref = refs[-1]
    share = own_ref.shape[0]
    total = jnp.zeros(out_ref.shape, jnp.float32)
    for index, piece_ref in enumerate((own_ref, *refs[:-1])):
        start = pl.multiple_of(meta_ref[1 + index] * share, share)
        total += exact_product(diag_ref[0, :, pl.ds(start, share)], piece_ref[...])
    out_ref[...] = total.astype(out_ref.dtype)


def solve_kernel(level, diag_ref, sum_ref, far_ref, out_ref):
    residual = sum_ref[...] + far_ref[...].astype(jnp.float32)
    out_ref[...] = exact_product(diag_ref[level], residual).astype(out_ref.dtype)


def slots_kernel(level, level_count, newest, whole, *refs):
    meta_ref, column_ref, count_ref, scale_ref, factor_ref = refs[:5]
    sources = 1 if newest else level - 1
    piece_refs = refs[5 : 5 + 3 * sources]
    refs = refs[5 + 3 * sources :]
    if newest:
        right_ref, refs = refs[0], refs[1:]
        if level > 1:
            older_ref, refs = refs[0], refs[1:]
        if whole is not None:
            diag_ref, refs = refs[0], refs[1:]
            own_ref, refs = refs[0], refs[1:]
            send_refs, refs = refs[:3], refs[3:]
            sum_ref, stored_ref, list_ref = refs
        else:
            sum_ref, coarse_ref, stored_ref, list_ref = refs
    else:
        sum_ref, stored_ref, list_ref = refs
    dep_row = level - 1
    own_chip = meta_ref[0] // 2
    core = meta_ref[0] % 2

    def collect(slot, found):
        from_level = column_ref[dep_row, slot] % level_count
        wanted = from_level == level - 1 if newest else from_level < level - 1

        @pl.when(wanted)
        def _():
            list_ref[found] = slot

        return found + wanted.astype(jnp.int32)

    list_ref[0] = 0
    found = lax.fori_loop(0, count_ref[dep_row], collect, 0)
    list_ref[found] = list_ref[0]

    for source in range(sources):
        pair_ref, mine_ref, other_ref = piece_refs[3 * source : 3 * source + 3]
        stored_ref[source, 0:2] = pair_ref[...]
        stored_ref[source, 2:6] = mine_ref[...]
        stored_ref[source, 6:10] = other_ref[...]

    share = factor_ref.shape[3]
    sum_ref[...] = -older_ref[...] if newest and level > 1 else jnp.zeros_like(sum_ref)
    if newest:
        start = pl.multiple_of(meta_ref[1] * share, share)
        sum_ref[pl.ds(start, share), :] += right_ref[level]

    def slot_product(slot):
        column = column_ref[dep_row, slot]
        shard = column // level_count
        away = shard // 2 - own_chip
        forward = jnp.where(core == 0, away, -away)
        start = jnp.where(
            away == 0, 0, jnp.where(forward > 0, 2 * forward, 4 - 2 * forward)
        )
        piece = stored_ref[0 if newest else column % level_count, start + shard % 2]
        return product(factor_ref[dep_row, slot], piece)

    sign = -1.0 if newest else 1.0

    def add_two(index, carry):
        one, two = list_ref[2 * index], list_ref[2 * index + 1]
        scale_one = sign * scale_ref[dep_row, one]
        scale_two = jnp.where(2 * index + 1 < found, sign * scale_ref[dep_row, two], 0.0)
        sum_ref[...] += scale_one * slot_product(one) + scale_two * slot_product(two)
        return carry

    lax.fori_loop(0, (found + 1) // 2, add_two, 0)
    if newest and whole is None:
        coarse_ref[...] = sum_ref[...].astype(coarse_ref.dtype)
    elif newest:
        high, low = split(sum_ref[...])
        for index in range(4):
            start = pl.multiple_of(meta_ref[1 + index] * share, share)
            block = diag_ref[whole, pl.ds(start, share), :]
            part = product(block, high) + product(block, low)
            if index == 0:
                own_ref[...] = part
            else:
                send_refs[index - 1][...] = part.astype(jnp.bfloat16)


def per_device(factor_blocks, block_scales, dep_column, dep_count, diag_inverse, right_side):
    level_count, share, block_rows = diag_inverse.shape
    slots = factor_blocks.shape[1]
    width = right_side.shape[2]
    rows, cols = lax.axis_size("row"), lax.axis_size("col")
    shard = lax.axis_index("row").astype(jnp.int32)
    col = lax.axis_index("col").astype(jnp.int32)
    even = shard % 2 == 0
    turn = jnp.where(even, 1, -1)
    turns = (2, 1, 3)
    targets = [(col + turn * step) % cols for step in turns]
    origins = [(col - turn * step) % cols for step in turns]
    out_meta = jnp.stack([shard, col, *targets])
    in_meta = jnp.stack([shard, col, *origins])
    tables = (dep_column, dep_count, block_scales)
    solved_shape = jax.ShapeDtypeStruct((share, width), jnp.bfloat16)
    wide = jax.ShapeDtypeStruct((block_rows, width), jnp.float32)

    def call(body, out_shape, smem_count, operands, limit, scratch=(), flops=2**27, name=None):
        return pl.pallas_call(
            body,
            out_shape=out_shape,
            in_specs=[SMEM] * smem_count + [VMEM] * (len(operands) - smem_count),
            out_specs=jax.tree.map(lambda _: VMEM, out_shape),
            scratch_shapes=list(scratch),
            cost_estimate=pl.CostEstimate(flops=flops, bytes_accessed=2 * MIB, transcendentals=0),
            compiler_params=pltpu.CompilerParams(vmem_limit_bytes=limit),
            name=name,
        )(*operands)

    def slots_call(level, newest, whole, pieces, extra, out_shape, scratch=()):
        sources = 1 if newest else level - 1
        return call(
            functools.partial(slots_kernel, level, level_count, newest, whole),
            out_shape,
            4,
            (out_meta, *tables, factor_blocks, *pieces, *extra),
            18 * MIB,
            (
                *scratch,
                pltpu.VMEM((sources, 10, share, width), jnp.bfloat16),
                pltpu.SMEM((slots + 1,), jnp.int32),
            ),
            flops=8 * 2 * block_rows * share * width,
            name=("new" if newest else "old") + "_slots",
        )

    def along_col(value, flip):
        return lax.ppermute(value, ("col", "row"), col_moves(cols, rows, flip))

    def around_col(value, step):
        return lax.ppermute(value, ("col", "row"), turn_moves(cols, rows, step))

    def spread(solved):
        other = lax.ppermute(solved, "row", swap_moves(rows))
        pair = jnp.where(even, jnp.stack([solved, other]), jnp.stack([other, solved]))
        far = lax.ppermute(pair, "row", row_moves(rows, 2))
        near = lax.ppermute(pair, "row", row_moves(rows, 1))
        return pair, near, far

    def share_out(pair, near, far):
        mine = jnp.concatenate([near, far], axis=0)
        theirs = lax.ppermute(mine, "row", swap_moves(rows))
        return [pair, mine, theirs]

    gathered = lax.all_gather(diag_inverse[2:], "col", axis=1, tiled=True)
    outputs = []
    pieces = []
    for level in range(level_count):
        if level == 0:
            own = right_side[0]
            arrived = [around_col(own, step) for step in turns]
            solved = call(
                first_kernel,
                solved_shape,
                1,
                (in_meta, diag_inverse, own, *arrived),
                4 * MIB,
                name="first_solve",
            )
        else:
            extra = [right_side]
            if level > 1:
                extra.append(older)
            newest = pieces[level - 1]
            if level == 1:
                coarse_shape = jax.ShapeDtypeStruct((block_rows, width), jnp.bfloat16)
                exact, coarse = slots_call(1, True, None, newest, extra, [wide, coarse_shape])
                total = exact + along_col(coarse, 0).astype(jnp.float32)
                arrived = along_col(total.astype(jnp.bfloat16), 1)
                solved = call(
                    functools.partial(solve_kernel, level),
                    solved_shape,
                    0,
                    (diag_inverse, total, arrived),
                    4 * MIB,
                    name="solve",
                )
            else:
                own_shape = jax.ShapeDtypeStruct((share, width), jnp.float32)
                own, *parts = slots_call(
                    level,
                    True,
                    level - 2,
                    newest,
                    [*extra, gathered],
                    [own_shape] + [solved_shape] * 3,
                    [pltpu.VMEM((block_rows, width), jnp.float32)],
                )
                arrived = [around_col(part, step) for part, step in zip(parts, turns)]
                total = own
                for part in arrived:
                    total = total + part.astype(jnp.float32)
                solved = total.astype(jnp.bfloat16)
        outputs.append(solved)
        if level + 1 < level_count:
            pair, near, far = spread(solved)
            if level > 0:
                older_pieces = [x for trio in pieces for x in trio]
                pair, older_pieces = lax.optimization_barrier((pair, older_pieces))
                older = slots_call(level + 1, False, None, older_pieces, [], wide)
                near, far, older = lax.optimization_barrier((near, far, older))
            pieces.append(share_out(pair, near, far))
    return jnp.stack(outputs, axis=0)


def solution(mesh):
    in_specs = (
        P("row", None, None, "col"),
        P("row", None),
        P("row", None),
        P("row"),
        P("row", "col", None),
        P("row", "col", None),
    )
    return jax.shard_map(
        per_device, mesh=mesh, in_specs=in_specs, out_specs=P("row", "col", None), check_vma=False
    )
```

time: 1090 us -> 174 us (0.16)
  waiting for transfers between devices: 428 us -> 85.1 us
  loops' own time: 270 us -> 0 us
  matrix products: 119 us -> 0 us
  starting transfers between devices: 114 us -> 34.2 us
  other arithmetic: 60.6 us -> 0.89 us
  local copies, waits for them, and re-layouts: 74.8 us -> 17.4 us
  Pallas kernels: 0 us -> 22.4 us
    psum x6 -> x0, waiting for transfers between devices: 413 us -> none  [per_device(): reduced = lax.psum(partial_value - placed, 'col')]
    another operation x5 -> x0, loops' own time: 270 us -> none  [row_products(): return lax.fori_loop(0, live_count, add_slot, running_init)]
    dot_general x66 -> x0, matrix products: 119 us -> none  [the longest x60 109 us: add_slot(): jnp.dot(factor_blocks[dep_row, slot_index], x_piece, preferred_element_ty...]
    ppermute x40 -> x37, starting transfers between devices: 113 us -> 34.2 us  [the longest x15 16.3 us: around_col(): return lax.ppermute(value, ('col', 'row'), turn_moves(cols, rows, step))]
    ppermute x40 -> x37, waiting for transfers between devices: 15.3 us -> 85.1 us  [the longest x5 24.3 us: spread(): near = lax.ppermute(pair, 'row', row_moves(rows, 1))]
    rem x60 -> x0, other arithmetic: 39.2 us -> none  [add_slot(): x_piece = stored[column % level_count, column // level_count - anchor]]
    dynamic_slice x60 -> x0, local copies, waits for them, and re-layouts: 38.7 us -> none  [add_slot(): return running + block_scales[dep_row, slot_index] * product]
    scatter x38 -> x0, local copies, waits for them, and re-layouts: 23.8 us -> none  [the longest x34 21.3 us: per_device(): stored = stored.at[level_index, offset + REACH].set(arrived)]
  transfers between devices with their start and end apart: 46 -> 38, of which waited for: 14 -> 37; matrix products, arithmetic and copies ran while one was open for 4% -> 1% of each run, Pallas kernels for 0% -> 7%
where the time goes in v1:
time: 174 us
  waiting for transfers between devices  85.1 us (49%)
  starting transfers between devices  34.2 us (20%)
  Pallas kernels  22.4 us (13%)
  local copies, waits for them, and re-layouts  17.4 us (10%)
  between operations  13.7 us (8%)
    ppermute x5, waiting for transfers between devices, spread(): near = lax.ppermute(pair, 'row', row_moves(rows, 1))  24.3 us
    ppermute x15, waiting for transfers between devices, around_col(): return lax.ppermute(value, ('col', 'row'), turn_moves(cols, rows, step))  23.8 us
    pallas_call x11, Pallas kernels, call(): pl.pallas_call(body, out_shape=out_shape, in_specs=[SMEM] * smem_count +...  22.4 us
    ppermute x5, waiting for transfers between devices, spread(): far = lax.ppermute(pair, 'row', row_moves(rows, 2))  16.6 us
    ppermute x15, starting transfers between devices, around_col(): return lax.ppermute(value, ('col', 'row'), turn_moves(cols, rows, step))  16.3 us
    unnamed x37, local copies, waits for them, and re-layouts  14.4 us
    ppermute x2, waiting for transfers between devices, along_col(): return lax.ppermute(value, ('col', 'row'), col_moves(cols, rows, flip))  9.87 us
    ppermute x5, waiting for transfers between devices, share_out(): theirs = lax.ppermute(mine, 'row', swap_moves(rows))  6.1 us
  transfers between devices with their start and end apart: 38, of which 37 were waited for; matrix products, arithmetic and copies ran while one was open for 1% of the time, Pallas kernels for 7%

profile of v1, /device:TPU:1, one launch (start us, length us, event | category | flops | bytes accessed | tf_op | source)
XLA Modules:
  0.0 173.8 jit_solution(16929009844841443986)
XLA Ops:
  6.5 1.9 %slice.7 = bf16[4,128,512]{2,1,0:T(8,128)(2,1)} slice(bf16[6,128,512]{2,1,0:T(8,128)(2,1)} %diag_ref.3), slice={[2:6], [0:128], [0:512]} | slice | bytes 1048576 | tf_op jit(solution)/shard_map/slice | solution.py:222
  9.4 3.8 %collective-permute-start = (f32[128,256]{1,0:T(8,128)S(1)}, f32[128,256]{1,0:T(8,128)S(1)}, u32[]{:S(2)}, u32[]{:S(2)}) collective-permute-start(f32[128,256]{1,0:T(8,128)S(1)} %slice_bitcast_fusion.own_ref), channel_id=1, source_target_pairs={{0,128},{1,129},{2,130},{3,131},{4,132},{5,133},{6,134},{7,135},{8... | collective-permute-start | bytes 393224 | tf_op jit(solution)/shard_map/ppermute | solution.py:208
  15.6 3.7 %collective-permute-done.1.refs_1_ = f32[128,256]{1,0:T(8,128)S(1)} collective-permute-done((f32[128,256]{1,0:T(8,128)S(1)}, f32[128,256]{1,0:T(8,128)S(1)}, u32[]{:S(2)}, u32[]{:S(2)}) %collective-permute-start.1) | collective-permute-done | bytes 131104 | tf_op jit(solution)/shard_map/ppermute | solution.py:208
  19.4 2.2 %collective-permute-done.2.refs_2_ = f32[128,256]{1,0:T(8,128)S(1)} collective-permute-done((f32[128,256]{1,0:T(8,128)S(1)}, f32[128,256]{1,0:T(8,128)S(1)}, u32[]{:S(2)}, u32[]{:S(2)}) %collective-permute-start.2) | collective-permute-done | bytes 131104 | tf_op jit(solution)/shard_map/ppermute | solution.py:208
  25.9 3.0 %collective-permute-start.5 = (bf16[2,128,256]{2,1,0:T(8,128)(2,1)S(1)}, bf16[2,128,256]{2,1,0:T(8,128)(2,1)S(1)}, u32[]{:S(2)}, u32[]{:S(2)}) collective-permute-start(bf16[2,128,256]{2,1,0:T(8,128)(2,1)S(1)} %maximum_select_fusion.refs_5_), channel_id=1, source_target_pairs={{4,0},{61,1},{6,2},{63,3},{8,4},{1,5},{10,6},{3,7},{12,8},{5,9},{1... | collective-permute-start | bytes 393224 | tf_op jit(solution)/shard_map/ppermute | solution.py:213
  28.9 5.5 %collective-permute-done.4 = bf16[2,128,256]{2,1,0:T(8,128)(2,1)S(1)} collective-permute-done((bf16[2,128,256]{2,1,0:T(8,128)(2,1)S(1)}, bf16[2,128,256]{2,1,0:T(8,128)(2,1)S(1)}, u32[]{:S(2)}, u32[]{:S(2)}) %collective-permute-start.4) | collective-permute-done | bytes 131104 | tf_op jit(solution)/shard_map/ppermute | solution.py:214
  34.4 3.1 %collective-permute-done.5 = bf16[2,128,256]{2,1,0:T(8,128)(2,1)S(1)} collective-permute-done((bf16[2,128,256]{2,1,0:T(8,128)(2,1)S(1)}, bf16[2,128,256]{2,1,0:T(8,128)(2,1)S(1)}, u32[]{:S(2)}, u32[]{:S(2)}) %collective-permute-start.5) | collective-permute-done | bytes 131104 | tf_op jit(solution)/shard_map/ppermute | solution.py:213
  39.9 4.2 %copy-done = bf16[5,17,512,128]{3,2,1,0:T(8,128)(2,1)S(1)} copy-done((bf16[5,17,512,128]{3,2,1,0:T(8,128)(2,1)S(1)}, bf16[5,17,512,128]{3,2,1,0:T(8,128)(2,1)}, u32[]{:S(2)}) %copy-start) | copy-done | bytes 11141144
  47.3 1.8 %new_slots.5 = (f32[512,256]{1,0:T(8,128)S(1)}, bf16[512,256]{1,0:T(8,128)(2,1)S(1)}) custom-call(s32[5]{0:T(128)S(1)} %stack.123.refs_0_, s32[5,17]{1,0:T(8,128)S(1)} %copy-done.8, s32[5]{0:T(128)S(1)} %copy-done.12, f32[5,17]{1,0:T(8,128)S(1)} %copy-done.10, bf16[5,17,512,128]{3,2,1,0:T(8,128)(2,1)S(1)} %copy-done, ...), custom_call_target="tpu_custom_call" | custom-call | flops 268435456 | bytes 2097152 | tf_op jit(solution)/shard_map/new_slots/pallas_call | solution.py:176
  49.2 2.2 %collective-permute-start.7 = (bf16[512,256]{1,0:T(8,128)(2,1)S(1)}, bf16[512,256]{1,0:T(8,128)(2,1)S(1)}, u32[]{:S(2)}, u32[]{:S(2)}) collective-permute-start(bf16[512,256]{1,0:T(8,128)(2,1)S(1)} %get-tuple-element.70), channel_id=1, source_target_pairs={{0,64},{1,193},{2,66},{3,195},{4,68},{5,197},{6,70},{7,199},{8,72}... | collective-permute-start | bytes 786440 | tf_op jit(solution)/shard_map/ppermute | solution.py:205
  51.3 4.4 %collective-permute-done.7 = bf16[512,256]{1,0:T(8,128)(2,1)S(1)} collective-permute-done((bf16[512,256]{1,0:T(8,128)(2,1)S(1)}, bf16[512,256]{1,0:T(8,128)(2,1)S(1)}, u32[]{:S(2)}, u32[]{:S(2)}) %collective-permute-start.7) | collective-permute-done | bytes 262176 | tf_op jit(solution)/shard_map/ppermute | solution.py:205
  55.9 5.5 %collective-permute-done.8.far_ref = bf16[512,256]{1,0:T(8,128)(2,1)S(1)} collective-permute-done((bf16[512,256]{1,0:T(8,128)(2,1)S(1)}, bf16[512,256]{1,0:T(8,128)(2,1)S(1)}, u32[]{:S(2)}, u32[]{:S(2)}) %collective-permute-start.8) | collective-permute-done | bytes 262176 | tf_op jit(solution)/shard_map/ppermute | solution.py:205
  61.7 2.2 %collective-permute-start.9 = (bf16[128,256]{1,0:T(8,128)(2,1)S(1)}, bf16[128,256]{1,0:T(8,128)(2,1)S(1)}, u32[]{:S(2)}, u32[]{:S(2)}) collective-permute-start(bf16[128,256]{1,0:T(8,128)(2,1)S(1)} %solve.1), channel_id=1, source_target_pairs={{0,1},{1,0},{2,3},{3,2},{4,5},{5,4},{6,7},{7,6},{8,9},{9,8},{10,11... | collective-permute-start | bytes 196616 | tf_op jit(solution)/shard_map/ppermute | solution.py:211
  67.6 5.2 %collective-permute-done.10 = bf16[2,128,256]{2,1,0:T(8,128)(2,1)S(1)} collective-permute-done((bf16[2,128,256]{2,1,0:T(8,128)(2,1)S(1)}, bf16[2,128,256]{2,1,0:T(8,128)(2,1)S(1)}, u32[]{:S(2)}, u32[]{:S(2)}) %collective-permute-start.10) | collective-permute-done | bytes 131104 | tf_op jit(solution)/shard_map/ppermute | solution.py:214
  72.8 4.0 %collective-permute-done.11 = bf16[2,128,256]{2,1,0:T(8,128)(2,1)S(1)} collective-permute-done((bf16[2,128,256]{2,1,0:T(8,128)(2,1)S(1)}, bf16[2,128,256]{2,1,0:T(8,128)(2,1)S(1)}, u32[]{:S(2)}, u32[]{:S(2)}) %collective-permute-start.11) | collective-permute-done | bytes 131104 | tf_op jit(solution)/shard_map/ppermute | solution.py:213
  78.5 4.2 %copy-done.1 = bf16[5,17,512,128]{3,2,1,0:T(8,128)(2,1)S(1)} copy-done((bf16[5,17,512,128]{3,2,1,0:T(8,128)(2,1)S(1)}, bf16[5,17,512,128]{3,2,1,0:T(8,128)(2,1)}, u32[]{:S(2)}) %copy-start.1) | copy-done | bytes 11141144
  84.3 2.4 %new_slots.6 = (f32[128,256]{1,0:T(8,128)S(1)}, bf16[128,256]{1,0:T(8,128)(2,1)S(1)}, bf16[128,256]{1,0:T(8,128)(2,1)S(1)}, bf16[128,256]{1,0:T(8,128)(2,1)S(1)}) custom-call(s32[5]{0:T(128)S(1)} %stack.123.refs_0_, s32[5,17]{1,0:T(8,128)S(1)} %copy-done.9, s32[5]{0:T(128)S(1)} %copy-done.13, f32[5,17]{1,0:T(8,128)S(1)} %copy-done.11, ...), custom_call_target="tpu_custom_call" | custom-call | flops 268435456 | bytes 2097152 | tf_op jit(solution)/shard_map/new_slots/pallas_call | solution.py:176
  89.4 2.3 %collective-permute-done.13 = bf16[128,256]{1,0:T(8,128)(2,1)S(1)} collective-permute-done((bf16[128,256]{1,0:T(8,128)(2,1)S(1)}, bf16[128,256]{1,0:T(8,128)(2,1)S(1)}, u32[]{:S(2)}, u32[]{:S(2)}) %collective-permute-start.13) | collective-permute-done | bytes 65568 | tf_op jit(solution)/shard_map/ppermute | solution.py:208
  95.7 2.4 %old_slots.5.refs_9_ = f32[512,256]{1,0:T(8,128)S(1)} custom-call(s32[5]{0:T(128)S(1)} %stack.123.refs_0_, s32[5,17]{1,0:T(8,128)S(1)} %copy-done.9, s32[5]{0:T(128)S(1)} %copy-done.13, f32[5,17]{1,0:T(8,128)S(1)} %copy-done.11, bf16[5,17,512,128]{3,2,1,0:T(8,128)(2,1)S(1)} %copy-done.1, bf16[2,128,256]{2,1,0:T(8,128)(2,1)S(1)} %maximum_select_fusion.refs_5_, ...), custom_call_target="tpu_custom_call" | custom-call | flops 268435456 | bytes 2097152 | tf_op jit(solution)/shard_map/old_slots/pallas_call | solution.py:176
  98.1 4.8 %collective-permute-done.17 = bf16[2,128,256]{2,1,0:T(8,128)(2,1)S(1)} collective-permute-done((bf16[2,128,256]{2,1,0:T(8,128)(2,1)S(1)}, bf16[2,128,256]{2,1,0:T(8,128)(2,1)S(1)}, u32[]{:S(2)}, u32[]{:S(2)}) %collective-permute-start.17) | collective-permute-done | bytes 131104 | tf_op jit(solution)/shard_map/ppermute | solution.py:214
  102.9 2.7 %collective-permute-done.18 = bf16[2,128,256]{2,1,0:T(8,128)(2,1)S(1)} collective-permute-done((bf16[2,128,256]{2,1,0:T(8,128)(2,1)S(1)}, bf16[2,128,256]{2,1,0:T(8,128)(2,1)S(1)}, u32[]{:S(2)}, u32[]{:S(2)}) %collective-permute-start.18) | collective-permute-done | bytes 131104 | tf_op jit(solution)/shard_map/ppermute | solution.py:213
  108.4 2.5 %new_slots.7 = (f32[128,256]{1,0:T(8,128)S(1)}, bf16[128,256]{1,0:T(8,128)(2,1)S(1)}, bf16[128,256]{1,0:T(8,128)(2,1)S(1)}, bf16[128,256]{1,0:T(8,128)(2,1)S(1)}) custom-call(s32[5]{0:T(128)S(1)} %stack.123.refs_0_, s32[5,17]{1,0:T(8,128)S(1)} %copy-done.9, s32[5]{0:T(128)S(1)} %copy-done.13, f32[5,17]{1,0:T(8,128)S(1)} %copy-done.11, ...), custom_call_target="tpu_custom_call" | custom-call | flops 268435456 | bytes 2097152 | tf_op jit(solution)/shard_map/new_slots/pallas_call | solution.py:176
  120.9 2.8 %old_slots.6.refs_9_ = f32[512,256]{1,0:T(8,128)S(1)} custom-call(s32[5]{0:T(128)S(1)} %stack.123.refs_0_, s32[5,17]{1,0:T(8,128)S(1)} %copy-done.9, s32[5]{0:T(128)S(1)} %copy-done.13, f32[5,17]{1,0:T(8,128)S(1)} %copy-done.11, bf16[5,17,512,128]{3,2,1,0:T(8,128)(2,1)S(1)} %copy-done.1, bf16[2,128,256]{2,1,0:T(8,128)(2,1)S(1)} %maximum_select_fusion.refs_5_, ...), custom_call_target="tpu_custom_call" | custom-call | flops 268435456 | bytes 2097152 | tf_op jit(solution)/shard_map/old_slots/pallas_call | solution.py:176
  123.7 4.5 %collective-permute-done.24 = bf16[2,128,256]{2,1,0:T(8,128)(2,1)S(1)} collective-permute-done((bf16[2,128,256]{2,1,0:T(8,128)(2,1)S(1)}, bf16[2,128,256]{2,1,0:T(8,128)(2,1)S(1)}, u32[]{:S(2)}, u32[]{:S(2)}) %collective-permute-start.24) | collective-permute-done | bytes 131104 | tf_op jit(solution)/shard_map/ppermute | solution.py:214
  128.2 4.0 %collective-permute-done.25 = bf16[2,128,256]{2,1,0:T(8,128)(2,1)S(1)} collective-permute-done((bf16[2,128,256]{2,1,0:T(8,128)(2,1)S(1)}, bf16[2,128,256]{2,1,0:T(8,128)(2,1)S(1)}, u32[]{:S(2)}, u32[]{:S(2)}) %collective-permute-start.25) | collective-permute-done | bytes 131104 | tf_op jit(solution)/shard_map/ppermute | solution.py:213
  133.8 2.5 %new_slots.8 = (f32[128,256]{1,0:T(8,128)S(1)}, bf16[128,256]{1,0:T(8,128)(2,1)S(1)}, bf16[128,256]{1,0:T(8,128)(2,1)S(1)}, bf16[128,256]{1,0:T(8,128)(2,1)S(1)}) custom-call(s32[5]{0:T(128)S(1)} %stack.123.refs_0_, s32[5,17]{1,0:T(8,128)S(1)} %copy-done.9, s32[5]{0:T(128)S(1)} %copy-done.13, f32[5,17]{1,0:T(8,128)S(1)} %copy-done.11, ...), custom_call_target="tpu_custom_call" | custom-call | flops 268435456 | bytes 2097152 | tf_op jit(solution)/shard_map/new_slots/pallas_call | solution.py:176
  138.7 2.7 %collective-permute-done.27 = bf16[128,256]{1,0:T(8,128)(2,1)S(1)} collective-permute-done((bf16[128,256]{1,0:T(8,128)(2,1)S(1)}, bf16[128,256]{1,0:T(8,128)(2,1)S(1)}, u32[]{:S(2)}, u32[]{:S(2)}) %collective-permute-start.27) | collective-permute-done | bytes 65568 | tf_op jit(solution)/shard_map/ppermute | solution.py:208
  145.0 2.8 %old_slots.7.refs_9_ = f32[512,256]{1,0:T(8,128)S(1)} custom-call(s32[5]{0:T(128)S(1)} %stack.123.refs_0_, s32[5,17]{1,0:T(8,128)S(1)} %copy-done.9, s32[5]{0:T(128)S(1)} %copy-done.13, f32[5,17]{1,0:T(8,128)S(1)} %copy-done.11, bf16[5,17,512,128]{3,2,1,0:T(8,128)(2,1)S(1)} %copy-done.1, bf16[2,128,256]{2,1,0:T(8,128)(2,1)S(1)} %maximum_select_fusion.refs_5_, ...), custom_call_target="tpu_custom_call" | custom-call | flops 268435456 | bytes 2097152 | tf_op jit(solution)/shard_map/old_slots/pallas_call | solution.py:176
  147.8 4.2 %collective-permute-done.31 = bf16[2,128,256]{2,1,0:T(8,128)(2,1)S(1)} collective-permute-done((bf16[2,128,256]{2,1,0:T(8,128)(2,1)S(1)}, bf16[2,128,256]{2,1,0:T(8,128)(2,1)S(1)}, u32[]{:S(2)}, u32[]{:S(2)}) %collective-permute-start.31) | collective-permute-done | bytes 131104 | tf_op jit(solution)/shard_map/ppermute | solution.py:214
  152.0 2.8 %collective-permute-done.32 = bf16[2,128,256]{2,1,0:T(8,128)(2,1)S(1)} collective-permute-done((bf16[2,128,256]{2,1,0:T(8,128)(2,1)S(1)}, bf16[2,128,256]{2,1,0:T(8,128)(2,1)S(1)}, u32[]{:S(2)}, u32[]{:S(2)}) %collective-permute-start.32) | collective-permute-done | bytes 131104 | tf_op jit(solution)/shard_map/ppermute | solution.py:213
  156.5 2.5 %new_slots.9 = (f32[128,256]{1,0:T(8,128)S(1)}, bf16[128,256]{1,0:T(8,128)(2,1)S(1)}, bf16[128,256]{1,0:T(8,128)(2,1)S(1)}, bf16[128,256]{1,0:T(8,128)(2,1)S(1)}) custom-call(s32[5]{0:T(128)S(1)} %stack.123.refs_0_, s32[5,17]{1,0:T(8,128)S(1)} %copy-done.9, s32[5]{0:T(128)S(1)} %copy-done.13, f32[5,17]{1,0:T(8,128)S(1)} %copy-done.11, ...), custom_call_target="tpu_custom_call" | custom-call | flops 268435456 | bytes 2097152 | tf_op jit(solution)/shard_map/new_slots/pallas_call | solution.py:176
  162.0 2.1 %collective-permute-done.34 = bf16[128,256]{1,0:T(8,128)(2,1)S(1)} collective-permute-done((bf16[128,256]{1,0:T(8,128)(2,1)S(1)}, bf16[128,256]{1,0:T(8,128)(2,1)S(1)}, u32[]{:S(2)}, u32[]{:S(2)}) %collective-permute-start.34) | collective-permute-done | bytes 65568 | tf_op jit(solution)/shard_map/ppermute | solution.py:208
  (112 shorter events, 55.3 us)
Async XLA Ops:
  6.5 71.9 %all-gather.2.cloned.1.call-start = ((), (), s32[]{:S(2)}) async-start(), calls=%async_computation | async-start | bytes 2621440 | tf_op jit(solution)/shard_map/all_gather | solution.py:222
  9.4 6.2 %collective-permute-start = (f32[128,256]{1,0:T(8,128)S(1)}, f32[128,256]{1,0:T(8,128)S(1)}, u32[]{:S(2)}, u32[]{:S(2)}) collective-permute-start(f32[128,256]{1,0:T(8,128)S(1)} %slice_bitcast_fusion.own_ref), channel_id=1, source_target_pairs={{0,128},{1,129},{2,130},{3,131},{4,132},{5,133},{6,134},{7,135},{8... | collective-permute-start | bytes 393224 | tf_op jit(solution)/shard_map/ppermute | solution.py:208
  13.3 6.1 %collective-permute-start.1 = (f32[128,256]{1,0:T(8,128)S(1)}, f32[128,256]{1,0:T(8,128)S(1)}, u32[]{:S(2)}, u32[]{:S(2)}) collective-permute-start(f32[128,256]{1,0:T(8,128)S(1)} %slice_bitcast_fusion.own_ref), channel_id=1, source_target_pairs={{0,64},{1,193},{2,66},{3,195},{4,68},{5,197},{6,70},{7,199},{8,72}... | collective-permute-start | bytes 393224 | tf_op jit(solution)/shard_map/ppermute | solution.py:208
  14.0 7.5 %collective-permute-start.2 = (f32[128,256]{1,0:T(8,128)S(1)}, f32[128,256]{1,0:T(8,128)S(1)}, u32[]{:S(2)}, u32[]{:S(2)}) collective-permute-start(f32[128,256]{1,0:T(8,128)S(1)} %slice_bitcast_fusion.own_ref), channel_id=1, source_target_pairs={{0,192},{1,65},{2,194},{3,67},{4,196},{5,69},{6,198},{7,71},{8,200... | collective-permute-start | bytes 393224 | tf_op jit(solution)/shard_map/ppermute | solution.py:208
  25.3 9.1 %collective-permute-start.4 = (bf16[2,128,256]{2,1,0:T(8,128)(2,1)S(1)}, bf16[2,128,256]{2,1,0:T(8,128)(2,1)S(1)}, u32[]{:S(2)}, u32[]{:S(2)}) collective-permute-start(bf16[2,128,256]{2,1,0:T(8,128)(2,1)S(1)} %maximum_select_fusion.refs_5_), channel_id=1, source_target_pairs={{2,0},{63,1},{4,2},{1,3},{6,4},{3,5},{8,6},{5,7},{10,8},{7,9},{12,... | collective-permute-start | bytes 393224 | tf_op jit(solution)/shard_map/ppermute | solution.py:214
  25.9 11.6 %collective-permute-start.5 = (bf16[2,128,256]{2,1,0:T(8,128)(2,1)S(1)}, bf16[2,128,256]{2,1,0:T(8,128)(2,1)S(1)}, u32[]{:S(2)}, u32[]{:S(2)}) collective-permute-start(bf16[2,128,256]{2,1,0:T(8,128)(2,1)S(1)} %maximum_select_fusion.refs_5_), channel_id=1, source_target_pairs={{4,0},{61,1},{6,2},{63,3},{8,4},{1,5},{10,6},{3,7},{12,8},{5,9},{1... | collective-permute-start | bytes 393224 | tf_op jit(solution)/shard_map/ppermute | solution.py:213
  37.6 2.4 %collective-permute-start.6 = (bf16[4,128,256]{2,1,0:T(8,128)(2,1)S(1)}, bf16[4,128,256]{2,1,0:T(8,128)(2,1)S(1)}, u32[]{:S(2)}, u32[]{:S(2)}) collective-permute-start(bf16[4,128,256]{2,1,0:T(8,128)(2,1)S(1)} %constant_dynamic-update-slice_fusion.refs_6_), channel_id=1, source_target_pairs={{0,1},{1,0},{2,3},{3,2},{4,5},{5,4},{6,7},{7,6},{8,9},{9,8},{10,11... | collective-permute-start | bytes 786440 | tf_op jit(solution)/shard_map/ppermute | solution.py:219
  49.2 6.5 %collective-permute-start.7 = (bf16[512,256]{1,0:T(8,128)(2,1)S(1)}, bf16[512,256]{1,0:T(8,128)(2,1)S(1)}, u32[]{:S(2)}, u32[]{:S(2)}) collective-permute-start(bf16[512,256]{1,0:T(8,128)(2,1)S(1)} %get-tuple-element.70), channel_id=1, source_target_pairs={{0,64},{1,193},{2,66},{3,195},{4,68},{5,197},{6,70},{7,199},{8,72}... | collective-permute-start | bytes 786440 | tf_op jit(solution)/shard_map/ppermute | solution.py:205
  55.8 5.6 %collective-permute-start.8 = (bf16[512,256]{1,0:T(8,128)(2,1)S(1)}, bf16[512,256]{1,0:T(8,128)(2,1)S(1)}, u32[]{:S(2)}, u32[]{:S(2)}) collective-permute-start(bf16[512,256]{1,0:T(8,128)(2,1)S(1)} %get-tuple-element.139), channel_id=1, source_target_pairs={{0,192},{1,65},{2,194},{3,67},{4,196},{5,69},{6,198},{7,71},{8,200... | collective-permute-start | bytes 786440 | tf_op jit(solution)/shard_map/ppermute | solution.py:205
  61.7 3.1 %collective-permute-start.9 = (bf16[128,256]{1,0:T(8,128)(2,1)S(1)}, bf16[128,256]{1,0:T(8,128)(2,1)S(1)}, u32[]{:S(2)}, u32[]{:S(2)}) collective-permute-start(bf16[128,256]{1,0:T(8,128)(2,1)S(1)} %solve.1), channel_id=1, source_target_pairs={{0,1},{1,0},{2,3},{3,2},{4,5},{5,4},{6,7},{7,6},{8,9},{9,8},{10,11... | collective-permute-start | bytes 196616 | tf_op jit(solution)/shard_map/ppermute | solution.py:211
  64.7 8.1 %collective-permute-start.10 = (bf16[2,128,256]{2,1,0:T(8,128)(2,1)S(1)}, bf16[2,128,256]{2,1,0:T(8,128)(2,1)S(1)}, u32[]{:S(2)}, u32[]{:S(2)}) collective-permute-start(bf16[2,128,256]{2,1,0:T(8,128)(2,1)S(1)} %maximum_select_fusion.1.refs_5_.refs_8_), channel_id=1, source_target_pairs={{2,0},{63,1},{4,2},{1,3},{6,4},{3,5},{8,6},{5,7},{10,8},{7,9},{12,... | collective-permute-start | bytes 393224 | tf_op jit(solution)/shard_map/ppermute | solution.py:214
  65.3 11.5 %collective-permute-start.11 = (bf16[2,128,256]{2,1,0:T(8,128)(2,1)S(1)}, bf16[2,128,256]{2,1,0:T(8,128)(2,1)S(1)}, u32[]{:S(2)}, u32[]{:S(2)}) collective-permute-start(bf16[2,128,256]{2,1,0:T(8,128)(2,1)S(1)} %maximum_select_fusion.1.refs_5_.refs_8_), channel_id=1, source_target_pairs={{4,0},{61,1},{6,2},{63,3},{8,4},{1,5},{10,6},{3,7},{12,8},{5,9},{1... | collective-permute-start | bytes 393224 | tf_op jit(solution)/shard_map/ppermute | solution.py:213
  86.7 5.1 %collective-permute-start.13 = (bf16[128,256]{1,0:T(8,128)(2,1)S(1)}, bf16[128,256]{1,0:T(8,128)(2,1)S(1)}, u32[]{:S(2)}, u32[]{:S(2)}) collective-permute-start(bf16[128,256]{1,0:T(8,128)(2,1)S(1)} %get-tuple-element.79), channel_id=1, source_target_pairs={{0,128},{1,129},{2,130},{3,131},{4,132},{5,133},{6,134},{7,135},{8... | collective-permute-start | bytes 196616 | tf_op jit(solution)/shard_map/ppermute | solution.py:208
  87.7 5.0 %collective-permute-start.14 = (bf16[128,256]{1,0:T(8,128)(2,1)S(1)}, bf16[128,256]{1,0:T(8,128)(2,1)S(1)}, u32[]{:S(2)}, u32[]{:S(2)}) collective-permute-start(bf16[128,256]{1,0:T(8,128)(2,1)S(1)} %get-tuple-element.80), channel_id=1, source_target_pairs={{0,64},{1,193},{2,66},{3,195},{4,68},{5,197},{6,70},{7,199},{8,72}... | collective-permute-start | bytes 196616 | tf_op jit(solution)/shard_map/ppermute | solution.py:208
  89.1 4.6 %collective-permute-start.15 = (bf16[128,256]{1,0:T(8,128)(2,1)S(1)}, bf16[128,256]{1,0:T(8,128)(2,1)S(1)}, u32[]{:S(2)}, u32[]{:S(2)}) collective-permute-start(bf16[128,256]{1,0:T(8,128)(2,1)S(1)} %get-tuple-element.81), channel_id=1, source_target_pairs={{0,192},{1,65},{2,194},{3,67},{4,196},{5,69},{6,198},{7,71},{8,200... | collective-permute-start | bytes 196616 | tf_op jit(solution)/shard_map/ppermute | solution.py:208
  95.5 7.4 %collective-permute-start.17 = (bf16[2,128,256]{2,1,0:T(8,128)(2,1)S(1)}, bf16[2,128,256]{2,1,0:T(8,128)(2,1)S(1)}, u32[]{:S(2)}, u32[]{:S(2)}) collective-permute-start(bf16[2,128,256]{2,1,0:T(8,128)(2,1)S(1)} %maximum_select_fusion.2.refs_5_.refs_11_), channel_id=1, source_target_pairs={{2,0},{63,1},{4,2},{1,3},{6,4},{3,5},{8,6},{5,7},{10,8},{7,9},{12,... | collective-permute-start | bytes 393224 | tf_op jit(solution)/shard_map/ppermute | solution.py:214
  95.6 9.9 %collective-permute-start.18 = (bf16[2,128,256]{2,1,0:T(8,128)(2,1)S(1)}, bf16[2,128,256]{2,1,0:T(8,128)(2,1)S(1)}, u32[]{:S(2)}, u32[]{:S(2)}) collective-permute-start(bf16[2,128,256]{2,1,0:T(8,128)(2,1)S(1)} %maximum_select_fusion.2.refs_5_.refs_11_), channel_id=1, source_target_pairs={{4,0},{61,1},{6,2},{63,3},{8,4},{1,5},{10,6},{3,7},{12,8},{5,9},{1... | collective-permute-start | bytes 393224 | tf_op jit(solution)/shard_map/ppermute | solution.py:213
  105.6 2.8 %collective-permute-start.19 = (bf16[4,128,256]{2,1,0:T(8,128)(2,1)S(1)}, bf16[4,128,256]{2,1,0:T(8,128)(2,1)S(1)}, u32[]{:S(2)}, u32[]{:S(2)}) collective-permute-start(bf16[4,128,256]{2,1,0:T(8,128)(2,1)S(1)} %constant_dynamic-update-slice_fusion.4.refs_6_.refs_12_), channel_id=1, source_target_pairs={{0,1},{1,0},{2,3},{3,2},{4,5},{5,4},{6,7},{7,6},{8,9},{9,8},{10,11... | collective-permute-start | bytes 786440 | tf_op jit(solution)/shard_map/ppermute | solution.py:219
  110.9 4.7 %collective-permute-start.20 = (bf16[128,256]{1,0:T(8,128)(2,1)S(1)}, bf16[128,256]{1,0:T(8,128)(2,1)S(1)}, u32[]{:S(2)}, u32[]{:S(2)}) collective-permute-start(bf16[128,256]{1,0:T(8,128)(2,1)S(1)} %get-tuple-element.93), channel_id=1, source_target_pairs={{0,128},{1,129},{2,130},{3,131},{4,132},{5,133},{6,134},{7,135},{8... | collective-permute-start | bytes 196616 | tf_op jit(solution)/shard_map/ppermute | solution.py:208
  111.6 5.4 %collective-permute-start.21 = (bf16[128,256]{1,0:T(8,128)(2,1)S(1)}, bf16[128,256]{1,0:T(8,128)(2,1)S(1)}, u32[]{:S(2)}, u32[]{:S(2)}) collective-permute-start(bf16[128,256]{1,0:T(8,128)(2,1)S(1)} %get-tuple-element.94), channel_id=1, source_target_pairs={{0,64},{1,193},{2,66},{3,195},{4,68},{5,197},{6,70},{7,199},{8,72}... | collective-permute-start | bytes 196616 | tf_op jit(solution)/shard_map/ppermute | solution.py:208
  113.4 4.5 %collective-permute-start.22 = (bf16[128,256]{1,0:T(8,128)(2,1)S(1)}, bf16[128,256]{1,0:T(8,128)(2,1)S(1)}, u32[]{:S(2)}, u32[]{:S(2)}) collective-permute-start(bf16[128,256]{1,0:T(8,128)(2,1)S(1)} %get-tuple-element.95), channel_id=1, source_target_pairs={{0,192},{1,65},{2,194},{3,67},{4,196},{5,69},{6,198},{7,71},{8,200... | collective-permute-start | bytes 196616 | tf_op jit(solution)/shard_map/ppermute | solution.py:208
  117.9 2.1 %collective-permute-start.23 = (bf16[128,256]{1,0:T(8,128)(2,1)S(1)}, bf16[128,256]{1,0:T(8,128)(2,1)S(1)}, u32[]{:S(2)}, u32[]{:S(2)}) collective-permute-start(bf16[128,256]{1,0:T(8,128)(2,1)S(1)} %get-tuple-element.136), channel_id=1, source_target_pairs={{0,1},{1,0},{2,3},{3,2},{4,5},{5,4},{6,7},{7,6},{8,9},{9,8},{10,11... | collective-permute-start | bytes 196616 | tf_op jit(solution)/shard_map/ppermute | solution.py:211
  120.0 8.2 %collective-permute-start.24 = (bf16[2,128,256]{2,1,0:T(8,128)(2,1)S(1)}, bf16[2,128,256]{2,1,0:T(8,128)(2,1)S(1)}, u32[]{:S(2)}, u32[]{:S(2)}) collective-permute-start(bf16[2,128,256]{2,1,0:T(8,128)(2,1)S(1)} %maximum_select_fusion.3.refs_5_.refs_14_), channel_id=1, source_target_pairs={{2,0},{63,1},{4,2},{1,3},{6,4},{3,5},{8,6},{5,7},{10,8},{7,9},{12,... | collective-permute-start | bytes 393224 | tf_op jit(solution)/shard_map/ppermute | solution.py:214
  120.9 11.3 %collective-permute-start.25 = (bf16[2,128,256]{2,1,0:T(8,128)(2,1)S(1)}, bf16[2,128,256]{2,1,0:T(8,128)(2,1)S(1)}, u32[]{:S(2)}, u32[]{:S(2)}) collective-permute-start(bf16[2,128,256]{2,1,0:T(8,128)(2,1)S(1)} %maximum_select_fusion.3.refs_5_.refs_14_), channel_id=1, source_target_pairs={{4,0},{61,1},{6,2},{63,3},{8,4},{1,5},{10,6},{3,7},{12,8},{5,9},{1... | collective-permute-start | bytes 393224 | tf_op jit(solution)/shard_map/ppermute | solution.py:213
  136.3 5.1 %collective-permute-start.27 = (bf16[128,256]{1,0:T(8,128)(2,1)S(1)}, bf16[128,256]{1,0:T(8,128)(2,1)S(1)}, u32[]{:S(2)}, u32[]{:S(2)}) collective-permute-start(bf16[128,256]{1,0:T(8,128)(2,1)S(1)} %get-tuple-element.110), channel_id=1, source_target_pairs={{0,128},{1,129},{2,130},{3,131},{4,132},{5,133},{6,134},{7,135},{8... | collective-permute-start | bytes 196616 | tf_op jit(solution)/shard_map/ppermute | solution.py:208
  137.2 4.9 %collective-permute-start.28 = (bf16[128,256]{1,0:T(8,128)(2,1)S(1)}, bf16[128,256]{1,0:T(8,128)(2,1)S(1)}, u32[]{:S(2)}, u32[]{:S(2)}) collective-permute-start(bf16[128,256]{1,0:T(8,128)(2,1)S(1)} %get-tuple-element.111), channel_id=1, source_target_pairs={{0,64},{1,193},{2,66},{3,195},{4,68},{5,197},{6,70},{7,199},{8,72}... | collective-permute-start | bytes 196616 | tf_op jit(solution)/shard_map/ppermute | solution.py:208
  138.7 4.5 %collective-permute-start.29 = (bf16[128,256]{1,0:T(8,128)(2,1)S(1)}, bf16[128,256]{1,0:T(8,128)(2,1)S(1)}, u32[]{:S(2)}, u32[]{:S(2)}) collective-permute-start(bf16[128,256]{1,0:T(8,128)(2,1)S(1)} %get-tuple-element.112), channel_id=1, source_target_pairs={{0,192},{1,65},{2,194},{3,67},{4,196},{5,69},{6,198},{7,71},{8,200... | collective-permute-start | bytes 196616 | tf_op jit(solution)/shard_map/ppermute | solution.py:208
  144.8 7.2 %collective-permute-start.31 = (bf16[2,128,256]{2,1,0:T(8,128)(2,1)S(1)}, bf16[2,128,256]{2,1,0:T(8,128)(2,1)S(1)}, u32[]{:S(2)}, u32[]{:S(2)}) collective-permute-start(bf16[2,128,256]{2,1,0:T(8,128)(2,1)S(1)} %maximum_select_fusion.4.refs_5_), channel_id=1, source_target_pairs={{2,0},{63,1},{4,2},{1,3},{6,4},{3,5},{8,6},{5,7},{10,8},{7,9},{12,... | collective-permute-start | bytes 393224 | tf_op jit(solution)/shard_map/ppermute | solution.py:214
  144.9 9.9 %collective-permute-start.32 = (bf16[2,128,256]{2,1,0:T(8,128)(2,1)S(1)}, bf16[2,128,256]{2,1,0:T(8,128)(2,1)S(1)}, u32[]{:S(2)}, u32[]{:S(2)}) collective-permute-start(bf16[2,128,256]{2,1,0:T(8,128)(2,1)S(1)} %maximum_select_fusion.4.refs_5_), channel_id=1, source_target_pairs={{4,0},{61,1},{6,2},{63,3},{8,4},{1,5},{10,6},{3,7},{12,8},{5,9},{1... | collective-permute-start | bytes 393224 | tf_op jit(solution)/shard_map/ppermute | solution.py:213
  159.0 5.1 %collective-permute-start.34 = (bf16[128,256]{1,0:T(8,128)(2,1)S(1)}, bf16[128,256]{1,0:T(8,128)(2,1)S(1)}, u32[]{:S(2)}, u32[]{:S(2)}) collective-permute-start(bf16[128,256]{1,0:T(8,128)(2,1)S(1)} %get-tuple-element.130), channel_id=1, source_target_pairs={{0,128},{1,129},{2,130},{3,131},{4,132},{5,133},{6,134},{7,135},{8... | collective-permute-start | bytes 196616 | tf_op jit(solution)/shard_map/ppermute | solution.py:208
  160.3 5.1 %collective-permute-start.35 = (bf16[128,256]{1,0:T(8,128)(2,1)S(1)}, bf16[128,256]{1,0:T(8,128)(2,1)S(1)}, u32[]{:S(2)}, u32[]{:S(2)}) collective-permute-start(bf16[128,256]{1,0:T(8,128)(2,1)S(1)} %get-tuple-element.131), channel_id=1, source_target_pairs={{0,64},{1,193},{2,66},{3,195},{4,68},{5,197},{6,70},{7,199},{8,72}... | collective-permute-start | bytes 196616 | tf_op jit(solution)/shard_map/ppermute | solution.py:208
  161.9 4.4 %collective-permute-start.36 = (bf16[128,256]{1,0:T(8,128)(2,1)S(1)}, bf16[128,256]{1,0:T(8,128)(2,1)S(1)}, u32[]{:S(2)}, u32[]{:S(2)}) collective-permute-start(bf16[128,256]{1,0:T(8,128)(2,1)S(1)} %get-tuple-element.132), channel_id=1, source_target_pairs={{0,192},{1,65},{2,194},{3,67},{4,196},{5,69},{6,198},{7,71},{8,200... | collective-permute-start | bytes 196616 | tf_op jit(solution)/shard_map/ppermute | solution.py:208
  (21 other events, 236.3 us)
Sparse Core Ops, SparseCore 0:
  9.2 37.2 all-gather.1

commit v2 on v0

v2 whole, which is shorter than its diff:
```python
import functools

import jax
import jax.numpy as jnp
from jax import lax
from jax.experimental import pallas as pl
from jax.experimental.pallas import tpu as pltpu
from jax.sharding import PartitionSpec as P

VMEM = pl.BlockSpec(memory_space=pltpu.VMEM)
SMEM = pl.BlockSpec(memory_space=pltpu.SMEM)
HBM = pl.BlockSpec(memory_space=pltpu.HBM)
MIB = 2**20
GROUP = 2
TABLE_LIMIT = 2 * MIB
SOON_LIMIT = 48 * MIB
LATE_LIMIT = 40 * MIB


def row_moves(count, delta):
    pairs = []
    for target in range(count):
        step = 2 * delta if target % 2 == 0 else -2 * delta
        pairs.append(((target + step) % count, target))
    return pairs


def swap_moves(count):
    return [(source, source ^ 1) for source in range(count)]


def partners(cols, col, odd):
    one, two = (col ^ 1, cols - 1 - col) if odd == 0 else (cols - 1 - col, col ^ 1)
    return one, two, (col + 2) % cols


def col_moves(cols, rows, which):
    return [
        (col * rows + row, partners(cols, col, row % 2)[which] * rows + row)
        for col in range(cols)
        for row in range(rows)
    ]


def split(value):
    high = value.astype(jnp.bfloat16)
    return high, (value - high.astype(jnp.float32)).astype(jnp.bfloat16)


def product(left, right):
    return jnp.dot(left, right, preferred_element_type=jnp.float32)


def exact_product(left, right):
    high, low = split(right)
    return product(left, high) + product(left, low)


def run_copies(copies):
    for copy in copies:
        copy.start()
    for copy in copies:
        copy.wait()


def fill_kernel(source_ref, start, out_ref, sem):
    run_copies([pltpu.make_async_copy(source_ref.at[pl.ds(start, out_ref.shape[0])], out_ref, sem)])


def soon_fill_kernel(factor_ref, out_ref, sems):
    fill_kernel(factor_ref, 0, out_ref, sems.at[0])


def late_fill_kernel(factor_ref, diag_ref, blocks_ref, late_ref, sems):
    late = late_ref.shape[0]
    run_copies(
        [
            pltpu.make_async_copy(
                factor_ref.at[pl.ds(1, blocks_ref.shape[0])], blocks_ref, sems.at[0]
            ),
            pltpu.make_async_copy(
                diag_ref.at[pl.ds(diag_ref.shape[0] - late, late)], late_ref, sems.at[1]
            ),
        ]
    )


def order_kernel(meta_ref, start_ref, first_ref):
    share = first_ref.shape[1]
    for index in range(4):
        start = pl.multiple_of(meta_ref[1 + index] * share, share)
        first_ref[index] = start_ref[:, pl.ds(start, share)]


def table_kernel(level_count, rows, meta_ref, column_ref, count_ref, scale_ref, index_ref, weight_ref):
    own_chip = meta_ref[0] // 2
    core = meta_ref[0] % 2
    turn = 1 - 2 * core
    room = room_of(index_ref)
    inverse = (2**16 + level_count - 1) // level_count
    for at, dep_row in enumerate(rows):

        def put(position, slot, place, scale):
            index_ref[at, position] = slot
            index_ref[at, 3 * room + position] = place
            weight_ref[at, position] = -scale

        def collect(slot, found):
            column = column_ref[dep_row, slot]
            shard = lax.shift_right_logical(column * inverse, 16)
            from_level = column - shard * level_count
            forward = (lax.shift_right_logical(shard, 1) - own_chip) * turn
            parity = lax.bitwise_and(shard, 1)
            older = from_level != dep_row
            kind = jnp.where(older | (forward == 0), 2, jnp.where(forward > 0, 1, 0))
            place = parity + jnp.where(forward == 0, 0, 2 * jnp.abs(forward) - 2)
            start = jnp.where(forward == 0, 2, jnp.where(forward > 0, 4, 8))
            place = jnp.where(older, 10 * from_level + start + place, place)
            before = jnp.where(kind == 2, found[2], jnp.where(kind == 1, found[1], found[0]))
            put(room * kind + before, slot, place, scale_ref[dep_row, slot])
            return tuple(found[k] + (kind == k).astype(jnp.int32) for k in range(3))

        found = lax.fori_loop(0, count_ref[dep_row], collect, (0, 0, 0))
        for kind in range(3):
            for extra in range(GROUP - 1):
                put(room * kind + found[kind] + extra, 0, 0, 0.0)
            index_ref[at, 6 * room + kind] = (found[kind] + GROUP - 1) // GROUP
        index_ref[at, 6 * room + 3] = meta_ref[1]


def room_of(index_ref):
    return index_ref.shape[1] // 6


def first_kernel(first_ref, *refs):
    *piece_refs, out_ref = refs
    total = jnp.zeros(out_ref.shape, jnp.float32)
    for index, piece_ref in enumerate(piece_refs):
        total += exact_product(first_ref[index], piece_ref[...])
    out_ref[...] = total.astype(out_ref.dtype)


def add_slots(sum_ref, stored, dep_row, kind, index_ref, weight_ref, blocks_ref):
    room = room_of(index_ref)
    at = max(dep_row - 1, 0)

    def add_group(step, carry):
        total = sum_ref[...]
        for offset in range(GROUP):
            position = room * kind + GROUP * step + offset
            part = product(
                blocks_ref[at, index_ref[at, position]],
                stored[index_ref[at, 3 * room + position]],
            )
            total += weight_ref[at, position] * part
        sum_ref[...] = total
        return carry

    lax.fori_loop(0, index_ref[at, 6 * room + kind], add_group, 0)


def early_kernel(level, index_ref, weight_ref, blocks_ref, right_ref, *refs):
    *piece_refs, sum_ref, stored_ref = refs
    start = 0
    for piece_ref in piece_refs:
        stored_ref[pl.ds(start, piece_ref.shape[0])] = piece_ref[...]
        start += piece_ref.shape[0]
    share = right_ref.shape[1]
    sum_ref[...] = jnp.zeros_like(sum_ref)
    start = pl.multiple_of(index_ref[0, 6 * room_of(index_ref) + 3] * share, share)
    sum_ref[pl.ds(start, share), :] = right_ref[level]
    add_slots(sum_ref, stored_ref, level - 1, 2, index_ref, weight_ref, blocks_ref)


def middle_kernel(level, index_ref, weight_ref, blocks_ref, before_ref, mine_ref, sum_ref):
    sum_ref[...] = before_ref[...]
    add_slots(sum_ref, mine_ref, level - 1, 1, index_ref, weight_ref, blocks_ref)


def last_kernel(level, index_ref, weight_ref, blocks_ref, before_ref, theirs_ref, *refs):
    *diag_refs, own_ref, one_ref, two_ref, across_ref, sum_ref = refs
    sum_ref[...] = before_ref[...]
    add_slots(sum_ref, theirs_ref, level - 1, 0, index_ref, weight_ref, blocks_ref)
    blocks = jnp.concatenate([ref[...] for ref in diag_refs], axis=0)
    total = exact_product(blocks, sum_ref[...])
    share = own_ref.shape[0]
    for index, ref in enumerate((own_ref, one_ref, two_ref, across_ref)):
        ref[...] = total[index * share : (index + 1) * share].astype(ref.dtype)


def per_device(factor_blocks, block_scales, dep_column, dep_count, diag_inverse, right_side):
    level_count, share, block_rows = diag_inverse.shape
    slots = factor_blocks.shape[1]
    width = right_side.shape[2]
    rows, cols = lax.axis_size("row"), lax.axis_size("col")
    shard = lax.axis_index("row").astype(jnp.int32)
    col = lax.axis_index("col").astype(jnp.int32)
    even = shard % 2 == 0
    one = jnp.where(even, col ^ 1, cols - 1 - col)
    two = jnp.where(even, cols - 1 - col, col ^ 1)
    meta = jnp.stack([shard, col, one, two, (col + 2) % cols])
    bf16, f32 = jnp.bfloat16, jnp.float32
    shape = jax.ShapeDtypeStruct
    room = slots + GROUP - 1
    soon = 2
    late = level_count - 1 - soon
    wide = shape((block_rows, width), f32)
    piece = shape((share, width), bf16)

    def call(body, out_shape, in_specs, out_specs, operands, limit, scratch=(), flops=2**27, name=None):
        return pl.pallas_call(
            body,
            out_shape=out_shape,
            in_specs=in_specs,
            out_specs=out_specs,
            scratch_shapes=list(scratch),
            cost_estimate=pl.CostEstimate(flops=flops, bytes_accessed=2 * MIB, transcendentals=0),
            compiler_params=pltpu.CompilerParams(vmem_limit_bytes=limit),
            name=name,
        )(*operands)

    def along_col(value, which):
        return lax.ppermute(value, ("col", "row"), col_moves(cols, rows, which))

    def swap(value):
        return lax.ppermute(value, "row", swap_moves(rows))

    def after(value, *others):
        return lax.optimization_barrier((value, *others))[0]

    own = right_side[0]
    arrived = [along_col(own, which) for which in (2, 0, 1)]
    diag_later = after(diag_inverse, own)
    soon_diag, start_diag = diag_later[1 : 1 + soon], diag_later[0]
    soon_one = along_col(soon_diag, 0)

    def list_slots(rows, meta):
        return call(
            functools.partial(table_kernel, level_count, rows),
            [shape((len(rows), 6 * room + 4), jnp.int32), shape((len(rows), 3 * room), f32)],
            [SMEM] * 4,
            [SMEM] * 2,
            (meta, dep_column, dep_count, block_scales),
            TABLE_LIMIT,
            name="table",
        )

    first = call(
        order_kernel,
        shape((4, share, share), bf16),
        [SMEM, VMEM],
        VMEM,
        (after(meta, own), start_diag),
        2 * MIB,
        name="order",
    )
    index, weight = list_slots((0,), after(meta, own))
    blocks = call(
        soon_fill_kernel,
        shape((1, *factor_blocks.shape[1:]), bf16),
        [HBM],
        VMEM,
        (after(factor_blocks, own),),
        SOON_LIMIT,
        [pltpu.SemaphoreType.DMA((1,))],
        name="soon_fill",
    )
    opposite, by_one, by_two = arrived
    opposite, by_one, by_two, first, blocks, soon_one, index = lax.optimization_barrier(
        (opposite, by_one, by_two, first, blocks, soon_one, index)
    )
    solved = call(
        first_kernel,
        piece,
        [VMEM] * 5,
        VMEM,
        (first, own, by_one, by_two, opposite),
        4 * MIB,
        name="first_solve",
    )
    outputs = [solved]
    pieces = []
    diags = {}
    for level in range(1, level_count):
        other = swap(solved)
        pair = jnp.where(even, jnp.stack([solved, other]), jnp.stack([other, solved]))
        far = lax.ppermute(pair, "row", row_moves(rows, 2))
        near = lax.ppermute(pair, "row", row_moves(rows, 1))
        far_first = far
        stored = after([pair, *(x for three in pieces for x in three)], pair)
        if level == 2:
            index, weight = list_slots(tuple(range(1, level_count - 1)), after(meta, pair))
            blocks = late_blocks
        tables = (index, weight, blocks)
        table_specs = [SMEM] * 2 + [VMEM]
        early = call(
            functools.partial(early_kernel, level),
            wide,
            table_specs + [VMEM] * (1 + len(stored)),
            VMEM,
            (*tables, right_side, *stored),
            20 * MIB,
            [pltpu.VMEM((2 + 10 * (level - 1), share, width), bf16)],
            name="early_slots",
        )
        ready = [near, far, early]
        if level == 1:
            soon_two = along_col(after(jnp.stack([soon_diag, soon_one]), early), 1)
            for at in range(soon):
                diags[1 + at] = (soon_diag[at], soon_one[at], soon_two[0, at], soon_two[1, at])
            fill = call(
                late_fill_kernel,
                [
                    shape((level_count - 2, *factor_blocks.shape[1:]), bf16),
                    shape((late, share, block_rows), bf16),
                ],
                [HBM, HBM],
                [VMEM, VMEM],
                (after(factor_blocks, early), diag_inverse),
                LATE_LIMIT,
                [pltpu.SemaphoreType.DMA((2,))],
                name="late_fill",
            )
            ready += fill
            near, far, early, late_blocks, late_diag = lax.optimization_barrier(ready)
            half_way = along_col(after(fill[1][0], far_first), 1)
            which = 0
        else:
            near, far, early = lax.optimization_barrier(ready)
            ahead = level + 1
            if ahead < level_count:
                mine_diag = late_diag[ahead - 1 - soon]
                sent = [mine_diag, half_way]
                if ahead + 1 < level_count:
                    sent.append(late_diag[ahead - soon])
                got = along_col(after(jnp.stack(sent), far_first), which)
                by = (got[0], half_way) if which == 0 else (half_way, got[0])
                diags[ahead] = (mine_diag, *by, got[1])
                half_way = got[2] if ahead + 1 < level_count else None
                which = 1 - which
        mine = jnp.concatenate([near, far], axis=0)
        theirs = swap(mine)
        middle = call(
            functools.partial(middle_kernel, level),
            wide,
            table_specs + [VMEM] * 2,
            VMEM,
            (*tables, early, mine),
            20 * MIB,
            name="middle_slots",
        )
        theirs, middle = lax.optimization_barrier((theirs, middle))
        pieces.append((pair, mine, theirs))
        own, *parts = call(
            functools.partial(last_kernel, level),
            [shape((share, width), f32)] + [piece] * 3,
            table_specs + [VMEM] * 6,
            [VMEM] * 4,
            (*tables, middle, theirs, *diags[level]),
            20 * MIB,
            [pltpu.VMEM((block_rows, width), f32)],
            name="last_slots",
        )
        total = own
        for which_part in (2, 0, 1):
            total = total + along_col(parts[which_part], which_part).astype(f32)
        solved = total.astype(bf16)
        outputs.append(solved)
    return jnp.stack(outputs, axis=0)


def solution(mesh):
    in_specs = (
        P("row", None, None, "col"),
        P("row", None),
        P("row", None),
        P("row"),
        P("row", "col", None),
        P("row", "col", None),
    )
    return jax.shard_map(
        per_device, mesh=mesh, in_specs=in_specs, out_specs=P("row", "col", None), check_vma=False
    )
```

time: 1090 us -> 139 us (0.13)
  waiting for transfers between devices: 428 us -> 51.4 us
  loops' own time: 270 us -> 0 us
  matrix products: 119 us -> 0 us
  local copies, waits for them, and re-layouts: 74.8 us -> 3.43 us
  starting transfers between devices: 114 us -> 50.5 us
  other arithmetic: 60.6 us -> 1.03 us
  Pallas kernels: 0 us -> 31.5 us
  between operations: 14.2 us -> 0.55 us
    psum x6 -> x0, waiting for transfers between devices: 413 us -> none  [per_device(): reduced = lax.psum(partial_value - placed, 'col')]
    another operation x5 -> x0, loops' own time: 270 us -> none  [row_products(): return lax.fori_loop(0, live_count, add_slot, running_init)]
    dot_general x66 -> x0, matrix products: 119 us -> none  [the longest x60 109 us: add_slot(): jnp.dot(factor_blocks[dep_row, slot_index], x_piece, preferred_element_ty...]
    ppermute x40 -> x44, starting transfers between devices: 113 us -> 50.5 us  [the longest x24 24.4 us: along_col(): return lax.ppermute(value, ('col', 'row'), col_moves(cols, rows, which))]
    rem x60 -> x0, other arithmetic: 39.2 us -> none  [add_slot(): x_piece = stored[column % level_count, column // level_count - anchor]]
    dynamic_slice x60 -> x0, local copies, waits for them, and re-layouts: 38.7 us -> none  [add_slot(): return running + block_scales[dep_row, slot_index] * product]
    ppermute x40 -> x44, waiting for transfers between devices: 15.3 us -> 51.4 us  [the longest x5 19.5 us: per_device(): far = lax.ppermute(pair, 'row', row_moves(rows, 2))]
    pallas_call x0 -> x21, Pallas kernels: none -> 31.5 us  [call(): pl.pallas_call(body, out_shape=out_shape, in_specs=in_specs, out_specs=ou...]
  transfers between devices with their start and end apart: 46 -> 44, of which waited for: 14 -> 33; matrix products, arithmetic and copies ran while one was open for 4% -> 2% of each run, Pallas kernels for 0% -> 18%
where the time goes in v2:
time: 139 us; the launch traced here: 138 us
  waiting for transfers between devices  51.4 us (37%)
  starting transfers between devices  50.5 us (36%)
  Pallas kernels  31.5 us (23%)
  local copies, waits for them, and re-layouts  3.43 us (2%)
    pallas_call x21, Pallas kernels, call(): pl.pallas_call(body, out_shape=out_shape, in_specs=in_specs, out_specs=ou...  31.5 us
    ppermute x24, starting transfers between devices, along_col(): return lax.ppermute(value, ('col', 'row'), col_moves(cols, rows, which))  24.4 us
    ppermute x5, waiting for transfers between devices, per_device(): far = lax.ppermute(pair, 'row', row_moves(rows, 2))  19.5 us
    ppermute x10, starting transfers between devices, swap(): return lax.ppermute(value, 'row', swap_moves(rows))  19.2 us
    ppermute x24, waiting for transfers between devices, along_col(): return lax.ppermute(value, ('col', 'row'), col_moves(cols, rows, which))  18.6 us
    ppermute x10, waiting for transfers between devices, swap(): return lax.ppermute(value, 'row', swap_moves(rows))  6.77 us
    ppermute x5, waiting for transfers between devices, per_device(): near = lax.ppermute(pair, 'row', row_moves(rows, 1))  6.55 us
    ppermute x5, starting transfers between devices, per_device(): far = lax.ppermute(pair, 'row', row_moves(rows, 2))  4.25 us
  transfers between devices with their start and end apart: 44, of which 33 were waited for; matrix products, arithmetic and copies ran while one was open for 2% of the time, Pallas kernels for 18%

profile of v2, /device:TPU:1, one launch (start us, length us, event | category | flops | bytes accessed | tf_op | source)
XLA Modules:
  0.0 138.4 jit_solution(1600729350694385680)
XLA Ops:
  1.0 2.2 %collective-permute-start.2 = (f32[128,256]{1,0:T(8,128)S(1)}, f32[128,256]{1,0:T(8,128)S(1)}, u32[]{:S(2)}, u32[]{:S(2)}) collective-permute-start(f32[128,256]{1,0:T(8,128)S(1)} %slice_bitcast_fusion.16.refs_0_), channel_id=1, source_target_pairs={{0,192},{1,65},{2,194},{3,67},{4,196},{5,69},{6,198},{7,71},{8,200... | collective-permute-start | bytes 393224 | tf_op jit(solution)/shard_map/ppermute | solution.py:223
  3.2 1.9 %collective-permute-start.1 = (f32[128,256]{1,0:T(8,128)S(1)}, f32[128,256]{1,0:T(8,128)S(1)}, u32[]{:S(2)}, u32[]{:S(2)}) collective-permute-start(f32[128,256]{1,0:T(8,128)S(1)} %slice_bitcast_fusion.16.refs_0_), channel_id=1, source_target_pairs={{0,64},{1,193},{2,66},{3,195},{4,68},{5,197},{6,70},{7,199},{8,72}... | collective-permute-start | bytes 393224 | tf_op jit(solution)/shard_map/ppermute | solution.py:223
  6.8 2.2 %collective-permute-start.3 = (bf16[2,128,512]{2,1,0:T(8,128)(2,1)S(1)}, bf16[2,128,512]{2,1,0:T(8,128)(2,1)S(1)}, u32[]{:S(2)}, u32[]{:S(2)}) collective-permute-start(bf16[2,128,512]{2,1,0:T(8,128)(2,1)S(1)} %get-tuple-element.227), channel_id=1, source_target_pairs={{0,64},{1,193},{2,66},{3,195},{4,68},{5,197},{6,70},{7,199},{8,72}... | collective-permute-start | bytes 786440 | tf_op jit(solution)/shard_map/ppermute | solution.py:223
  10.1 1.7 %soon_fill.1.blocks_ref = bf16[1,17,512,128]{3,2,1,0:T(8,128)(2,1)S(1)} custom-call(bf16[5,17,512,128]{3,2,1,0:T(8,128)(2,1)} %factor_ref.1), custom_call_target="tpu_custom_call" | custom-call | flops 134217728 | bytes 2097152 | tf_op jit(solution)/shard_map/soon_fill/pallas_call | solution.py:211
  17.8 2.1 %collective-permute-start.6 = (bf16[2,128,256]{2,1,0:T(8,128)(2,1)S(1)}, bf16[2,128,256]{2,1,0:T(8,128)(2,1)S(1)}, u32[]{:S(2)}, u32[]{:S(2)}) collective-permute-start(bf16[2,128,256]{2,1,0:T(8,128)(2,1)S(1)} %maximum_select_fusion.refs_0_.refs_1_), channel_id=1, source_target_pairs={{4,0},{61,1},{6,2},{63,3},{8,4},{1,5},{10,6},{3,7},{12,8},{5,9},{1... | collective-permute-start | bytes 393224 | tf_op jit(solution)/shard_map/ppermute | solution.py:287
  23.0 3.5 %late_fill.1 = (bf16[4,17,512,128]{3,2,1,0:T(8,128)(2,1)S(1)}, bf16[3,128,512]{2,1,0:T(8,128)(2,1)S(1)}) custom-call(bf16[5,17,512,128]{3,2,1,0:T(8,128)(2,1)} %factor_ref.1, bf16[6,128,512]{2,1,0:T(8,128)(2,1)S(1)} %copy-done.1), custom_call_target="tpu_custom_call" | custom-call | flops 134217728 | bytes 2097152 | tf_op jit(solution)/shard_map/late_fill/pallas_call | solution.py:211
  27.6 2.3 %collective-permute-done.5 = bf16[2,128,256]{2,1,0:T(8,128)(2,1)S(1)} collective-permute-done((bf16[2,128,256]{2,1,0:T(8,128)(2,1)S(1)}, bf16[2,128,256]{2,1,0:T(8,128)(2,1)S(1)}, u32[]{:S(2)}, u32[]{:S(2)}) %collective-permute-start.5) | collective-permute-done | bytes 131104 | tf_op jit(solution)/shard_map/ppermute | solution.py:288
  29.9 3.8 %collective-permute-start.7 = (bf16[4,128,256]{2,1,0:T(8,128)(2,1)S(1)}, bf16[4,128,256]{2,1,0:T(8,128)(2,1)S(1)}, u32[]{:S(2)}, u32[]{:S(2)}) collective-permute-start(bf16[4,128,256]{2,1,0:T(8,128)(2,1)S(1)} %constant_dynamic-update-slice_fusion.mine_ref.refs_2_), channel_id=1, source_target_pairs={{0,1},{1,0},{2,3},{3,2},{4,5},{5,4},{6,7},{7,6},{8,9},{9,8},{10,11... | collective-permute-start | bytes 786440 | tf_op jit(solution)/shard_map/ppermute | solution.py:226
  36.9 1.9 %collective-permute-start.10 = (bf16[128,256]{1,0:T(8,128)(2,1)S(1)}, bf16[128,256]{1,0:T(8,128)(2,1)S(1)}, u32[]{:S(2)}, u32[]{:S(2)}) collective-permute-start(bf16[128,256]{1,0:T(8,128)(2,1)S(1)} %get-tuple-element.134), channel_id=1, source_target_pairs={{0,64},{1,193},{2,66},{3,195},{4,68},{5,197},{6,70},{7,199},{8,72}... | collective-permute-start | bytes 196616 | tf_op jit(solution)/shard_map/ppermute | solution.py:223
  39.3 2.1 %collective-permute-done.9 = bf16[128,256]{1,0:T(8,128)(2,1)S(1)} collective-permute-done((bf16[128,256]{1,0:T(8,128)(2,1)S(1)}, bf16[128,256]{1,0:T(8,128)(2,1)S(1)}, u32[]{:S(2)}, u32[]{:S(2)}) %collective-permute-start.9) | collective-permute-done | bytes 65568 | tf_op jit(solution)/shard_map/ppermute | solution.py:223
  42.0 6.0 %collective-permute-start.12 = (bf16[128,256]{1,0:T(8,128)(2,1)S(1)}, bf16[128,256]{1,0:T(8,128)(2,1)S(1)}, u32[]{:S(2)}, u32[]{:S(2)}) collective-permute-start(bf16[128,256]{1,0:T(8,128)(2,1)S(1)} %get-tuple-element.222), channel_id=1, source_target_pairs={{0,1},{1,0},{2,3},{3,2},{4,5},{5,4},{6,7},{7,6},{8,9},{9,8},{10,11... | collective-permute-start | bytes 196616 | tf_op jit(solution)/shard_map/ppermute | solution.py:226
  48.9 1.8 %collective-permute-start.14 = (bf16[2,128,256]{2,1,0:T(8,128)(2,1)S(1)}, bf16[2,128,256]{2,1,0:T(8,128)(2,1)S(1)}, u32[]{:S(2)}, u32[]{:S(2)}) collective-permute-start(bf16[2,128,256]{2,1,0:T(8,128)(2,1)S(1)} %maximum_select_fusion.1.refs_0_.refs_4_), channel_id=1, source_target_pairs={{4,0},{61,1},{6,2},{63,3},{8,4},{1,5},{10,6},{3,7},{12,8},{5,9},{1... | collective-permute-start | bytes 393224 | tf_op jit(solution)/shard_map/ppermute | solution.py:287
  50.8 3.0 %table.3 = (s32[4,112]{1,0:T(4,128)S(1)}, f32[4,54]{1,0:T(4,128)S(1)}) custom-call(s32[5]{0:T(128)S(1)} %stack.125.meta_ref, s32[5,17]{1,0:T(8,128)S(1)} %copy-done.2, s32[5]{0:T(128)S(1)} %copy-done.4, f32[5,17]{1,0:T(8,128)S(1)} %copy-done.3), custom_call_target="tpu_custom_call" | custom-call | flops 134217728 | bytes 2097152 | tf_op jit(solution)/shard_map/table/pallas_call | solution.py:211
  55.4 1.8 %collective-permute-done.14 = bf16[2,128,256]{2,1,0:T(8,128)(2,1)S(1)} collective-permute-done((bf16[2,128,256]{2,1,0:T(8,128)(2,1)S(1)}, bf16[2,128,256]{2,1,0:T(8,128)(2,1)S(1)}, u32[]{:S(2)}, u32[]{:S(2)}) %collective-permute-start.14) | collective-permute-done | bytes 131104 | tf_op jit(solution)/shard_map/ppermute | solution.py:287
  57.2 2.5 %collective-permute-done.13 = bf16[2,128,256]{2,1,0:T(8,128)(2,1)S(1)} collective-permute-done((bf16[2,128,256]{2,1,0:T(8,128)(2,1)S(1)}, bf16[2,128,256]{2,1,0:T(8,128)(2,1)S(1)}, u32[]{:S(2)}, u32[]{:S(2)}) %collective-permute-start.13) | collective-permute-done | bytes 131104 | tf_op jit(solution)/shard_map/ppermute | solution.py:288
  61.5 1.6 %last_slots.6 = (f32[128,256]{1,0:T(8,128)S(1)}, bf16[128,256]{1,0:T(8,128)(2,1)S(1)}, bf16[128,256]{1,0:T(8,128)(2,1)S(1)}, bf16[128,256]{1,0:T(8,128)(2,1)S(1)}) custom-call(s32[4,112]{1,0:T(4,128)S(1)} %get-tuple-element.137.index_ref, f32[4,54]{1,0:T(4,128)S(1)} %get-tuple-element.138.weight_ref, ...), custom_call_target="tpu_custom_call" | custom-call | flops 134217728 | bytes 2097152 | tf_op jit(solution)/shard_map/last_slots/pallas_call | solution.py:211
  64.2 2.1 %collective-permute-start.17 = (bf16[128,256]{1,0:T(8,128)(2,1)S(1)}, bf16[128,256]{1,0:T(8,128)(2,1)S(1)}, u32[]{:S(2)}, u32[]{:S(2)}) collective-permute-start(bf16[128,256]{1,0:T(8,128)(2,1)S(1)} %get-tuple-element.151), channel_id=1, source_target_pairs={{0,64},{1,193},{2,66},{3,195},{4,68},{5,197},{6,70},{7,199},{8,72}... | collective-permute-start | bytes 196616 | tf_op jit(solution)/shard_map/ppermute | solution.py:223
  70.3 2.4 %collective-permute-start.19 = (bf16[128,256]{1,0:T(8,128)(2,1)S(1)}, bf16[128,256]{1,0:T(8,128)(2,1)S(1)}, u32[]{:S(2)}, u32[]{:S(2)}) collective-permute-start(bf16[128,256]{1,0:T(8,128)(2,1)S(1)} %get-tuple-element.220), channel_id=1, source_target_pairs={{0,1},{1,0},{2,3},{3,2},{4,5},{5,4},{6,7},{7,6},{8,9},{9,8},{10,11... | collective-permute-start | bytes 196616 | tf_op jit(solution)/shard_map/ppermute | solution.py:226
  74.0 2.2 %early_slots.7.before_ref = f32[512,256]{1,0:T(8,128)S(1)} custom-call(s32[4,112]{1,0:T(4,128)S(1)} %get-tuple-element.137.index_ref, f32[4,54]{1,0:T(4,128)S(1)} %get-tuple-element.138.weight_ref, bf16[4,17,512,128]{3,2,1,0:T(8,128)(2,1)S(1)} %get-tuple-element.139.blocks_ref, f32[6,128,256]{2,1,0:T(8,128)S(1)} %copy-done, ...), custom_call_target="tpu_custom_call" | custom-call | flops 134217728 | bytes 2097152 | tf_op jit(solution)/shard_map/early_slots/pallas_call | solution.py:211
  76.1 6.0 %collective-permute-done.21 = bf16[2,128,256]{2,1,0:T(8,128)(2,1)S(1)} collective-permute-done((bf16[2,128,256]{2,1,0:T(8,128)(2,1)S(1)}, bf16[2,128,256]{2,1,0:T(8,128)(2,1)S(1)}, u32[]{:S(2)}, u32[]{:S(2)}) %collective-permute-start.21) | collective-permute-done | bytes 131104 | tf_op jit(solution)/shard_map/ppermute | solution.py:287
  86.8 2.0 %collective-permute-start.26 = (bf16[128,256]{1,0:T(8,128)(2,1)S(1)}, bf16[128,256]{1,0:T(8,128)(2,1)S(1)}, u32[]{:S(2)}, u32[]{:S(2)}) collective-permute-start(bf16[128,256]{1,0:T(8,128)(2,1)S(1)} %get-tuple-element.170), channel_id=1, source_target_pairs={{0,64},{1,193},{2,66},{3,195},{4,68},{5,197},{6,70},{7,199},{8,72}... | collective-permute-start | bytes 196616 | tf_op jit(solution)/shard_map/ppermute | solution.py:223
  89.5 2.9 %collective-permute-done.25 = bf16[128,256]{1,0:T(8,128)(2,1)S(1)} collective-permute-done((bf16[128,256]{1,0:T(8,128)(2,1)S(1)}, bf16[128,256]{1,0:T(8,128)(2,1)S(1)}, u32[]{:S(2)}, u32[]{:S(2)}) %collective-permute-start.25) | collective-permute-done | bytes 65568 | tf_op jit(solution)/shard_map/ppermute | solution.py:223
  93.3 1.8 %collective-permute-start.28 = (bf16[128,256]{1,0:T(8,128)(2,1)S(1)}, bf16[128,256]{1,0:T(8,128)(2,1)S(1)}, u32[]{:S(2)}, u32[]{:S(2)}) collective-permute-start(bf16[128,256]{1,0:T(8,128)(2,1)S(1)} %get-tuple-element.218), channel_id=1, source_target_pairs={{0,1},{1,0},{2,3},{3,2},{4,5},{5,4},{6,7},{7,6},{8,9},{9,8},{10,11... | collective-permute-start | bytes 196616 | tf_op jit(solution)/shard_map/ppermute | solution.py:226
  96.5 2.5 %early_slots.8.before_ref = f32[512,256]{1,0:T(8,128)S(1)} custom-call(s32[4,112]{1,0:T(4,128)S(1)} %get-tuple-element.137.index_ref, f32[4,54]{1,0:T(4,128)S(1)} %get-tuple-element.138.weight_ref, bf16[4,17,512,128]{3,2,1,0:T(8,128)(2,1)S(1)} %get-tuple-element.139.blocks_ref, f32[6,128,256]{2,1,0:T(8,128)S(1)} %copy-done, ...), custom_call_target="tpu_custom_call" | custom-call | flops 134217728 | bytes 2097152 | tf_op jit(solution)/shard_map/early_slots/pallas_call | solution.py:211
  99.0 6.1 %collective-permute-done.30 = bf16[2,128,256]{2,1,0:T(8,128)(2,1)S(1)} collective-permute-done((bf16[2,128,256]{2,1,0:T(8,128)(2,1)S(1)}, bf16[2,128,256]{2,1,0:T(8,128)(2,1)S(1)}, u32[]{:S(2)}, u32[]{:S(2)}) %collective-permute-start.30) | collective-permute-done | bytes 131104 | tf_op jit(solution)/shard_map/ppermute | solution.py:287
  107.6 1.7 %last_slots.8 = (f32[128,256]{1,0:T(8,128)S(1)}, bf16[128,256]{1,0:T(8,128)(2,1)S(1)}, bf16[128,256]{1,0:T(8,128)(2,1)S(1)}, bf16[128,256]{1,0:T(8,128)(2,1)S(1)}) custom-call(s32[4,112]{1,0:T(4,128)S(1)} %get-tuple-element.137.index_ref, f32[4,54]{1,0:T(4,128)S(1)} %get-tuple-element.138.weight_ref, ...), custom_call_target="tpu_custom_call" | custom-call | flops 134217728 | bytes 2097152 | tf_op jit(solution)/shard_map/last_slots/pallas_call | solution.py:211
  112.0 2.7 %collective-permute-done.33 = bf16[128,256]{1,0:T(8,128)(2,1)S(1)} collective-permute-done((bf16[128,256]{1,0:T(8,128)(2,1)S(1)}, bf16[128,256]{1,0:T(8,128)(2,1)S(1)}, u32[]{:S(2)}, u32[]{:S(2)}) %collective-permute-start.33) | collective-permute-done | bytes 65568 | tf_op jit(solution)/shard_map/ppermute | solution.py:223
  118.4 2.0 %collective-permute-start.40 = (bf16[2,128,512]{2,1,0:T(8,128)(2,1)S(1)}, bf16[2,128,512]{2,1,0:T(8,128)(2,1)S(1)}, u32[]{:S(2)}, u32[]{:S(2)}) collective-permute-start(bf16[2,128,512]{2,1,0:T(8,128)(2,1)S(1)} %pad_maximum_fusion.3), channel_id=1, source_target_pairs={{0,64},{1,193},{2,66},{3,195},{4,68},{5,197},{6,70},{7,199},{8,72}... | collective-permute-start | bytes 786440 | tf_op jit(solution)/shard_map/ppermute | solution.py:223
  120.4 2.5 %early_slots.9.before_ref = f32[512,256]{1,0:T(8,128)S(1)} custom-call(s32[4,112]{1,0:T(4,128)S(1)} %get-tuple-element.137.index_ref, f32[4,54]{1,0:T(4,128)S(1)} %get-tuple-element.138.weight_ref, bf16[4,17,512,128]{3,2,1,0:T(8,128)(2,1)S(1)} %get-tuple-element.139.blocks_ref, f32[6,128,256]{2,1,0:T(8,128)S(1)} %copy-done, ...), custom_call_target="tpu_custom_call" | custom-call | flops 134217728 | bytes 2097152 | tf_op jit(solution)/shard_map/early_slots/pallas_call | solution.py:211
  122.9 4.5 %collective-permute-done.38 = bf16[2,128,256]{2,1,0:T(8,128)(2,1)S(1)} collective-permute-done((bf16[2,128,256]{2,1,0:T(8,128)(2,1)S(1)}, bf16[2,128,256]{2,1,0:T(8,128)(2,1)S(1)}, u32[]{:S(2)}, u32[]{:S(2)}) %collective-permute-start.38) | collective-permute-done | bytes 131104 | tf_op jit(solution)/shard_map/ppermute | solution.py:287
  129.9 1.6 %last_slots.9 = (f32[128,256]{1,0:T(8,128)S(1)}, bf16[128,256]{1,0:T(8,128)(2,1)S(1)}, bf16[128,256]{1,0:T(8,128)(2,1)S(1)}, bf16[128,256]{1,0:T(8,128)(2,1)S(1)}) custom-call(s32[4,112]{1,0:T(4,128)S(1)} %get-tuple-element.137.index_ref, f32[4,54]{1,0:T(4,128)S(1)} %get-tuple-element.138.weight_ref, ...), custom_call_target="tpu_custom_call" | custom-call | flops 134217728 | bytes 2097152 | tf_op jit(solution)/shard_map/last_slots/pallas_call | solution.py:211
  134.3 2.4 %collective-permute-done.41 = bf16[128,256]{1,0:T(8,128)(2,1)S(1)} collective-permute-done((bf16[128,256]{1,0:T(8,128)(2,1)S(1)}, bf16[128,256]{1,0:T(8,128)(2,1)S(1)}, u32[]{:S(2)}, u32[]{:S(2)}) %collective-permute-start.41) | collective-permute-done | bytes 65568 | tf_op jit(solution)/shard_map/ppermute | solution.py:223
  (125 shorter events, 51.7 us)
Async XLA Ops:
  1.0 12.9 %collective-permute-start.2 = (f32[128,256]{1,0:T(8,128)S(1)}, f32[128,256]{1,0:T(8,128)S(1)}, u32[]{:S(2)}, u32[]{:S(2)}) collective-permute-start(f32[128,256]{1,0:T(8,128)S(1)} %slice_bitcast_fusion.16.refs_0_), channel_id=1, source_target_pairs={{0,192},{1,65},{2,194},{3,67},{4,196},{5,69},{6,198},{7,71},{8,200... | collective-permute-start | bytes 393224 | tf_op jit(solution)/shard_map/ppermute | solution.py:223
  3.2 10.7 %collective-permute-start.1 = (f32[128,256]{1,0:T(8,128)S(1)}, f32[128,256]{1,0:T(8,128)S(1)}, u32[]{:S(2)}, u32[]{:S(2)}) collective-permute-start(f32[128,256]{1,0:T(8,128)S(1)} %slice_bitcast_fusion.16.refs_0_), channel_id=1, source_target_pairs={{0,64},{1,193},{2,66},{3,195},{4,68},{5,197},{6,70},{7,199},{8,72}... | collective-permute-start | bytes 393224 | tf_op jit(solution)/shard_map/ppermute | solution.py:223
  5.1 8.8 %collective-permute-start = (f32[128,256]{1,0:T(8,128)S(1)}, f32[128,256]{1,0:T(8,128)S(1)}, u32[]{:S(2)}, u32[]{:S(2)}) collective-permute-start(f32[128,256]{1,0:T(8,128)S(1)} %slice_bitcast_fusion.16.refs_0_), channel_id=1, source_target_pairs={{0,128},{1,129},{2,130},{3,131},{4,132},{5,133},{6,134},{7,135},{8... | collective-permute-start | bytes 393224 | tf_op jit(solution)/shard_map/ppermute | solution.py:223
  6.8 8.6 %collective-permute-start.3 = (bf16[2,128,512]{2,1,0:T(8,128)(2,1)S(1)}, bf16[2,128,512]{2,1,0:T(8,128)(2,1)S(1)}, u32[]{:S(2)}, u32[]{:S(2)}) collective-permute-start(bf16[2,128,512]{2,1,0:T(8,128)(2,1)S(1)} %get-tuple-element.227), channel_id=1, source_target_pairs={{0,64},{1,193},{2,66},{3,195},{4,68},{5,197},{6,70},{7,199},{8,72}... | collective-permute-start | bytes 786440 | tf_op jit(solution)/shard_map/ppermute | solution.py:223
  17.8 9.8 %collective-permute-start.6 = (bf16[2,128,256]{2,1,0:T(8,128)(2,1)S(1)}, bf16[2,128,256]{2,1,0:T(8,128)(2,1)S(1)}, u32[]{:S(2)}, u32[]{:S(2)}) collective-permute-start(bf16[2,128,256]{2,1,0:T(8,128)(2,1)S(1)} %maximum_select_fusion.refs_0_.refs_1_), channel_id=1, source_target_pairs={{4,0},{61,1},{6,2},{63,3},{8,4},{1,5},{10,6},{3,7},{12,8},{5,9},{1... | collective-permute-start | bytes 393224 | tf_op jit(solution)/shard_map/ppermute | solution.py:287
  19.9 9.9 %collective-permute-start.5 = (bf16[2,128,256]{2,1,0:T(8,128)(2,1)S(1)}, bf16[2,128,256]{2,1,0:T(8,128)(2,1)S(1)}, u32[]{:S(2)}, u32[]{:S(2)}) collective-permute-start(bf16[2,128,256]{2,1,0:T(8,128)(2,1)S(1)} %maximum_select_fusion.refs_0_.refs_1_), channel_id=1, source_target_pairs={{2,0},{63,1},{4,2},{1,3},{6,4},{3,5},{8,6},{5,7},{10,8},{7,9},{12,... | collective-permute-start | bytes 393224 | tf_op jit(solution)/shard_map/ppermute | solution.py:288
  22.5 12.4 %collective-permute-start.8 = (bf16[2,2,128,512]{3,2,1,0:T(8,128)(2,1)S(1)}, bf16[2,2,128,512]{3,2,1,0:T(8,128)(2,1)S(1)}, u32[]{:S(2)}, u32[]{:S(2)}) collective-permute-start(bf16[2,2,128,512]{3,2,1,0:T(8,128)(2,1)S(1)} %pad_maximum_fusion), channel_id=1, source_target_pairs={{0,192},{1,65},{2,194},{3,67},{4,196},{5,69},{6,198},{7,71},{8,200... | collective-permute-start | bytes 1572872 | tf_op jit(solution)/shard_map/ppermute | solution.py:223
  29.9 5.0 %collective-permute-start.7 = (bf16[4,128,256]{2,1,0:T(8,128)(2,1)S(1)}, bf16[4,128,256]{2,1,0:T(8,128)(2,1)S(1)}, u32[]{:S(2)}, u32[]{:S(2)}) collective-permute-start(bf16[4,128,256]{2,1,0:T(8,128)(2,1)S(1)} %constant_dynamic-update-slice_fusion.mine_ref.refs_2_), channel_id=1, source_target_pairs={{0,1},{1,0},{2,3},{3,2},{4,5},{5,4},{6,7},{7,6},{8,9},{9,8},{10,11... | collective-permute-start | bytes 786440 | tf_op jit(solution)/shard_map/ppermute | solution.py:226
  36.5 4.8 %collective-permute-start.9 = (bf16[128,256]{1,0:T(8,128)(2,1)S(1)}, bf16[128,256]{1,0:T(8,128)(2,1)S(1)}, u32[]{:S(2)}, u32[]{:S(2)}) collective-permute-start(bf16[128,256]{1,0:T(8,128)(2,1)S(1)} %get-tuple-element.133), channel_id=1, source_target_pairs={{0,128},{1,129},{2,130},{3,131},{4,132},{5,133},{6,134},{7,135},{8... | collective-permute-start | bytes 196616 | tf_op jit(solution)/shard_map/ppermute | solution.py:223
  36.9 5.0 %collective-permute-start.10 = (bf16[128,256]{1,0:T(8,128)(2,1)S(1)}, bf16[128,256]{1,0:T(8,128)(2,1)S(1)}, u32[]{:S(2)}, u32[]{:S(2)}) collective-permute-start(bf16[128,256]{1,0:T(8,128)(2,1)S(1)} %get-tuple-element.134), channel_id=1, source_target_pairs={{0,64},{1,193},{2,66},{3,195},{4,68},{5,197},{6,70},{7,199},{8,72}... | collective-permute-start | bytes 196616 | tf_op jit(solution)/shard_map/ppermute | solution.py:223
  42.0 6.9 %collective-permute-start.12 = (bf16[128,256]{1,0:T(8,128)(2,1)S(1)}, bf16[128,256]{1,0:T(8,128)(2,1)S(1)}, u32[]{:S(2)}, u32[]{:S(2)}) collective-permute-start(bf16[128,256]{1,0:T(8,128)(2,1)S(1)} %get-tuple-element.222), channel_id=1, source_target_pairs={{0,1},{1,0},{2,3},{3,2},{4,5},{5,4},{6,7},{7,6},{8,9},{9,8},{10,11... | collective-permute-start | bytes 196616 | tf_op jit(solution)/shard_map/ppermute | solution.py:226
  48.9 8.3 %collective-permute-start.14 = (bf16[2,128,256]{2,1,0:T(8,128)(2,1)S(1)}, bf16[2,128,256]{2,1,0:T(8,128)(2,1)S(1)}, u32[]{:S(2)}, u32[]{:S(2)}) collective-permute-start(bf16[2,128,256]{2,1,0:T(8,128)(2,1)S(1)} %maximum_select_fusion.1.refs_0_.refs_4_), channel_id=1, source_target_pairs={{4,0},{61,1},{6,2},{63,3},{8,4},{1,5},{10,6},{3,7},{12,8},{5,9},{1... | collective-permute-start | bytes 393224 | tf_op jit(solution)/shard_map/ppermute | solution.py:287
  50.8 8.9 %collective-permute-start.13 = (bf16[2,128,256]{2,1,0:T(8,128)(2,1)S(1)}, bf16[2,128,256]{2,1,0:T(8,128)(2,1)S(1)}, u32[]{:S(2)}, u32[]{:S(2)}) collective-permute-start(bf16[2,128,256]{2,1,0:T(8,128)(2,1)S(1)} %maximum_select_fusion.1.refs_0_.refs_4_), channel_id=1, source_target_pairs={{2,0},{63,1},{4,2},{1,3},{6,4},{3,5},{8,6},{5,7},{10,8},{7,9},{12,... | collective-permute-start | bytes 393224 | tf_op jit(solution)/shard_map/ppermute | solution.py:288
  60.0 12.7 %collective-permute-start.23 = (bf16[128,512]{1,0:T(8,128)(2,1)S(1)}, bf16[128,512]{1,0:T(8,128)(2,1)S(1)}, u32[]{:S(2)}, u32[]{:S(2)}) collective-permute-start(bf16[128,512]{1,0:T(8,128)(2,1)S(1)} %slice_bitcast_fusion.10), channel_id=1, source_target_pairs={{0,192},{1,65},{2,194},{3,67},{4,196},{5,69},{6,198},{7,71},{8,200... | collective-permute-start | bytes 393224 | tf_op jit(solution)/shard_map/ppermute | solution.py:223
  63.2 4.7 %collective-permute-start.16 = (bf16[128,256]{1,0:T(8,128)(2,1)S(1)}, bf16[128,256]{1,0:T(8,128)(2,1)S(1)}, u32[]{:S(2)}, u32[]{:S(2)}) collective-permute-start(bf16[128,256]{1,0:T(8,128)(2,1)S(1)} %get-tuple-element.150), channel_id=1, source_target_pairs={{0,128},{1,129},{2,130},{3,131},{4,132},{5,133},{6,134},{7,135},{8... | collective-permute-start | bytes 196616 | tf_op jit(solution)/shard_map/ppermute | solution.py:223
  64.2 5.1 %collective-permute-start.17 = (bf16[128,256]{1,0:T(8,128)(2,1)S(1)}, bf16[128,256]{1,0:T(8,128)(2,1)S(1)}, u32[]{:S(2)}, u32[]{:S(2)}) collective-permute-start(bf16[128,256]{1,0:T(8,128)(2,1)S(1)} %get-tuple-element.151), channel_id=1, source_target_pairs={{0,64},{1,193},{2,66},{3,195},{4,68},{5,197},{6,70},{7,199},{8,72}... | collective-permute-start | bytes 196616 | tf_op jit(solution)/shard_map/ppermute | solution.py:223
  72.7 10.8 %collective-permute-start.24 = (bf16[3,128,512]{2,1,0:T(8,128)(2,1)S(1)}, bf16[3,128,512]{2,1,0:T(8,128)(2,1)S(1)}, u32[]{:S(2)}, u32[]{:S(2)}) collective-permute-start(bf16[3,128,512]{2,1,0:T(8,128)(2,1)S(1)} %pad_maximum_fusion.1), channel_id=1, source_target_pairs={{0,64},{1,193},{2,66},{3,195},{4,68},{5,197},{6,70},{7,199},{8,72}... | collective-permute-start | bytes 1179656 | tf_op jit(solution)/shard_map/ppermute | solution.py:223
  73.6 8.5 %collective-permute-start.21 = (bf16[2,128,256]{2,1,0:T(8,128)(2,1)S(1)}, bf16[2,128,256]{2,1,0:T(8,128)(2,1)S(1)}, u32[]{:S(2)}, u32[]{:S(2)}) collective-permute-start(bf16[2,128,256]{2,1,0:T(8,128)(2,1)S(1)} %maximum_select_fusion.2.refs_0_.refs_7_), channel_id=1, source_target_pairs={{4,0},{61,1},{6,2},{63,3},{8,4},{1,5},{10,6},{3,7},{12,8},{5,9},{1... | collective-permute-start | bytes 393224 | tf_op jit(solution)/shard_map/ppermute | solution.py:287
  73.7 9.7 %collective-permute-start.20 = (bf16[2,128,256]{2,1,0:T(8,128)(2,1)S(1)}, bf16[2,128,256]{2,1,0:T(8,128)(2,1)S(1)}, u32[]{:S(2)}, u32[]{:S(2)}) collective-permute-start(bf16[2,128,256]{2,1,0:T(8,128)(2,1)S(1)} %maximum_select_fusion.2.refs_0_.refs_7_), channel_id=1, source_target_pairs={{2,0},{63,1},{4,2},{1,3},{6,4},{3,5},{8,6},{5,7},{10,8},{7,9},{12,... | collective-permute-start | bytes 393224 | tf_op jit(solution)/shard_map/ppermute | solution.py:288
  86.7 5.6 %collective-permute-start.25 = (bf16[128,256]{1,0:T(8,128)(2,1)S(1)}, bf16[128,256]{1,0:T(8,128)(2,1)S(1)}, u32[]{:S(2)}, u32[]{:S(2)}) collective-permute-start(bf16[128,256]{1,0:T(8,128)(2,1)S(1)} %get-tuple-element.169), channel_id=1, source_target_pairs={{0,128},{1,129},{2,130},{3,131},{4,132},{5,133},{6,134},{7,135},{8... | collective-permute-start | bytes 196616 | tf_op jit(solution)/shard_map/ppermute | solution.py:223
  86.8 5.8 %collective-permute-start.26 = (bf16[128,256]{1,0:T(8,128)(2,1)S(1)}, bf16[128,256]{1,0:T(8,128)(2,1)S(1)}, u32[]{:S(2)}, u32[]{:S(2)}) collective-permute-start(bf16[128,256]{1,0:T(8,128)(2,1)S(1)} %get-tuple-element.170), channel_id=1, source_target_pairs={{0,64},{1,193},{2,66},{3,195},{4,68},{5,197},{6,70},{7,199},{8,72}... | collective-permute-start | bytes 196616 | tf_op jit(solution)/shard_map/ppermute | solution.py:223
  88.9 4.4 %collective-permute-start.27 = (bf16[128,256]{1,0:T(8,128)(2,1)S(1)}, bf16[128,256]{1,0:T(8,128)(2,1)S(1)}, u32[]{:S(2)}, u32[]{:S(2)}) collective-permute-start(bf16[128,256]{1,0:T(8,128)(2,1)S(1)} %get-tuple-element.171), channel_id=1, source_target_pairs={{0,192},{1,65},{2,194},{3,67},{4,196},{5,69},{6,198},{7,71},{8,200... | collective-permute-start | bytes 196616 | tf_op jit(solution)/shard_map/ppermute | solution.py:223
  95.2 11.2 %collective-permute-start.32 = (bf16[3,128,512]{2,1,0:T(8,128)(2,1)S(1)}, bf16[3,128,512]{2,1,0:T(8,128)(2,1)S(1)}, u32[]{:S(2)}, u32[]{:S(2)}) collective-permute-start(bf16[3,128,512]{2,1,0:T(8,128)(2,1)S(1)} %pad_maximum_fusion.2), channel_id=1, source_target_pairs={{0,192},{1,65},{2,194},{3,67},{4,196},{5,69},{6,198},{7,71},{8,200... | collective-permute-start | bytes 1179656 | tf_op jit(solution)/shard_map/ppermute | solution.py:223
  96.1 9.0 %collective-permute-start.30 = (bf16[2,128,256]{2,1,0:T(8,128)(2,1)S(1)}, bf16[2,128,256]{2,1,0:T(8,128)(2,1)S(1)}, u32[]{:S(2)}, u32[]{:S(2)}) collective-permute-start(bf16[2,128,256]{2,1,0:T(8,128)(2,1)S(1)} %maximum_select_fusion.3.refs_0_.refs_10_), channel_id=1, source_target_pairs={{4,0},{61,1},{6,2},{63,3},{8,4},{1,5},{10,6},{3,7},{12,8},{5,9},{1... | collective-permute-start | bytes 393224 | tf_op jit(solution)/shard_map/ppermute | solution.py:287
  96.2 8.9 %collective-permute-start.29 = (bf16[2,128,256]{2,1,0:T(8,128)(2,1)S(1)}, bf16[2,128,256]{2,1,0:T(8,128)(2,1)S(1)}, u32[]{:S(2)}, u32[]{:S(2)}) collective-permute-start(bf16[2,128,256]{2,1,0:T(8,128)(2,1)S(1)} %maximum_select_fusion.3.refs_0_.refs_10_), channel_id=1, source_target_pairs={{2,0},{63,1},{4,2},{1,3},{6,4},{3,5},{8,6},{5,7},{10,8},{7,9},{12,... | collective-permute-start | bytes 393224 | tf_op jit(solution)/shard_map/ppermute | solution.py:288
  109.2 5.5 %collective-permute-start.33 = (bf16[128,256]{1,0:T(8,128)(2,1)S(1)}, bf16[128,256]{1,0:T(8,128)(2,1)S(1)}, u32[]{:S(2)}, u32[]{:S(2)}) collective-permute-start(bf16[128,256]{1,0:T(8,128)(2,1)S(1)} %get-tuple-element.189), channel_id=1, source_target_pairs={{0,128},{1,129},{2,130},{3,131},{4,132},{5,133},{6,134},{7,135},{8... | collective-permute-start | bytes 196616 | tf_op jit(solution)/shard_map/ppermute | solution.py:223
  110.4 5.0 %collective-permute-start.34 = (bf16[128,256]{1,0:T(8,128)(2,1)S(1)}, bf16[128,256]{1,0:T(8,128)(2,1)S(1)}, u32[]{:S(2)}, u32[]{:S(2)}) collective-permute-start(bf16[128,256]{1,0:T(8,128)(2,1)S(1)} %get-tuple-element.190), channel_id=1, source_target_pairs={{0,64},{1,193},{2,66},{3,195},{4,68},{5,197},{6,70},{7,199},{8,72}... | collective-permute-start | bytes 196616 | tf_op jit(solution)/shard_map/ppermute | solution.py:223
  117.8 9.6 %collective-permute-start.38 = (bf16[2,128,256]{2,1,0:T(8,128)(2,1)S(1)}, bf16[2,128,256]{2,1,0:T(8,128)(2,1)S(1)}, u32[]{:S(2)}, u32[]{:S(2)}) collective-permute-start(bf16[2,128,256]{2,1,0:T(8,128)(2,1)S(1)} %maximum_select_fusion.4.refs_0_), channel_id=1, source_target_pairs={{4,0},{61,1},{6,2},{63,3},{8,4},{1,5},{10,6},{3,7},{12,8},{5,9},{1... | collective-permute-start | bytes 393224 | tf_op jit(solution)/shard_map/ppermute | solution.py:287
  117.9 10.0 %collective-permute-start.37 = (bf16[2,128,256]{2,1,0:T(8,128)(2,1)S(1)}, bf16[2,128,256]{2,1,0:T(8,128)(2,1)S(1)}, u32[]{:S(2)}, u32[]{:S(2)}) collective-permute-start(bf16[2,128,256]{2,1,0:T(8,128)(2,1)S(1)} %maximum_select_fusion.4.refs_0_), channel_id=1, source_target_pairs={{2,0},{63,1},{4,2},{1,3},{6,4},{3,5},{8,6},{5,7},{10,8},{7,9},{12,... | collective-permute-start | bytes 393224 | tf_op jit(solution)/shard_map/ppermute | solution.py:288
  118.4 10.3 %collective-permute-start.40 = (bf16[2,128,512]{2,1,0:T(8,128)(2,1)S(1)}, bf16[2,128,512]{2,1,0:T(8,128)(2,1)S(1)}, u32[]{:S(2)}, u32[]{:S(2)}) collective-permute-start(bf16[2,128,512]{2,1,0:T(8,128)(2,1)S(1)} %pad_maximum_fusion.3), channel_id=1, source_target_pairs={{0,64},{1,193},{2,66},{3,195},{4,68},{5,197},{6,70},{7,199},{8,72}... | collective-permute-start | bytes 786440 | tf_op jit(solution)/shard_map/ppermute | solution.py:223
  131.6 5.2 %collective-permute-start.41 = (bf16[128,256]{1,0:T(8,128)(2,1)S(1)}, bf16[128,256]{1,0:T(8,128)(2,1)S(1)}, u32[]{:S(2)}, u32[]{:S(2)}) collective-permute-start(bf16[128,256]{1,0:T(8,128)(2,1)S(1)} %get-tuple-element.212), channel_id=1, source_target_pairs={{0,128},{1,129},{2,130},{3,131},{4,132},{5,133},{6,134},{7,135},{8... | collective-permute-start | bytes 196616 | tf_op jit(solution)/shard_map/ppermute | solution.py:223
  132.1 5.6 %collective-permute-start.42 = (bf16[128,256]{1,0:T(8,128)(2,1)S(1)}, bf16[128,256]{1,0:T(8,128)(2,1)S(1)}, u32[]{:S(2)}, u32[]{:S(2)}) collective-permute-start(bf16[128,256]{1,0:T(8,128)(2,1)S(1)} %get-tuple-element.213), channel_id=1, source_target_pairs={{0,64},{1,193},{2,66},{3,195},{4,68},{5,197},{6,70},{7,199},{8,72}... | collective-permute-start | bytes 196616 | tf_op jit(solution)/shard_map/ppermute | solution.py:223
  (18 other events, 118.0 us)

commit v3 on v2

v3 whole, which is shorter than its diff:
```python
import functools

import jax
import jax.numpy as jnp
from jax import lax
from jax.experimental import pallas as pl
from jax.experimental.pallas import tpu as pltpu
from jax.sharding import PartitionSpec as P

VMEM = pl.BlockSpec(memory_space=pltpu.VMEM)
SMEM = pl.BlockSpec(memory_space=pltpu.SMEM)
HBM = pl.BlockSpec(memory_space=pltpu.HBM)
MIB = 2**20
GROUP = 4
NEAR = 8
TABLE_LIMIT = 2 * MIB
SOON_LIMIT = 48 * MIB
LATE_LIMIT = 40 * MIB


def row_moves(count, delta):
    pairs = []
    for target in range(count):
        step = 2 * delta if target % 2 == 0 else -2 * delta
        pairs.append(((target + step) % count, target))
    return pairs


def swap_moves(count):
    return [(source, source ^ 1) for source in range(count)]


def partners(cols, col, odd):
    one, two = (col ^ 1, cols - 1 - col) if odd == 0 else (cols - 1 - col, col ^ 1)
    return one, two, (col + 2) % cols


def col_moves(cols, rows, which):
    return [
        (col * rows + row, partners(cols, col, row % 2)[which] * rows + row)
        for col in range(cols)
        for row in range(rows)
    ]


def split(value):
    high = value.astype(jnp.bfloat16)
    return high, (value - high.astype(jnp.float32)).astype(jnp.bfloat16)


def product(left, right):
    return jnp.dot(left, right, preferred_element_type=jnp.float32)


def exact_product(left, right):
    high, low = split(right)
    return product(left, high) + product(left, low)


def run_copies(copies):
    for copy in copies:
        copy.start()
    for copy in copies:
        copy.wait()


def fill_kernel(source_ref, start, out_ref, sem):
    run_copies([pltpu.make_async_copy(source_ref.at[pl.ds(start, out_ref.shape[0])], out_ref, sem)])


def soon_fill_kernel(factor_ref, out_ref, sems):
    fill_kernel(factor_ref, 0, out_ref, sems.at[0])


def late_fill_kernel(factor_ref, out_ref, sems):
    fill_kernel(factor_ref, 1, out_ref, sems.at[0])


def order_kernel(meta_ref, start_ref, first_ref):
    share = first_ref.shape[1]
    for index in range(4):
        start = pl.multiple_of(meta_ref[1 + index] * share, share)
        first_ref[index] = start_ref[:, pl.ds(start, share)]


def table_kernel(
    level_count, dep_rows, meta_ref, column_ref, count_ref, scale_ref, index_ref, weight_ref
):
    own_chip = meta_ref[0] // 2
    turn = 1 - 2 * (meta_ref[0] % 2)
    room = weight_ref.shape[1]
    inverse = (2**16 + level_count - 1) // level_count
    for at, dep_row in enumerate(dep_rows):
        for position in range(NEAR):
            index_ref[at, position] = 0
            weight_ref[at, position] = 0.0

        def put(position, slot, place, scale):
            index_ref[at, position] = slot
            index_ref[at, room + position] = place
            weight_ref[at, position] = -scale

        def collect(slot, found):
            column = column_ref[dep_row, slot]
            shard = lax.shift_right_logical(column * inverse, 16)
            from_level = column - shard * level_count
            forward = (lax.shift_right_logical(shard, 1) - own_chip) * turn
            parity = lax.bitwise_and(shard, 1)
            rest = (from_level != dep_row) | (forward == 0)
            piece = parity + jnp.where(forward == 0, 0, 2 * jnp.abs(forward) - 2)
            start = jnp.where(forward == 0, 2, jnp.where(forward > 0, 4, 8))
            place = jnp.where(from_level != dep_row, 10 * from_level + start, 0) + piece
            position = jnp.where(rest, NEAR + found, jnp.where(forward > 0, 4, 0) + piece)
            put(position, slot, place, scale_ref[dep_row, slot])
            return found + rest.astype(jnp.int32)

        found = lax.fori_loop(0, count_ref[dep_row], collect, 0)
        for extra in range(GROUP - 1):
            put(NEAR + found + extra, 0, 0, 0.0)
        index_ref[at, 2 * room] = (found + GROUP - 1) // GROUP
        index_ref[at, 2 * room + 1] = meta_ref[1]


def first_kernel(first_ref, *refs):
    own_ref, *piece_refs, out_ref = refs
    total = exact_product(first_ref[0], own_ref[...])
    for index, piece_ref in enumerate(piece_refs):
        total += product(first_ref[1 + index], piece_ref[...])
    out_ref[...] = total.astype(out_ref.dtype)


def early_kernel(level, row, index_ref, weight_ref, blocks_ref, right_ref, *refs):
    *piece_refs, sum_ref, near_ref, near_weight_ref, stored_ref = refs
    at = max(level - 2, 0)
    room = weight_ref.shape[1]
    start = 0
    for piece_ref in piece_refs:
        stored_ref[pl.ds(start, piece_ref.shape[0])] = piece_ref[...]
        start += piece_ref.shape[0]
    share = right_ref.shape[1]
    sum_ref[...] = jnp.zeros_like(sum_ref)
    start = pl.multiple_of(index_ref[row, 2 * room + 1] * share, share)
    sum_ref[pl.ds(start, share), :] = right_ref[level]

    def add_group(step, carry):
        total = sum_ref[...]
        for offset in range(GROUP):
            position = NEAR + GROUP * step + offset
            part = product(
                blocks_ref[at, index_ref[row, position]],
                stored_ref[index_ref[row, room + position]],
            )
            total += weight_ref[row, position] * part
        sum_ref[...] = total
        return carry

    lax.fori_loop(0, index_ref[row, 2 * room], add_group, 0)
    for position in range(NEAR):
        near_ref[position] = blocks_ref[at, index_ref[row, position]]
        near_weight_ref[position] = jnp.full(near_weight_ref.shape[1:], weight_ref[row, position])


def with_pieces(total, first, near_ref, near_weight_ref, pieces_ref):
    for index in range(pieces_ref.shape[0]):
        part = product(near_ref[first + index], pieces_ref[index])
        total += near_weight_ref[first + index] * part
    return total


def middle_kernel(near_ref, near_weight_ref, before_ref, mine_ref, sum_ref):
    sum_ref[...] = with_pieces(before_ref[...], 4, near_ref, near_weight_ref, mine_ref)


def last_kernel(near_ref, near_weight_ref, before_ref, theirs_ref, *refs):
    *diag_refs, own_ref, one_ref, two_ref, across_ref = refs
    total = with_pieces(before_ref[...], 0, near_ref, near_weight_ref, theirs_ref)
    blocks = jnp.concatenate([ref[...] for ref in diag_refs], axis=0)
    total = exact_product(blocks, total)
    share = own_ref.shape[0]
    for index, ref in enumerate((own_ref, one_ref, two_ref, across_ref)):
        ref[...] = total[index * share : (index + 1) * share].astype(ref.dtype)


def per_device(factor_blocks, block_scales, dep_column, dep_count, diag_inverse, right_side):
    level_count, share, block_rows = diag_inverse.shape
    slots = factor_blocks.shape[1]
    width = right_side.shape[2]
    rows, cols = lax.axis_size("row"), lax.axis_size("col")
    shard = lax.axis_index("row").astype(jnp.int32)
    col = lax.axis_index("col").astype(jnp.int32)
    even = shard % 2 == 0
    one = jnp.where(even, col ^ 1, cols - 1 - col)
    two = jnp.where(even, cols - 1 - col, col ^ 1)
    meta = jnp.stack([shard, col, one, two, (col + 2) % cols])
    bf16, f32 = jnp.bfloat16, jnp.float32
    shape = jax.ShapeDtypeStruct
    room = NEAR + slots + GROUP - 1
    wide = shape((block_rows, width), f32)
    piece = shape((share, width), bf16)

    def call(body, out_shape, in_specs, out_specs, operands, limit, scratch=(), flops=2**27, name=None):
        return pl.pallas_call(
            body,
            out_shape=out_shape,
            in_specs=in_specs,
            out_specs=out_specs,
            scratch_shapes=list(scratch),
            cost_estimate=pl.CostEstimate(flops=flops, bytes_accessed=2 * MIB, transcendentals=0),
            compiler_params=pltpu.CompilerParams(vmem_limit_bytes=limit),
            name=name,
        )(*operands)

    def along_col(value, which):
        return lax.ppermute(value, ("col", "row"), col_moves(cols, rows, which))

    def swap(value):
        return lax.ppermute(value, "row", swap_moves(rows))

    def after(value, *others):
        return lax.optimization_barrier((value, *others))[0]

    own = right_side[0]
    own_rounded = own.astype(bf16)
    arrived = [along_col(own_rounded, which) for which in (2, 0, 1)]
    diag_later = after(diag_inverse, own_rounded)
    start_diag, *own_diags = [diag_later[at] for at in range(level_count)]
    half_way = along_col(own_diags[0], 0)

    def list_slots(dep_rows, meta):
        return call(
            functools.partial(table_kernel, level_count, dep_rows),
            [shape((len(dep_rows), 2 * room + 2), jnp.int32), shape((len(dep_rows), room), f32)],
            [SMEM] * 4,
            [SMEM] * 2,
            (meta, dep_column, dep_count, block_scales),
            TABLE_LIMIT,
            name="table",
        )

    first = call(
        order_kernel,
        shape((4, share, share), bf16),
        [SMEM, VMEM],
        VMEM,
        (after(meta, own_rounded), start_diag),
        2 * MIB,
        name="order",
    )
    opposite, by_one, by_two = arrived
    opposite, by_one, by_two, first = lax.optimization_barrier((opposite, by_one, by_two, first))
    solved = call(
        first_kernel,
        piece,
        [VMEM] * 5,
        VMEM,
        (first, own, by_one, by_two, opposite),
        4 * MIB,
        name="first_solve",
    )
    outputs = [solved]
    pieces = []
    diags = {}
    late = level_count - 3
    for level in range(1, level_count):
        other = swap(solved)
        if level == 1:
            sent = [own_diags[0], half_way, own_diags[1]]
            got = along_col(after(jnp.stack(sent), solved), 1)
            diags[1] = (own_diags[0], half_way, got[0], got[1])
            half_way = got[2]
        elif level == 2:
            sent = [own_diags[1], half_way, *own_diags[2:]]
            got = along_col(after(jnp.stack(sent), solved), 0)
            diags[2] = (own_diags[1], got[0], half_way, got[1])
            by_one_diags = got[2:]
        elif level == 3:
            sent = [*own_diags[2:], *(by_one_diags[at] for at in range(late))]
            got = along_col(after(jnp.stack(sent), solved), 1)
            for at in range(late):
                diags[3 + at] = (own_diags[2 + at], by_one_diags[at], got[at], got[late + at])
        pair = jnp.where(even, jnp.stack([solved, other]), jnp.stack([other, solved]))
        far = lax.ppermute(pair, "row", row_moves(rows, 2))
        near = lax.ppermute(pair, "row", row_moves(rows, 1))
        stored = after([pair, *(x for three in pieces for x in three)], pair)
        if level == 1:
            index, weight = list_slots((0, 1), after(meta, pair))
            blocks = call(
                soon_fill_kernel,
                shape((1, *factor_blocks.shape[1:]), bf16),
                [HBM],
                VMEM,
                (after(factor_blocks, pair),),
                SOON_LIMIT,
                [pltpu.SemaphoreType.DMA((1,))],
                name="soon_fill",
            )
        early, near_blocks, near_weight = call(
            functools.partial(early_kernel, level, 1 if level == 2 else 0),
            [
                wide,
                shape((NEAR, *factor_blocks.shape[2:]), bf16),
                shape((NEAR, 1, width), f32),
            ],
            [SMEM] * 2 + [VMEM] * (2 + len(stored)),
            [VMEM] * 3,
            (index, weight, blocks, right_side, *stored),
            20 * MIB,
            [pltpu.VMEM((2 + 10 * (level - 1), share, width), bf16)],
            name="early_slots",
        )
        near, far, early = lax.optimization_barrier((near, far, early))
        mine = jnp.concatenate([near, far], axis=0)
        theirs = swap(mine)
        middle = call(
            middle_kernel,
            wide,
            [VMEM] * 4,
            VMEM,
            (near_blocks, near_weight, early, mine),
            8 * MIB,
            name="middle_slots",
        )
        theirs, middle = lax.optimization_barrier((theirs, middle))
        pieces.append((pair, mine, theirs))
        own, *parts = call(
            last_kernel,
            [shape((share, width), f32)] + [piece] * 3,
            [VMEM] * 8,
            [VMEM] * 4,
            (near_blocks, near_weight, middle, theirs, *diags[level]),
            8 * MIB,
            name="last_slots",
        )
        arrived = [along_col(parts[which_part], which_part) for which_part in (2, 0, 1)]
        if level == 1:
            blocks = call(
                late_fill_kernel,
                shape((level_count - 2, *factor_blocks.shape[1:]), bf16),
                [HBM],
                VMEM,
                (after(factor_blocks, parts[0]),),
                LATE_LIMIT,
                [pltpu.SemaphoreType.DMA((1,))],
                name="late_fill",
            )
            *arrived, blocks = lax.optimization_barrier((*arrived, blocks))
        elif level + 1 < level_count:
            index, weight = list_slots((level,), after(meta, parts[0]))
            *arrived, index = lax.optimization_barrier((*arrived, index))
        total = own
        for part in arrived:
            total = total + part.astype(f32)
        solved = total.astype(bf16)
        outputs.append(solved)
    return jnp.stack(outputs, axis=0)


def solution(mesh):
    in_specs = (
        P("row", None, None, "col"),
        P("row", None),
        P("row", None),
        P("row"),
        P("row", "col", None),
        P("row", "col", None),
    )
    return jax.shard_map(
        per_device, mesh=mesh, in_specs=in_specs, out_specs=P("row", "col", None), check_vma=False
    )
```

time: 139 us -> 129 us (0.928)
  starting transfers between devices: 50.5 us -> 42.3 us
  Pallas kernels: 31.5 us -> 29.7 us
    ppermute x5, waiting for transfers between devices: 19.5 us -> 28 us  [per_device(): far = lax.ppermute(pair, 'row', row_moves(rows, 2))]
    ppermute x10, starting transfers between devices: 19.2 us -> 11.1 us  [swap(): return lax.ppermute(value, 'row', swap_moves(rows))]
    ppermute x24 -> x22, waiting for transfers between devices: 18.6 us -> 13.3 us  [along_col(): return lax.ppermute(value, ('col', 'row'), col_moves(cols, rows, which))]
    ppermute x5, waiting for transfers between devices: 6.55 us -> 3.86 us  [per_device(): near = lax.ppermute(pair, 'row', row_moves(rows, 1))]
    pallas_call x21 -> x23, Pallas kernels: 31.5 us -> 29.7 us  [call(): pl.pallas_call(body, out_shape=out_shape, in_specs=in_specs, out_specs=ou...]
    ppermute x24 -> x22, starting transfers between devices: 24.4 us -> 24.2 us  [along_col(): return lax.ppermute(value, ('col', 'row'), col_moves(cols, rows, which))]
  transfers between devices with their start and end apart: 44 -> 42, of which waited for: 33 -> 28; matrix products, arithmetic and copies ran while one was open for 2% -> 2% of each run, Pallas kernels for 18% -> 19%
where the time goes in v3:
time: 129 us; the launch traced here: 128 us
  waiting for transfers between devices  51.4 us (40%)
  starting transfers between devices  42.3 us (33%)
  Pallas kernels  29.7 us (23%)
  local copies, waits for them, and re-layouts  3.58 us (3%)
    pallas_call x23, Pallas kernels, call(): pl.pallas_call(body, out_shape=out_shape, in_specs=in_specs, out_specs=ou...  29.7 us
    ppermute x5, waiting for transfers between devices, per_device(): far = lax.ppermute(pair, 'row', row_moves(rows, 2))  28 us
    ppermute x22, starting transfers between devices, along_col(): return lax.ppermute(value, ('col', 'row'), col_moves(cols, rows, which))  24.2 us
    ppermute x22, waiting for transfers between devices, along_col(): return lax.ppermute(value, ('col', 'row'), col_moves(cols, rows, which))  13.3 us
    ppermute x10, starting transfers between devices, swap(): return lax.ppermute(value, 'row', swap_moves(rows))  11.1 us
    ppermute x10, waiting for transfers between devices, swap(): return lax.ppermute(value, 'row', swap_moves(rows))  6.29 us
    ppermute x5, starting transfers between devices, per_device(): far = lax.ppermute(pair, 'row', row_moves(rows, 2))  4.85 us
    ppermute x5, waiting for transfers between devices, per_device(): near = lax.ppermute(pair, 'row', row_moves(rows, 1))  3.86 us
  transfers between devices with their start and end apart: 42, of which 28 were waited for; matrix products, arithmetic and copies ran while one was open for 2% of the time, Pallas kernels for 19%

profile of v3, /device:TPU:1, one launch (start us, length us, event | category | flops | bytes accessed | tf_op | source)
XLA Modules:
  0.0 128.5 jit_solution(5206074606612878541)
XLA Ops:
  1.0 2.2 %collective-permute-start.2 = (bf16[128,256]{1,0:T(8,128)(2,1)S(1)}, bf16[128,256]{1,0:T(8,128)(2,1)S(1)}, u32[]{:S(2)}, u32[]{:S(2)}) collective-permute-start(bf16[128,256]{1,0:T(8,128)(2,1)S(1)} %fusion.2), channel_id=1, source_target_pairs={{0,192},{1,65},{2,194},{3,67},{4,196},{5,69},{6,198},{7,71},{8,200... | collective-permute-start | bytes 196616 | tf_op jit(solution)/shard_map/ppermute | solution.py:214
  3.2 1.9 %collective-permute-start.1 = (bf16[128,256]{1,0:T(8,128)(2,1)S(1)}, bf16[128,256]{1,0:T(8,128)(2,1)S(1)}, u32[]{:S(2)}, u32[]{:S(2)}) collective-permute-start(bf16[128,256]{1,0:T(8,128)(2,1)S(1)} %fusion.2), channel_id=1, source_target_pairs={{0,64},{1,193},{2,66},{3,195},{4,68},{5,197},{6,70},{7,199},{8,72}... | collective-permute-start | bytes 196616 | tf_op jit(solution)/shard_map/ppermute | solution.py:214
  10.0 2.2 %collective-permute-start.3 = (bf16[128,256]{1,0:T(8,128)(2,1)S(1)}, bf16[128,256]{1,0:T(8,128)(2,1)S(1)}, u32[]{:S(2)}, u32[]{:S(2)}) collective-permute-start(bf16[128,256]{1,0:T(8,128)(2,1)S(1)} %first_solve.1), channel_id=1, source_target_pairs={{0,1},{1,0},{2,3},{3,2},{4,5},{5,4},{6,7},{7,6},{8,9},{9,8},{10,11... | collective-permute-start | bytes 196616 | tf_op jit(solution)/shard_map/ppermute | solution.py:217
  13.4 3.0 %collective-permute-start.5 = (bf16[2,128,256]{2,1,0:T(8,128)(2,1)S(1)}, bf16[2,128,256]{2,1,0:T(8,128)(2,1)S(1)}, u32[]{:S(2)}, u32[]{:S(2)}) collective-permute-start(bf16[2,128,256]{2,1,0:T(8,128)(2,1)S(1)} %maximum_select_fusion.refs_0_.refs_1_), channel_id=1, source_target_pairs={{4,0},{61,1},{6,2},{63,3},{8,4},{1,5},{10,6},{3,7},{12,8},{5,9},{1... | collective-permute-start | bytes 393224 | tf_op jit(solution)/shard_map/ppermute | solution.py:282
  16.4 1.6 %collective-permute-start.4 = (bf16[2,128,256]{2,1,0:T(8,128)(2,1)S(1)}, bf16[2,128,256]{2,1,0:T(8,128)(2,1)S(1)}, u32[]{:S(2)}, u32[]{:S(2)}) collective-permute-start(bf16[2,128,256]{2,1,0:T(8,128)(2,1)S(1)} %maximum_select_fusion.refs_0_.refs_1_), channel_id=1, source_target_pairs={{2,0},{63,1},{4,2},{1,3},{6,4},{3,5},{8,6},{5,7},{10,8},{7,9},{12,... | collective-permute-start | bytes 393224 | tf_op jit(solution)/shard_map/ppermute | solution.py:283
  19.2 1.6 %soon_fill.1.blocks_ref = bf16[1,17,512,128]{3,2,1,0:T(8,128)(2,1)S(1)} custom-call(bf16[5,17,512,128]{3,2,1,0:T(8,128)(2,1)} %factor_ref.1), custom_call_target="tpu_custom_call" | custom-call | flops 134217728 | bytes 2097152 | tf_op jit(solution)/shard_map/soon_fill/pallas_call | solution.py:202
  20.9 1.8 %table.4 = (s32[2,58]{1,0:T(2,128)S(1)}, f32[2,28]{1,0:T(2,128)S(1)}) custom-call(s32[5]{0:T(128)S(1)} %stack.118.meta_ref, s32[5,17]{1,0:T(8,128)S(1)} %copy-done.1, s32[5]{0:T(128)S(1)} %copy-done.3, f32[5,17]{1,0:T(8,128)S(1)} %copy-done.2), custom_call_target="tpu_custom_call" | custom-call | flops 134217728 | bytes 2097152 | tf_op jit(solution)/shard_map/table/pallas_call | solution.py:202
  24.0 2.3 %collective-permute-done.4 = bf16[2,128,256]{2,1,0:T(8,128)(2,1)S(1)} collective-permute-done((bf16[2,128,256]{2,1,0:T(8,128)(2,1)S(1)}, bf16[2,128,256]{2,1,0:T(8,128)(2,1)S(1)}, u32[]{:S(2)}, u32[]{:S(2)}) %collective-permute-start.4) | collective-permute-done | bytes 131104 | tf_op jit(solution)/shard_map/ppermute | solution.py:283
  26.3 2.9 %collective-permute-start.6 = (bf16[4,128,256]{2,1,0:T(8,128)(2,1)S(1)}, bf16[4,128,256]{2,1,0:T(8,128)(2,1)S(1)}, u32[]{:S(2)}, u32[]{:S(2)}) collective-permute-start(bf16[4,128,256]{2,1,0:T(8,128)(2,1)S(1)} %constant_dynamic-update-slice_fusion.mine_ref.refs_2_), channel_id=1, source_target_pairs={{0,1},{1,0},{2,3},{3,2},{4,5},{5,4},{6,7},{7,6},{8,9},{9,8},{10,11... | collective-permute-start | bytes 786440 | tf_op jit(solution)/shard_map/ppermute | solution.py:217
  31.6 2.0 %collective-permute-start.9 = (bf16[128,256]{1,0:T(8,128)(2,1)S(1)}, bf16[128,256]{1,0:T(8,128)(2,1)S(1)}, u32[]{:S(2)}, u32[]{:S(2)}) collective-permute-start(bf16[128,256]{1,0:T(8,128)(2,1)S(1)} %get-tuple-element.160), channel_id=1, source_target_pairs={{0,128},{1,129},{2,130},{3,131},{4,132},{5,133},{6,134},{7,135},{8... | collective-permute-start | bytes 196616 | tf_op jit(solution)/shard_map/ppermute | solution.py:214
  34.9 3.5 %late_fill.1.blocks_ref = bf16[4,17,512,128]{3,2,1,0:T(8,128)(2,1)S(1)} custom-call(bf16[5,17,512,128]{3,2,1,0:T(8,128)(2,1)} %factor_ref.1), custom_call_target="tpu_custom_call" | custom-call | flops 134217728 | bytes 2097152 | tf_op jit(solution)/shard_map/late_fill/pallas_call | solution.py:202
  38.5 1.4 %collective-permute-done.10 = bf16[128,256]{1,0:T(8,128)(2,1)S(1)} collective-permute-done((bf16[128,256]{1,0:T(8,128)(2,1)S(1)}, bf16[128,256]{1,0:T(8,128)(2,1)S(1)}, u32[]{:S(2)}, u32[]{:S(2)}) %collective-permute-start.10) | collective-permute-done | bytes 65568 | tf_op jit(solution)/shard_map/ppermute | solution.py:214
  41.9 1.4 %collective-permute-start.14 = (bf16[2,128,256]{2,1,0:T(8,128)(2,1)S(1)}, bf16[2,128,256]{2,1,0:T(8,128)(2,1)S(1)}, u32[]{:S(2)}, u32[]{:S(2)}) collective-permute-start(bf16[2,128,256]{2,1,0:T(8,128)(2,1)S(1)} %maximum_select_fusion.1.refs_0_.refs_4_), channel_id=1, source_target_pairs={{4,0},{61,1},{6,2},{63,3},{8,4},{1,5},{10,6},{3,7},{12,8},{5,9},{1... | collective-permute-start | bytes 393224 | tf_op jit(solution)/shard_map/ppermute | solution.py:282
  43.3 1.6 %early_slots.6 = (f32[512,256]{1,0:T(8,128)S(1)}, bf16[8,512,128]{2,1,0:T(8,128)(2,1)S(1)}, f32[8,1,256]{2,1,0:T(1,128)S(1)}) custom-call(s32[2,58]{1,0:T(2,128)S(1)} %get-tuple-element.146.index_ref, f32[2,28]{1,0:T(2,128)S(1)} %get-tuple-element.147.weight_ref, bf16[4,17,512,128]{3,2,1,0:T(8,128)(2,1)S(1)} %late_fill.1.blocks_ref, ...), custom_call_target="tpu_custom_call" | custom-call | flops 134217728 | bytes 2097152 | tf_op jit(solution)/shard_map/early_slots/pallas_call | solution.py:202
  44.9 6.5 %collective-permute-done.14 = bf16[2,128,256]{2,1,0:T(8,128)(2,1)S(1)} collective-permute-done((bf16[2,128,256]{2,1,0:T(8,128)(2,1)S(1)}, bf16[2,128,256]{2,1,0:T(8,128)(2,1)S(1)}, u32[]{:S(2)}, u32[]{:S(2)}) %collective-permute-start.14) | collective-permute-done | bytes 131104 | tf_op jit(solution)/shard_map/ppermute | solution.py:282
  55.2 2.0 %collective-permute-start.17 = (bf16[128,256]{1,0:T(8,128)(2,1)S(1)}, bf16[128,256]{1,0:T(8,128)(2,1)S(1)}, u32[]{:S(2)}, u32[]{:S(2)}) collective-permute-start(bf16[128,256]{1,0:T(8,128)(2,1)S(1)} %get-tuple-element.182), channel_id=1, source_target_pairs={{0,128},{1,129},{2,130},{3,131},{4,132},{5,133},{6,134},{7,135},{8... | collective-permute-start | bytes 196616 | tf_op jit(solution)/shard_map/ppermute | solution.py:214
  58.6 1.7 %table.5 = (s32[1,58]{1,0:T(1,128)S(1)}, f32[1,28]{1,0:T(1,128)S(1)}) custom-call(s32[5]{0:T(128)S(1)} %stack.118.meta_ref, s32[5,17]{1,0:T(8,128)S(1)} %copy-done.1, s32[5]{0:T(128)S(1)} %copy-done.3, f32[5,17]{1,0:T(8,128)S(1)} %copy-done.2), custom_call_target="tpu_custom_call" | custom-call | flops 134217728 | bytes 2097152 | tf_op jit(solution)/shard_map/table/pallas_call | solution.py:202
  60.9 1.9 %collective-permute-done.18 = bf16[128,256]{1,0:T(8,128)(2,1)S(1)} collective-permute-done((bf16[128,256]{1,0:T(8,128)(2,1)S(1)}, bf16[128,256]{1,0:T(8,128)(2,1)S(1)}, u32[]{:S(2)}, u32[]{:S(2)}) %collective-permute-start.18) | collective-permute-done | bytes 65568 | tf_op jit(solution)/shard_map/ppermute | solution.py:214
  64.8 2.0 %early_slots.7 = (f32[512,256]{1,0:T(8,128)S(1)}, bf16[8,512,128]{2,1,0:T(8,128)(2,1)S(1)}, f32[8,1,256]{2,1,0:T(1,128)S(1)}) custom-call(s32[1,58]{1,0:T(1,128)S(1)} %get-tuple-element.190.index_ref, f32[1,28]{1,0:T(1,128)S(1)} %get-tuple-element.191.weight_ref, bf16[4,17,512,128]{3,2,1,0:T(8,128)(2,1)S(1)} %late_fill.1.blocks_ref, ...), custom_call_target="tpu_custom_call" | custom-call | flops 134217728 | bytes 2097152 | tf_op jit(solution)/shard_map/early_slots/pallas_call | solution.py:202
  66.8 7.3 %collective-permute-done.22 = bf16[2,128,256]{2,1,0:T(8,128)(2,1)S(1)} collective-permute-done((bf16[2,128,256]{2,1,0:T(8,128)(2,1)S(1)}, bf16[2,128,256]{2,1,0:T(8,128)(2,1)S(1)}, u32[]{:S(2)}, u32[]{:S(2)}) %collective-permute-start.22) | collective-permute-done | bytes 131104 | tf_op jit(solution)/shard_map/ppermute | solution.py:282
  78.8 1.3 %collective-permute-start.27 = (bf16[128,256]{1,0:T(8,128)(2,1)S(1)}, bf16[128,256]{1,0:T(8,128)(2,1)S(1)}, u32[]{:S(2)}, u32[]{:S(2)}) collective-permute-start(bf16[128,256]{1,0:T(8,128)(2,1)S(1)} %get-tuple-element.211), channel_id=1, source_target_pairs={{0,192},{1,65},{2,194},{3,67},{4,196},{5,69},{6,198},{7,71},{8,200... | collective-permute-start | bytes 196616 | tf_op jit(solution)/shard_map/ppermute | solution.py:214
  81.0 1.6 %table.6 = (s32[1,58]{1,0:T(1,128)S(1)}, f32[1,28]{1,0:T(1,128)S(1)}) custom-call(s32[5]{0:T(128)S(1)} %stack.118.meta_ref, s32[5,17]{1,0:T(8,128)S(1)} %copy-done.1, s32[5]{0:T(128)S(1)} %copy-done.3, f32[5,17]{1,0:T(8,128)S(1)} %copy-done.2), custom_call_target="tpu_custom_call" | custom-call | flops 134217728 | bytes 2097152 | tf_op jit(solution)/shard_map/table/pallas_call | solution.py:202
  83.3 1.9 %collective-permute-done.26 = bf16[128,256]{1,0:T(8,128)(2,1)S(1)} collective-permute-done((bf16[128,256]{1,0:T(8,128)(2,1)S(1)}, bf16[128,256]{1,0:T(8,128)(2,1)S(1)}, u32[]{:S(2)}, u32[]{:S(2)}) %collective-permute-start.26) | collective-permute-done | bytes 65568 | tf_op jit(solution)/shard_map/ppermute | solution.py:214
  87.2 2.1 %early_slots.8 = (f32[512,256]{1,0:T(8,128)S(1)}, bf16[8,512,128]{2,1,0:T(8,128)(2,1)S(1)}, f32[8,1,256]{2,1,0:T(1,128)S(1)}) custom-call(s32[1,58]{1,0:T(1,128)S(1)} %get-tuple-element.217.index_ref, f32[1,28]{1,0:T(1,128)S(1)} %get-tuple-element.218.weight_ref, bf16[4,17,512,128]{3,2,1,0:T(8,128)(2,1)S(1)} %late_fill.1.blocks_ref, ...), custom_call_target="tpu_custom_call" | custom-call | flops 134217728 | bytes 2097152 | tf_op jit(solution)/shard_map/early_slots/pallas_call | solution.py:202
  89.2 7.2 %collective-permute-done.30 = bf16[2,128,256]{2,1,0:T(8,128)(2,1)S(1)} collective-permute-done((bf16[2,128,256]{2,1,0:T(8,128)(2,1)S(1)}, bf16[2,128,256]{2,1,0:T(8,128)(2,1)S(1)}, u32[]{:S(2)}, u32[]{:S(2)}) %collective-permute-start.30) | collective-permute-done | bytes 131104 | tf_op jit(solution)/shard_map/ppermute | solution.py:282
  99.7 1.6 %collective-permute-start.32 = (bf16[128,256]{1,0:T(8,128)(2,1)S(1)}, bf16[128,256]{1,0:T(8,128)(2,1)S(1)}, u32[]{:S(2)}, u32[]{:S(2)}) collective-permute-start(bf16[128,256]{1,0:T(8,128)(2,1)S(1)} %get-tuple-element.238), channel_id=1, source_target_pairs={{0,128},{1,129},{2,130},{3,131},{4,132},{5,133},{6,134},{7,135},{8... | collective-permute-start | bytes 196616 | tf_op jit(solution)/shard_map/ppermute | solution.py:214
  103.0 1.7 %table.7 = (s32[1,58]{1,0:T(1,128)S(1)}, f32[1,28]{1,0:T(1,128)S(1)}) custom-call(s32[5]{0:T(128)S(1)} %stack.118.meta_ref, s32[5,17]{1,0:T(8,128)S(1)} %copy-done.1, s32[5]{0:T(128)S(1)} %copy-done.3, f32[5,17]{1,0:T(8,128)S(1)} %copy-done.2), custom_call_target="tpu_custom_call" | custom-call | flops 134217728 | bytes 2097152 | tf_op jit(solution)/shard_map/table/pallas_call | solution.py:202
  105.4 1.8 %collective-permute-done.33 = bf16[128,256]{1,0:T(8,128)(2,1)S(1)} collective-permute-done((bf16[128,256]{1,0:T(8,128)(2,1)S(1)}, bf16[128,256]{1,0:T(8,128)(2,1)S(1)}, u32[]{:S(2)}, u32[]{:S(2)}) %collective-permute-start.33) | collective-permute-done | bytes 65568 | tf_op jit(solution)/shard_map/ppermute | solution.py:214
  109.2 2.5 %early_slots.9 = (f32[512,256]{1,0:T(8,128)S(1)}, bf16[8,512,128]{2,1,0:T(8,128)(2,1)S(1)}, f32[8,1,256]{2,1,0:T(1,128)S(1)}) custom-call(s32[1,58]{1,0:T(1,128)S(1)} %get-tuple-element.246.index_ref, f32[1,28]{1,0:T(1,128)S(1)} %get-tuple-element.247.weight_ref, bf16[4,17,512,128]{3,2,1,0:T(8,128)(2,1)S(1)} %late_fill.1.blocks_ref, ...), custom_call_target="tpu_custom_call" | custom-call | flops 134217728 | bytes 2097152 | tf_op jit(solution)/shard_map/early_slots/pallas_call | solution.py:202
  111.8 6.7 %collective-permute-done.37 = bf16[2,128,256]{2,1,0:T(8,128)(2,1)S(1)} collective-permute-done((bf16[2,128,256]{2,1,0:T(8,128)(2,1)S(1)}, bf16[2,128,256]{2,1,0:T(8,128)(2,1)S(1)}, u32[]{:S(2)}, u32[]{:S(2)}) %collective-permute-start.37) | collective-permute-done | bytes 131104 | tf_op jit(solution)/shard_map/ppermute | solution.py:282
  124.5 2.0 %collective-permute-done.39 = bf16[128,256]{1,0:T(8,128)(2,1)S(1)} collective-permute-done((bf16[128,256]{1,0:T(8,128)(2,1)S(1)}, bf16[128,256]{1,0:T(8,128)(2,1)S(1)}, u32[]{:S(2)}, u32[]{:S(2)}) %collective-permute-start.39) | collective-permute-done | bytes 65568 | tf_op jit(solution)/shard_map/ppermute | solution.py:214
  126.4 1.4 %collective-permute-done.40 = bf16[128,256]{1,0:T(8,128)(2,1)S(1)} collective-permute-done((bf16[128,256]{1,0:T(8,128)(2,1)S(1)}, bf16[128,256]{1,0:T(8,128)(2,1)S(1)}, u32[]{:S(2)}, u32[]{:S(2)}) %collective-permute-start.40) | collective-permute-done | bytes 65568 | tf_op jit(solution)/shard_map/ppermute | solution.py:214
  (120 shorter events, 45.3 us)
Async XLA Ops:
  1.0 7.8 %collective-permute-start.2 = (bf16[128,256]{1,0:T(8,128)(2,1)S(1)}, bf16[128,256]{1,0:T(8,128)(2,1)S(1)}, u32[]{:S(2)}, u32[]{:S(2)}) collective-permute-start(bf16[128,256]{1,0:T(8,128)(2,1)S(1)} %fusion.2), channel_id=1, source_target_pairs={{0,192},{1,65},{2,194},{3,67},{4,196},{5,69},{6,198},{7,71},{8,200... | collective-permute-start | bytes 196616 | tf_op jit(solution)/shard_map/ppermute | solution.py:214
  3.2 5.5 %collective-permute-start.1 = (bf16[128,256]{1,0:T(8,128)(2,1)S(1)}, bf16[128,256]{1,0:T(8,128)(2,1)S(1)}, u32[]{:S(2)}, u32[]{:S(2)}) collective-permute-start(bf16[128,256]{1,0:T(8,128)(2,1)S(1)} %fusion.2), channel_id=1, source_target_pairs={{0,64},{1,193},{2,66},{3,195},{4,68},{5,197},{6,70},{7,199},{8,72}... | collective-permute-start | bytes 196616 | tf_op jit(solution)/shard_map/ppermute | solution.py:214
  5.1 4.7 %collective-permute-start = (bf16[128,256]{1,0:T(8,128)(2,1)S(1)}, bf16[128,256]{1,0:T(8,128)(2,1)S(1)}, u32[]{:S(2)}, u32[]{:S(2)}) collective-permute-start(bf16[128,256]{1,0:T(8,128)(2,1)S(1)} %fusion.2), channel_id=1, source_target_pairs={{0,128},{1,129},{2,130},{3,131},{4,132},{5,133},{6,134},{7,135},{8... | collective-permute-start | bytes 196616 | tf_op jit(solution)/shard_map/ppermute | solution.py:214
  12.3 5.7 %collective-permute-start.7 = (bf16[128,512]{1,0:T(8,128)(2,1)S(1)}, bf16[128,512]{1,0:T(8,128)(2,1)S(1)}, u32[]{:S(2)}, u32[]{:S(2)}) collective-permute-start(bf16[128,512]{1,0:T(8,128)(2,1)S(1)} %get-tuple-element.288.refs_0_), channel_id=1, source_target_pairs={{0,64},{1,193},{2,66},{3,195},{4,68},{5,197},{6,70},{7,199},{8,72}... | collective-permute-start | bytes 393224 | tf_op jit(solution)/shard_map/ppermute | solution.py:214
  13.4 10.7 %collective-permute-start.5 = (bf16[2,128,256]{2,1,0:T(8,128)(2,1)S(1)}, bf16[2,128,256]{2,1,0:T(8,128)(2,1)S(1)}, u32[]{:S(2)}, u32[]{:S(2)}) collective-permute-start(bf16[2,128,256]{2,1,0:T(8,128)(2,1)S(1)} %maximum_select_fusion.refs_0_.refs_1_), channel_id=1, source_target_pairs={{4,0},{61,1},{6,2},{63,3},{8,4},{1,5},{10,6},{3,7},{12,8},{5,9},{1... | collective-permute-start | bytes 393224 | tf_op jit(solution)/shard_map/ppermute | solution.py:282
  16.4 9.9 %collective-permute-start.4 = (bf16[2,128,256]{2,1,0:T(8,128)(2,1)S(1)}, bf16[2,128,256]{2,1,0:T(8,128)(2,1)S(1)}, u32[]{:S(2)}, u32[]{:S(2)}) collective-permute-start(bf16[2,128,256]{2,1,0:T(8,128)(2,1)S(1)} %maximum_select_fusion.refs_0_.refs_1_), channel_id=1, source_target_pairs={{2,0},{63,1},{4,2},{1,3},{6,4},{3,5},{8,6},{5,7},{10,8},{7,9},{12,... | collective-permute-start | bytes 393224 | tf_op jit(solution)/shard_map/ppermute | solution.py:283
  18.1 12.3 %collective-permute-start.8 = (bf16[3,128,512]{2,1,0:T(8,128)(2,1)S(1)}, bf16[3,128,512]{2,1,0:T(8,128)(2,1)S(1)}, u32[]{:S(2)}, u32[]{:S(2)}) collective-permute-start(bf16[3,128,512]{2,1,0:T(8,128)(2,1)S(1)} %pad_maximum_fusion.2), channel_id=1, source_target_pairs={{0,192},{1,65},{2,194},{3,67},{4,196},{5,69},{6,198},{7,71},{8,200... | collective-permute-start | bytes 1179656 | tf_op jit(solution)/shard_map/ppermute | solution.py:214
  26.3 4.1 %collective-permute-start.6 = (bf16[4,128,256]{2,1,0:T(8,128)(2,1)S(1)}, bf16[4,128,256]{2,1,0:T(8,128)(2,1)S(1)}, u32[]{:S(2)}, u32[]{:S(2)}) collective-permute-start(bf16[4,128,256]{2,1,0:T(8,128)(2,1)S(1)} %constant_dynamic-update-slice_fusion.mine_ref.refs_2_), channel_id=1, source_target_pairs={{0,1},{1,0},{2,3},{3,2},{4,5},{5,4},{6,7},{7,6},{8,9},{9,8},{10,11... | collective-permute-start | bytes 786440 | tf_op jit(solution)/shard_map/ppermute | solution.py:217
  31.6 6.9 %collective-permute-start.9 = (bf16[128,256]{1,0:T(8,128)(2,1)S(1)}, bf16[128,256]{1,0:T(8,128)(2,1)S(1)}, u32[]{:S(2)}, u32[]{:S(2)}) collective-permute-start(bf16[128,256]{1,0:T(8,128)(2,1)S(1)} %get-tuple-element.160), channel_id=1, source_target_pairs={{0,128},{1,129},{2,130},{3,131},{4,132},{5,133},{6,134},{7,135},{8... | collective-permute-start | bytes 196616 | tf_op jit(solution)/shard_map/ppermute | solution.py:214
  33.6 4.9 %collective-permute-start.11 = (bf16[128,256]{1,0:T(8,128)(2,1)S(1)}, bf16[128,256]{1,0:T(8,128)(2,1)S(1)}, u32[]{:S(2)}, u32[]{:S(2)}) collective-permute-start(bf16[128,256]{1,0:T(8,128)(2,1)S(1)} %get-tuple-element.162), channel_id=1, source_target_pairs={{0,192},{1,65},{2,194},{3,67},{4,196},{5,69},{6,198},{7,71},{8,200... | collective-permute-start | bytes 196616 | tf_op jit(solution)/shard_map/ppermute | solution.py:214
  34.2 5.6 %collective-permute-start.10 = (bf16[128,256]{1,0:T(8,128)(2,1)S(1)}, bf16[128,256]{1,0:T(8,128)(2,1)S(1)}, u32[]{:S(2)}, u32[]{:S(2)}) collective-permute-start(bf16[128,256]{1,0:T(8,128)(2,1)S(1)} %get-tuple-element.161), channel_id=1, source_target_pairs={{0,64},{1,193},{2,66},{3,195},{4,68},{5,197},{6,70},{7,199},{8,72}... | collective-permute-start | bytes 196616 | tf_op jit(solution)/shard_map/ppermute | solution.py:214
  41.0 13.0 %collective-permute-start.16 = (bf16[5,128,512]{2,1,0:T(8,128)(2,1)S(1)}, bf16[5,128,512]{2,1,0:T(8,128)(2,1)S(1)}, u32[]{:S(2)}, u32[]{:S(2)}) collective-permute-start(bf16[5,128,512]{2,1,0:T(8,128)(2,1)S(1)} %pad_maximum_fusion.1), channel_id=1, source_target_pairs={{0,64},{1,193},{2,66},{3,195},{4,68},{5,197},{6,70},{7,199},{8,72}... | collective-permute-start | bytes 1966088 | tf_op jit(solution)/shard_map/ppermute | solution.py:214
  41.9 9.5 %collective-permute-start.14 = (bf16[2,128,256]{2,1,0:T(8,128)(2,1)S(1)}, bf16[2,128,256]{2,1,0:T(8,128)(2,1)S(1)}, u32[]{:S(2)}, u32[]{:S(2)}) collective-permute-start(bf16[2,128,256]{2,1,0:T(8,128)(2,1)S(1)} %maximum_select_fusion.1.refs_0_.refs_4_), channel_id=1, source_target_pairs={{4,0},{61,1},{6,2},{63,3},{8,4},{1,5},{10,6},{3,7},{12,8},{5,9},{1... | collective-permute-start | bytes 393224 | tf_op jit(solution)/shard_map/ppermute | solution.py:282
  43.3 9.1 %collective-permute-start.13 = (bf16[2,128,256]{2,1,0:T(8,128)(2,1)S(1)}, bf16[2,128,256]{2,1,0:T(8,128)(2,1)S(1)}, u32[]{:S(2)}, u32[]{:S(2)}) collective-permute-start(bf16[2,128,256]{2,1,0:T(8,128)(2,1)S(1)} %maximum_select_fusion.1.refs_0_.refs_4_), channel_id=1, source_target_pairs={{2,0},{63,1},{4,2},{1,3},{6,4},{3,5},{8,6},{5,7},{10,8},{7,9},{12,... | collective-permute-start | bytes 393224 | tf_op jit(solution)/shard_map/ppermute | solution.py:283
  55.2 5.1 %collective-permute-start.17 = (bf16[128,256]{1,0:T(8,128)(2,1)S(1)}, bf16[128,256]{1,0:T(8,128)(2,1)S(1)}, u32[]{:S(2)}, u32[]{:S(2)}) collective-permute-start(bf16[128,256]{1,0:T(8,128)(2,1)S(1)} %get-tuple-element.182), channel_id=1, source_target_pairs={{0,128},{1,129},{2,130},{3,131},{4,132},{5,133},{6,134},{7,135},{8... | collective-permute-start | bytes 196616 | tf_op jit(solution)/shard_map/ppermute | solution.py:214
  57.8 5.0 %collective-permute-start.18 = (bf16[128,256]{1,0:T(8,128)(2,1)S(1)}, bf16[128,256]{1,0:T(8,128)(2,1)S(1)}, u32[]{:S(2)}, u32[]{:S(2)}) collective-permute-start(bf16[128,256]{1,0:T(8,128)(2,1)S(1)} %get-tuple-element.183), channel_id=1, source_target_pairs={{0,64},{1,193},{2,66},{3,195},{4,68},{5,197},{6,70},{7,199},{8,72}... | collective-permute-start | bytes 196616 | tf_op jit(solution)/shard_map/ppermute | solution.py:214
  63.7 12.8 %collective-permute-start.24 = (bf16[6,128,512]{2,1,0:T(8,128)(2,1)S(1)}, bf16[6,128,512]{2,1,0:T(8,128)(2,1)S(1)}, u32[]{:S(2)}, u32[]{:S(2)}) collective-permute-start(bf16[6,128,512]{2,1,0:T(8,128)(2,1)S(1)} %pad_maximum_fusion), channel_id=1, source_target_pairs={{0,192},{1,65},{2,194},{3,67},{4,196},{5,69},{6,198},{7,71},{8,200... | collective-permute-start | bytes 2359304 | tf_op jit(solution)/shard_map/ppermute | solution.py:214
  64.6 9.5 %collective-permute-start.22 = (bf16[2,128,256]{2,1,0:T(8,128)(2,1)S(1)}, bf16[2,128,256]{2,1,0:T(8,128)(2,1)S(1)}, u32[]{:S(2)}, u32[]{:S(2)}) collective-permute-start(bf16[2,128,256]{2,1,0:T(8,128)(2,1)S(1)} %maximum_select_fusion.2.refs_0_.refs_7_), channel_id=1, source_target_pairs={{4,0},{61,1},{6,2},{63,3},{8,4},{1,5},{10,6},{3,7},{12,8},{5,9},{1... | collective-permute-start | bytes 393224 | tf_op jit(solution)/shard_map/ppermute | solution.py:282
  64.7 9.4 %collective-permute-start.21 = (bf16[2,128,256]{2,1,0:T(8,128)(2,1)S(1)}, bf16[2,128,256]{2,1,0:T(8,128)(2,1)S(1)}, u32[]{:S(2)}, u32[]{:S(2)}) collective-permute-start(bf16[2,128,256]{2,1,0:T(8,128)(2,1)S(1)} %maximum_select_fusion.2.refs_0_.refs_7_), channel_id=1, source_target_pairs={{2,0},{63,1},{4,2},{1,3},{6,4},{3,5},{8,6},{5,7},{10,8},{7,9},{12,... | collective-permute-start | bytes 393224 | tf_op jit(solution)/shard_map/ppermute | solution.py:283
  77.7 5.0 %collective-permute-start.25 = (bf16[128,256]{1,0:T(8,128)(2,1)S(1)}, bf16[128,256]{1,0:T(8,128)(2,1)S(1)}, u32[]{:S(2)}, u32[]{:S(2)}) collective-permute-start(bf16[128,256]{1,0:T(8,128)(2,1)S(1)} %get-tuple-element.209), channel_id=1, source_target_pairs={{0,128},{1,129},{2,130},{3,131},{4,132},{5,133},{6,134},{7,135},{8... | collective-permute-start | bytes 196616 | tf_op jit(solution)/shard_map/ppermute | solution.py:214
  78.8 4.5 %collective-permute-start.27 = (bf16[128,256]{1,0:T(8,128)(2,1)S(1)}, bf16[128,256]{1,0:T(8,128)(2,1)S(1)}, u32[]{:S(2)}, u32[]{:S(2)}) collective-permute-start(bf16[128,256]{1,0:T(8,128)(2,1)S(1)} %get-tuple-element.211), channel_id=1, source_target_pairs={{0,192},{1,65},{2,194},{3,67},{4,196},{5,69},{6,198},{7,71},{8,200... | collective-permute-start | bytes 196616 | tf_op jit(solution)/shard_map/ppermute | solution.py:214
  80.1 5.1 %collective-permute-start.26 = (bf16[128,256]{1,0:T(8,128)(2,1)S(1)}, bf16[128,256]{1,0:T(8,128)(2,1)S(1)}, u32[]{:S(2)}, u32[]{:S(2)}) collective-permute-start(bf16[128,256]{1,0:T(8,128)(2,1)S(1)} %get-tuple-element.210), channel_id=1, source_target_pairs={{0,64},{1,193},{2,66},{3,195},{4,68},{5,197},{6,70},{7,199},{8,72}... | collective-permute-start | bytes 196616 | tf_op jit(solution)/shard_map/ppermute | solution.py:214
  86.6 9.8 %collective-permute-start.30 = (bf16[2,128,256]{2,1,0:T(8,128)(2,1)S(1)}, bf16[2,128,256]{2,1,0:T(8,128)(2,1)S(1)}, u32[]{:S(2)}, u32[]{:S(2)}) collective-permute-start(bf16[2,128,256]{2,1,0:T(8,128)(2,1)S(1)} %maximum_select_fusion.3.refs_0_.refs_10_), channel_id=1, source_target_pairs={{4,0},{61,1},{6,2},{63,3},{8,4},{1,5},{10,6},{3,7},{12,8},{5,9},{1... | collective-permute-start | bytes 393224 | tf_op jit(solution)/shard_map/ppermute | solution.py:282
  86.9 9.8 %collective-permute-start.29 = (bf16[2,128,256]{2,1,0:T(8,128)(2,1)S(1)}, bf16[2,128,256]{2,1,0:T(8,128)(2,1)S(1)}, u32[]{:S(2)}, u32[]{:S(2)}) collective-permute-start(bf16[2,128,256]{2,1,0:T(8,128)(2,1)S(1)} %maximum_select_fusion.3.refs_0_.refs_10_), channel_id=1, source_target_pairs={{2,0},{63,1},{4,2},{1,3},{6,4},{3,5},{8,6},{5,7},{10,8},{7,9},{12,... | collective-permute-start | bytes 393224 | tf_op jit(solution)/shard_map/ppermute | solution.py:283
  99.7 5.1 %collective-permute-start.32 = (bf16[128,256]{1,0:T(8,128)(2,1)S(1)}, bf16[128,256]{1,0:T(8,128)(2,1)S(1)}, u32[]{:S(2)}, u32[]{:S(2)}) collective-permute-start(bf16[128,256]{1,0:T(8,128)(2,1)S(1)} %get-tuple-element.238), channel_id=1, source_target_pairs={{0,128},{1,129},{2,130},{3,131},{4,132},{5,133},{6,134},{7,135},{8... | collective-permute-start | bytes 196616 | tf_op jit(solution)/shard_map/ppermute | solution.py:214
  101.3 4.1 %collective-permute-start.34 = (bf16[128,256]{1,0:T(8,128)(2,1)S(1)}, bf16[128,256]{1,0:T(8,128)(2,1)S(1)}, u32[]{:S(2)}, u32[]{:S(2)}) collective-permute-start(bf16[128,256]{1,0:T(8,128)(2,1)S(1)} %get-tuple-element.240), channel_id=1, source_target_pairs={{0,192},{1,65},{2,194},{3,67},{4,196},{5,69},{6,198},{7,71},{8,200... | collective-permute-start | bytes 196616 | tf_op jit(solution)/shard_map/ppermute | solution.py:214
  102.0 5.2 %collective-permute-start.33 = (bf16[128,256]{1,0:T(8,128)(2,1)S(1)}, bf16[128,256]{1,0:T(8,128)(2,1)S(1)}, u32[]{:S(2)}, u32[]{:S(2)}) collective-permute-start(bf16[128,256]{1,0:T(8,128)(2,1)S(1)} %get-tuple-element.239), channel_id=1, source_target_pairs={{0,64},{1,193},{2,66},{3,195},{4,68},{5,197},{6,70},{7,199},{8,72}... | collective-permute-start | bytes 196616 | tf_op jit(solution)/shard_map/ppermute | solution.py:214
  108.9 9.5 %collective-permute-start.37 = (bf16[2,128,256]{2,1,0:T(8,128)(2,1)S(1)}, bf16[2,128,256]{2,1,0:T(8,128)(2,1)S(1)}, u32[]{:S(2)}, u32[]{:S(2)}) collective-permute-start(bf16[2,128,256]{2,1,0:T(8,128)(2,1)S(1)} %maximum_select_fusion.4.refs_0_), channel_id=1, source_target_pairs={{4,0},{61,1},{6,2},{63,3},{8,4},{1,5},{10,6},{3,7},{12,8},{5,9},{1... | collective-permute-start | bytes 393224 | tf_op jit(solution)/shard_map/ppermute | solution.py:282
  109.0 9.8 %collective-permute-start.36 = (bf16[2,128,256]{2,1,0:T(8,128)(2,1)S(1)}, bf16[2,128,256]{2,1,0:T(8,128)(2,1)S(1)}, u32[]{:S(2)}, u32[]{:S(2)}) collective-permute-start(bf16[2,128,256]{2,1,0:T(8,128)(2,1)S(1)} %maximum_select_fusion.4.refs_0_), channel_id=1, source_target_pairs={{2,0},{63,1},{4,2},{1,3},{6,4},{3,5},{8,6},{5,7},{10,8},{7,9},{12,... | collective-permute-start | bytes 393224 | tf_op jit(solution)/shard_map/ppermute | solution.py:283
  121.7 4.7 %collective-permute-start.39 = (bf16[128,256]{1,0:T(8,128)(2,1)S(1)}, bf16[128,256]{1,0:T(8,128)(2,1)S(1)}, u32[]{:S(2)}, u32[]{:S(2)}) collective-permute-start(bf16[128,256]{1,0:T(8,128)(2,1)S(1)} %get-tuple-element.270), channel_id=1, source_target_pairs={{0,128},{1,129},{2,130},{3,131},{4,132},{5,133},{6,134},{7,135},{8... | collective-permute-start | bytes 196616 | tf_op jit(solution)/shard_map/ppermute | solution.py:214
  122.7 5.1 %collective-permute-start.40 = (bf16[128,256]{1,0:T(8,128)(2,1)S(1)}, bf16[128,256]{1,0:T(8,128)(2,1)S(1)}, u32[]{:S(2)}, u32[]{:S(2)}) collective-permute-start(bf16[128,256]{1,0:T(8,128)(2,1)S(1)} %get-tuple-element.271), channel_id=1, source_target_pairs={{0,64},{1,193},{2,66},{3,195},{4,68},{5,197},{6,70},{7,199},{8,72}... | collective-permute-start | bytes 196616 | tf_op jit(solution)/shard_map/ppermute | solution.py:214
  124.0 3.8 %collective-permute-start.41 = (bf16[128,256]{1,0:T(8,128)(2,1)S(1)}, bf16[128,256]{1,0:T(8,128)(2,1)S(1)}, u32[]{:S(2)}, u32[]{:S(2)}) collective-permute-start(bf16[128,256]{1,0:T(8,128)(2,1)S(1)} %get-tuple-element.272), channel_id=1, source_target_pairs={{0,192},{1,65},{2,194},{3,67},{4,196},{5,69},{6,198},{7,71},{8,200... | collective-permute-start | bytes 196616 | tf_op jit(solution)/shard_map/ppermute | solution.py:214
  (16 other events, 131.4 us)

commit v4 on v3

--- a/solution.py
+++ b/solution.py
@@ -224,7 +224,7 @@
     arrived = [along_col(own_rounded, which) for which in (2, 0, 1)]
     diag_later = after(diag_inverse, own_rounded)
     start_diag, *own_diags = [diag_later[at] for at in range(level_count)]
-    half_way = along_col(own_diags[0], 0)
+    half_way = along_col(jnp.stack(own_diags[:2]), 0)
 
     def list_slots(dep_rows, meta):
         return call(
@@ -263,27 +263,21 @@
     late = level_count - 3
     for level in range(1, level_count):
         other = swap(solved)
-        if level == 1:
-            sent = [own_diags[0], half_way, own_diags[1]]
+        if level == 2:
+            sent = [own_diags[1], half_way[1], *own_diags[2:]]
             got = along_col(after(jnp.stack(sent), solved), 1)
-            diags[1] = (own_diags[0], half_way, got[0], got[1])
-            half_way = got[2]
-        elif level == 2:
-            sent = [own_diags[1], half_way, *own_diags[2:]]
+            diags[2] = (own_diags[1], half_way[1], got[0], got[1])
+            by_two_diags = got[2:]
+        elif level == 3:
+            sent = [*own_diags[2:], *(by_two_diags[at] for at in range(late))]
             got = along_col(after(jnp.stack(sent), solved), 0)
-            diags[2] = (own_diags[1], got[0], half_way, got[1])
-            by_one_diags = got[2:]
-        elif level == 3:
-            sent = [*own_diags[2:], *(by_one_diags[at] for at in range(late))]
-            got = along_col(after(jnp.stack(sent), solved), 1)
             for at in range(late):
-                diags[3 + at] = (own_diags[2 + at], by_one_diags[at], got[at], got[late + at])
+                diags[3 + at] = (own_diags[2 + at], got[at], by_two_diags[at], got[late + at])
         pair = jnp.where(even, jnp.stack([solved, other]), jnp.stack([other, solved]))
         far = lax.ppermute(pair, "row", row_moves(rows, 2))
         near = lax.ppermute(pair, "row", row_moves(rows, 1))
         stored = after([pair, *(x for three in pieces for x in three)], pair)
         if level == 1:
-            index, weight = list_slots((0, 1), after(meta, pair))
             blocks = call(
                 soon_fill_kernel,
                 shape((1, *factor_blocks.shape[1:]), bf16),
@@ -294,6 +288,9 @@
                 [pltpu.SemaphoreType.DMA((1,))],
                 name="soon_fill",
             )
+            got = along_col(after(jnp.stack([own_diags[0], half_way[0]]), blocks), 1)
+            diags[1] = (own_diags[0], half_way[0], got[0], got[1])
+            index, weight = list_slots((0, 1), after(meta, blocks))
         early, near_blocks, near_weight = call(
             functools.partial(early_kernel, level, 1 if level == 2 else 0),
             [

time: 129 us -> 135 us (1.047)
  starting transfers between devices: 42.3 us -> 46.6 us
    ppermute x22, starting transfers between devices: 24.2 us -> 26.8 us  [along_col(): return lax.ppermute(value, ('col', 'row'), col_moves(cols, rows, which))]
    ppermute x5, waiting for transfers between devices: 3.86 us -> 5.99 us  [per_device(): near = lax.ppermute(pair, 'row', row_moves(rows, 1))]
    ppermute x10, starting transfers between devices: 11.1 us -> 12.6 us  [swap(): return lax.ppermute(value, 'row', swap_moves(rows))]
  transfers between devices with their start and end apart: 42 -> 42, of which waited for: 28 -> 28; matrix products, arithmetic and copies ran while one was open for 2% -> 3% of each run, Pallas kernels for 19% -> 18%
where the time goes in v4:
time: 135 us
  waiting for transfers between devices  52.4 us (39%)
  starting transfers between devices  46.6 us (35%)
  Pallas kernels  29.6 us (22%)
  local copies, waits for them, and re-layouts  4.57 us (3%)
    pallas_call x23, Pallas kernels, call(): pl.pallas_call(body, out_shape=out_shape, in_specs=in_specs, out_specs=ou...  29.6 us
    ppermute x5, waiting for transfers between devices, per_device(): far = lax.ppermute(pair, 'row', row_moves(rows, 2))  27.2 us
    ppermute x22, starting transfers between devices, along_col(): return lax.ppermute(value, ('col', 'row'), col_moves(cols, rows, which))  26.8 us
    ppermute x22, waiting for transfers between devices, along_col(): return lax.ppermute(value, ('col', 'row'), col_moves(cols, rows, which))  13 us
    ppermute x10, starting transfers between devices, swap(): return lax.ppermute(value, 'row', swap_moves(rows))  12.6 us
    ppermute x10, waiting for transfers between devices, swap(): return lax.ppermute(value, 'row', swap_moves(rows))  6.17 us
    ppermute x5, waiting for transfers between devices, per_device(): near = lax.ppermute(pair, 'row', row_moves(rows, 1))  5.99 us
    ppermute x5, starting transfers between devices, per_device(): far = lax.ppermute(pair, 'row', row_moves(rows, 2))  4.3 us
  transfers between devices with their start and end apart: 42, of which 28 were waited for; matrix products, arithmetic and copies ran while one was open for 3% of the time, Pallas kernels for 18%

profile of v4, /device:TPU:1, one launch (start us, length us, event | category | flops | bytes accessed | tf_op | source)
XLA Modules:
  0.0 134.8 jit_solution(17861418419103807092)
XLA Ops:
  1.0 2.2 %collective-permute-start.2 = (bf16[128,256]{1,0:T(8,128)(2,1)S(1)}, bf16[128,256]{1,0:T(8,128)(2,1)S(1)}, u32[]{:S(2)}, u32[]{:S(2)}) collective-permute-start(bf16[128,256]{1,0:T(8,128)(2,1)S(1)} %fusion.2), channel_id=1, source_target_pairs={{0,192},{1,65},{2,194},{3,67},{4,196},{5,69},{6,198},{7,71},{8,200... | collective-permute-start | bytes 196616 | tf_op jit(solution)/shard_map/ppermute | solution.py:214
  3.2 1.9 %collective-permute-start.1 = (bf16[128,256]{1,0:T(8,128)(2,1)S(1)}, bf16[128,256]{1,0:T(8,128)(2,1)S(1)}, u32[]{:S(2)}, u32[]{:S(2)}) collective-permute-start(bf16[128,256]{1,0:T(8,128)(2,1)S(1)} %fusion.2), channel_id=1, source_target_pairs={{0,64},{1,193},{2,66},{3,195},{4,68},{5,197},{6,70},{7,199},{8,72}... | collective-permute-start | bytes 196616 | tf_op jit(solution)/shard_map/ppermute | solution.py:214
  6.8 2.2 %collective-permute-start.7 = (bf16[2,128,512]{2,1,0:T(8,128)(2,1)S(1)}, bf16[2,128,512]{2,1,0:T(8,128)(2,1)S(1)}, u32[]{:S(2)}, u32[]{:S(2)}) collective-permute-start(bf16[2,128,512]{2,1,0:T(8,128)(2,1)S(1)} %stack.123), channel_id=1, source_target_pairs={{0,64},{1,193},{2,66},{3,195},{4,68},{5,197},{6,70},{7,199},{8,72}... | collective-permute-start | bytes 786440 | tf_op jit(solution)/shard_map/ppermute | solution.py:214
  14.3 2.3 %collective-permute-start.5 = (bf16[2,128,256]{2,1,0:T(8,128)(2,1)S(1)}, bf16[2,128,256]{2,1,0:T(8,128)(2,1)S(1)}, u32[]{:S(2)}, u32[]{:S(2)}) collective-permute-start(bf16[2,128,256]{2,1,0:T(8,128)(2,1)S(1)} %maximum_select_fusion.refs_0_.refs_1_), channel_id=1, source_target_pairs={{4,0},{61,1},{6,2},{63,3},{8,4},{1,5},{10,6},{3,7},{12,8},{5,9},{1... | collective-permute-start | bytes 393224 | tf_op jit(solution)/shard_map/ppermute | solution.py:277
  16.6 1.6 %collective-permute-start.4 = (bf16[2,128,256]{2,1,0:T(8,128)(2,1)S(1)}, bf16[2,128,256]{2,1,0:T(8,128)(2,1)S(1)}, u32[]{:S(2)}, u32[]{:S(2)}) collective-permute-start(bf16[2,128,256]{2,1,0:T(8,128)(2,1)S(1)} %maximum_select_fusion.refs_0_.refs_1_), channel_id=1, source_target_pairs={{2,0},{63,1},{4,2},{1,3},{6,4},{3,5},{8,6},{5,7},{10,8},{7,9},{12,... | collective-permute-start | bytes 393224 | tf_op jit(solution)/shard_map/ppermute | solution.py:278
  18.2 1.6 %soon_fill.1.blocks_ref = bf16[1,17,512,128]{3,2,1,0:T(8,128)(2,1)S(1)} custom-call(bf16[5,17,512,128]{3,2,1,0:T(8,128)(2,1)} %factor_ref.1), custom_call_target="tpu_custom_call" | custom-call | flops 134217728 | bytes 2097152 | tf_op jit(solution)/shard_map/soon_fill/pallas_call | solution.py:202
  19.9 1.7 %table.4 = (s32[2,58]{1,0:T(2,128)S(1)}, f32[2,28]{1,0:T(2,128)S(1)}) custom-call(s32[5]{0:T(128)S(1)} %stack.118.meta_ref, s32[5,17]{1,0:T(8,128)S(1)} %copy-done.1, s32[5]{0:T(128)S(1)} %copy-done.3, f32[5,17]{1,0:T(8,128)S(1)} %copy-done.2), custom_call_target="tpu_custom_call" | custom-call | flops 134217728 | bytes 2097152 | tf_op jit(solution)/shard_map/table/pallas_call | solution.py:202
  24.2 2.3 %collective-permute-done.4 = bf16[2,128,256]{2,1,0:T(8,128)(2,1)S(1)} collective-permute-done((bf16[2,128,256]{2,1,0:T(8,128)(2,1)S(1)}, bf16[2,128,256]{2,1,0:T(8,128)(2,1)S(1)}, u32[]{:S(2)}, u32[]{:S(2)}) %collective-permute-start.4) | collective-permute-done | bytes 131104 | tf_op jit(solution)/shard_map/ppermute | solution.py:278
  29.6 3.9 %collective-permute-done.8 = bf16[2,128,512]{2,1,0:T(8,128)(2,1)S(1)} collective-permute-done((bf16[2,128,512]{2,1,0:T(8,128)(2,1)S(1)}, bf16[2,128,512]{2,1,0:T(8,128)(2,1)S(1)}, u32[]{:S(2)}, u32[]{:S(2)}) %collective-permute-start.8) | collective-permute-done | bytes 262176 | tf_op jit(solution)/shard_map/ppermute | solution.py:214
  34.6 3.5 %collective-permute-start.9 = (bf16[128,256]{1,0:T(8,128)(2,1)S(1)}, bf16[128,256]{1,0:T(8,128)(2,1)S(1)}, u32[]{:S(2)}, u32[]{:S(2)}) collective-permute-start(bf16[128,256]{1,0:T(8,128)(2,1)S(1)} %get-tuple-element.160), channel_id=1, source_target_pairs={{0,128},{1,129},{2,130},{3,131},{4,132},{5,133},{6,134},{7,135},{8... | collective-permute-start | bytes 196616 | tf_op jit(solution)/shard_map/ppermute | solution.py:214
  38.5 3.5 %late_fill.1.blocks_ref = bf16[4,17,512,128]{3,2,1,0:T(8,128)(2,1)S(1)} custom-call(bf16[5,17,512,128]{3,2,1,0:T(8,128)(2,1)} %factor_ref.1), custom_call_target="tpu_custom_call" | custom-call | flops 134217728 | bytes 2097152 | tf_op jit(solution)/shard_map/late_fill/pallas_call | solution.py:202
  42.6 2.3 %collective-permute-start.12 = (bf16[128,256]{1,0:T(8,128)(2,1)S(1)}, bf16[128,256]{1,0:T(8,128)(2,1)S(1)}, u32[]{:S(2)}, u32[]{:S(2)}) collective-permute-start(bf16[128,256]{1,0:T(8,128)(2,1)S(1)} %get-tuple-element.280), channel_id=1, source_target_pairs={{0,1},{1,0},{2,3},{3,2},{4,5},{5,4},{6,7},{7,6},{8,9},{9,8},{10,11... | collective-permute-start | bytes 196616 | tf_op jit(solution)/shard_map/ppermute | solution.py:217
  47.4 1.6 %early_slots.6 = (f32[512,256]{1,0:T(8,128)S(1)}, bf16[8,512,128]{2,1,0:T(8,128)(2,1)S(1)}, f32[8,1,256]{2,1,0:T(1,128)S(1)}) custom-call(s32[2,58]{1,0:T(2,128)S(1)} %get-tuple-element.147.index_ref, f32[2,28]{1,0:T(2,128)S(1)} %get-tuple-element.148.weight_ref, bf16[4,17,512,128]{3,2,1,0:T(8,128)(2,1)S(1)} %late_fill.1.blocks_ref, ...), custom_call_target="tpu_custom_call" | custom-call | flops 134217728 | bytes 2097152 | tf_op jit(solution)/shard_map/early_slots/pallas_call | solution.py:202
  49.0 5.1 %collective-permute-done.14 = bf16[2,128,256]{2,1,0:T(8,128)(2,1)S(1)} collective-permute-done((bf16[2,128,256]{2,1,0:T(8,128)(2,1)S(1)}, bf16[2,128,256]{2,1,0:T(8,128)(2,1)S(1)}, u32[]{:S(2)}, u32[]{:S(2)}) %collective-permute-start.14) | collective-permute-done | bytes 131104 | tf_op jit(solution)/shard_map/ppermute | solution.py:277
  54.1 2.4 %collective-permute-done.13 = bf16[2,128,256]{2,1,0:T(8,128)(2,1)S(1)} collective-permute-done((bf16[2,128,256]{2,1,0:T(8,128)(2,1)S(1)}, bf16[2,128,256]{2,1,0:T(8,128)(2,1)S(1)}, u32[]{:S(2)}, u32[]{:S(2)}) %collective-permute-start.13) | collective-permute-done | bytes 131104 | tf_op jit(solution)/shard_map/ppermute | solution.py:278
  56.5 2.2 %collective-permute-start.15 = (bf16[4,128,256]{2,1,0:T(8,128)(2,1)S(1)}, bf16[4,128,256]{2,1,0:T(8,128)(2,1)S(1)}, u32[]{:S(2)}, u32[]{:S(2)}) collective-permute-start(bf16[4,128,256]{2,1,0:T(8,128)(2,1)S(1)} %constant_dynamic-update-slice_fusion.2.mine_ref.refs_5_), channel_id=1, source_target_pairs={{0,1},{1,0},{2,3},{3,2},{4,5},{5,4},{6,7},{7,6},{8,9},{9,8},{10,11... | collective-permute-start | bytes 786440 | tf_op jit(solution)/shard_map/ppermute | solution.py:217
  61.0 1.7 %collective-permute-start.17 = (bf16[128,256]{1,0:T(8,128)(2,1)S(1)}, bf16[128,256]{1,0:T(8,128)(2,1)S(1)}, u32[]{:S(2)}, u32[]{:S(2)}) collective-permute-start(bf16[128,256]{1,0:T(8,128)(2,1)S(1)} %get-tuple-element.182), channel_id=1, source_target_pairs={{0,128},{1,129},{2,130},{3,131},{4,132},{5,133},{6,134},{7,135},{8... | collective-permute-start | bytes 196616 | tf_op jit(solution)/shard_map/ppermute | solution.py:214
  62.7 1.7 %collective-permute-start.18 = (bf16[128,256]{1,0:T(8,128)(2,1)S(1)}, bf16[128,256]{1,0:T(8,128)(2,1)S(1)}, u32[]{:S(2)}, u32[]{:S(2)}) collective-permute-start(bf16[128,256]{1,0:T(8,128)(2,1)S(1)} %get-tuple-element.183), channel_id=1, source_target_pairs={{0,64},{1,193},{2,66},{3,195},{4,68},{5,197},{6,70},{7,199},{8,72}... | collective-permute-start | bytes 196616 | tf_op jit(solution)/shard_map/ppermute | solution.py:214
  64.4 1.7 %table.5 = (s32[1,58]{1,0:T(1,128)S(1)}, f32[1,28]{1,0:T(1,128)S(1)}) custom-call(s32[5]{0:T(128)S(1)} %stack.118.meta_ref, s32[5,17]{1,0:T(8,128)S(1)} %copy-done.1, s32[5]{0:T(128)S(1)} %copy-done.3, f32[5,17]{1,0:T(8,128)S(1)} %copy-done.2), custom_call_target="tpu_custom_call" | custom-call | flops 134217728 | bytes 2097152 | tf_op jit(solution)/shard_map/table/pallas_call | solution.py:202
  67.4 1.9 %collective-permute-start.20 = (bf16[128,256]{1,0:T(8,128)(2,1)S(1)}, bf16[128,256]{1,0:T(8,128)(2,1)S(1)}, u32[]{:S(2)}, u32[]{:S(2)}) collective-permute-start(bf16[128,256]{1,0:T(8,128)(2,1)S(1)} %get-tuple-element.278), channel_id=1, source_target_pairs={{0,1},{1,0},{2,3},{3,2},{4,5},{5,4},{6,7},{7,6},{8,9},{9,8},{10,11... | collective-permute-start | bytes 196616 | tf_op jit(solution)/shard_map/ppermute | solution.py:217
  71.3 2.4 %early_slots.7 = (f32[512,256]{1,0:T(8,128)S(1)}, bf16[8,512,128]{2,1,0:T(8,128)(2,1)S(1)}, f32[8,1,256]{2,1,0:T(1,128)S(1)}) custom-call(s32[1,58]{1,0:T(1,128)S(1)} %get-tuple-element.190.index_ref, f32[1,28]{1,0:T(1,128)S(1)} %get-tuple-element.191.weight_ref, bf16[4,17,512,128]{3,2,1,0:T(8,128)(2,1)S(1)} %late_fill.1.blocks_ref, ...), custom_call_target="tpu_custom_call" | custom-call | flops 134217728 | bytes 2097152 | tf_op jit(solution)/shard_map/early_slots/pallas_call | solution.py:202
  73.8 6.7 %collective-permute-done.22 = bf16[2,128,256]{2,1,0:T(8,128)(2,1)S(1)} collective-permute-done((bf16[2,128,256]{2,1,0:T(8,128)(2,1)S(1)}, bf16[2,128,256]{2,1,0:T(8,128)(2,1)S(1)}, u32[]{:S(2)}, u32[]{:S(2)}) %collective-permute-start.22) | collective-permute-done | bytes 131104 | tf_op jit(solution)/shard_map/ppermute | solution.py:277
  83.7 1.8 %collective-permute-start.25 = (bf16[128,256]{1,0:T(8,128)(2,1)S(1)}, bf16[128,256]{1,0:T(8,128)(2,1)S(1)}, u32[]{:S(2)}, u32[]{:S(2)}) collective-permute-start(bf16[128,256]{1,0:T(8,128)(2,1)S(1)} %get-tuple-element.209), channel_id=1, source_target_pairs={{0,128},{1,129},{2,130},{3,131},{4,132},{5,133},{6,134},{7,135},{8... | collective-permute-start | bytes 196616 | tf_op jit(solution)/shard_map/ppermute | solution.py:214
  87.1 1.6 %table.6 = (s32[1,58]{1,0:T(1,128)S(1)}, f32[1,28]{1,0:T(1,128)S(1)}) custom-call(s32[5]{0:T(128)S(1)} %stack.118.meta_ref, s32[5,17]{1,0:T(8,128)S(1)} %copy-done.1, s32[5]{0:T(128)S(1)} %copy-done.3, f32[5,17]{1,0:T(8,128)S(1)} %copy-done.2), custom_call_target="tpu_custom_call" | custom-call | flops 134217728 | bytes 2097152 | tf_op jit(solution)/shard_map/table/pallas_call | solution.py:202
  90.2 2.0 %collective-permute-start.28 = (bf16[128,256]{1,0:T(8,128)(2,1)S(1)}, bf16[128,256]{1,0:T(8,128)(2,1)S(1)}, u32[]{:S(2)}, u32[]{:S(2)}) collective-permute-start(bf16[128,256]{1,0:T(8,128)(2,1)S(1)} %get-tuple-element.276), channel_id=1, source_target_pairs={{0,1},{1,0},{2,3},{3,2},{4,5},{5,4},{6,7},{7,6},{8,9},{9,8},{10,11... | collective-permute-start | bytes 196616 | tf_op jit(solution)/shard_map/ppermute | solution.py:217
  93.8 2.1 %early_slots.8 = (f32[512,256]{1,0:T(8,128)S(1)}, bf16[8,512,128]{2,1,0:T(8,128)(2,1)S(1)}, f32[8,1,256]{2,1,0:T(1,128)S(1)}) custom-call(s32[1,58]{1,0:T(1,128)S(1)} %get-tuple-element.217.index_ref, f32[1,28]{1,0:T(1,128)S(1)} %get-tuple-element.218.weight_ref, bf16[4,17,512,128]{3,2,1,0:T(8,128)(2,1)S(1)} %late_fill.1.blocks_ref, ...), custom_call_target="tpu_custom_call" | custom-call | flops 134217728 | bytes 2097152 | tf_op jit(solution)/shard_map/early_slots/pallas_call | solution.py:202
  95.8 7.1 %collective-permute-done.30 = bf16[2,128,256]{2,1,0:T(8,128)(2,1)S(1)} collective-permute-done((bf16[2,128,256]{2,1,0:T(8,128)(2,1)S(1)}, bf16[2,128,256]{2,1,0:T(8,128)(2,1)S(1)}, u32[]{:S(2)}, u32[]{:S(2)}) %collective-permute-start.30) | collective-permute-done | bytes 131104 | tf_op jit(solution)/shard_map/ppermute | solution.py:277
  109.4 1.7 %table.7 = (s32[1,58]{1,0:T(1,128)S(1)}, f32[1,28]{1,0:T(1,128)S(1)}) custom-call(s32[5]{0:T(128)S(1)} %stack.118.meta_ref, s32[5,17]{1,0:T(8,128)S(1)} %copy-done.1, s32[5]{0:T(128)S(1)} %copy-done.3, f32[5,17]{1,0:T(8,128)S(1)} %copy-done.2), custom_call_target="tpu_custom_call" | custom-call | flops 134217728 | bytes 2097152 | tf_op jit(solution)/shard_map/table/pallas_call | solution.py:202
  111.5 1.9 %collective-permute-done.33 = bf16[128,256]{1,0:T(8,128)(2,1)S(1)} collective-permute-done((bf16[128,256]{1,0:T(8,128)(2,1)S(1)}, bf16[128,256]{1,0:T(8,128)(2,1)S(1)}, u32[]{:S(2)}, u32[]{:S(2)}) %collective-permute-start.33) | collective-permute-done | bytes 65568 | tf_op jit(solution)/shard_map/ppermute | solution.py:214
  115.5 2.1 %early_slots.9 = (f32[512,256]{1,0:T(8,128)S(1)}, bf16[8,512,128]{2,1,0:T(8,128)(2,1)S(1)}, f32[8,1,256]{2,1,0:T(1,128)S(1)}) custom-call(s32[1,58]{1,0:T(1,128)S(1)} %get-tuple-element.246.index_ref, f32[1,28]{1,0:T(1,128)S(1)} %get-tuple-element.247.weight_ref, bf16[4,17,512,128]{3,2,1,0:T(8,128)(2,1)S(1)} %late_fill.1.blocks_ref, ...), custom_call_target="tpu_custom_call" | custom-call | flops 134217728 | bytes 2097152 | tf_op jit(solution)/shard_map/early_slots/pallas_call | solution.py:202
  117.6 6.9 %collective-permute-done.37 = bf16[2,128,256]{2,1,0:T(8,128)(2,1)S(1)} collective-permute-done((bf16[2,128,256]{2,1,0:T(8,128)(2,1)S(1)}, bf16[2,128,256]{2,1,0:T(8,128)(2,1)S(1)}, u32[]{:S(2)}, u32[]{:S(2)}) %collective-permute-start.37) | collective-permute-done | bytes 131104 | tf_op jit(solution)/shard_map/ppermute | solution.py:277
  130.6 2.0 %collective-permute-done.39 = bf16[128,256]{1,0:T(8,128)(2,1)S(1)} collective-permute-done((bf16[128,256]{1,0:T(8,128)(2,1)S(1)}, bf16[128,256]{1,0:T(8,128)(2,1)S(1)}, u32[]{:S(2)}, u32[]{:S(2)}) %collective-permute-start.39) | collective-permute-done | bytes 65568 | tf_op jit(solution)/shard_map/ppermute | solution.py:214
  (122 shorter events, 48.7 us)
Async XLA Ops:
  1.0 10.9 %collective-permute-start.2 = (bf16[128,256]{1,0:T(8,128)(2,1)S(1)}, bf16[128,256]{1,0:T(8,128)(2,1)S(1)}, u32[]{:S(2)}, u32[]{:S(2)}) collective-permute-start(bf16[128,256]{1,0:T(8,128)(2,1)S(1)} %fusion.2), channel_id=1, source_target_pairs={{0,192},{1,65},{2,194},{3,67},{4,196},{5,69},{6,198},{7,71},{8,200... | collective-permute-start | bytes 196616 | tf_op jit(solution)/shard_map/ppermute | solution.py:214
  3.2 8.7 %collective-permute-start.1 = (bf16[128,256]{1,0:T(8,128)(2,1)S(1)}, bf16[128,256]{1,0:T(8,128)(2,1)S(1)}, u32[]{:S(2)}, u32[]{:S(2)}) collective-permute-start(bf16[128,256]{1,0:T(8,128)(2,1)S(1)} %fusion.2), channel_id=1, source_target_pairs={{0,64},{1,193},{2,66},{3,195},{4,68},{5,197},{6,70},{7,199},{8,72}... | collective-permute-start | bytes 196616 | tf_op jit(solution)/shard_map/ppermute | solution.py:214
  5.1 6.8 %collective-permute-start = (bf16[128,256]{1,0:T(8,128)(2,1)S(1)}, bf16[128,256]{1,0:T(8,128)(2,1)S(1)}, u32[]{:S(2)}, u32[]{:S(2)}) collective-permute-start(bf16[128,256]{1,0:T(8,128)(2,1)S(1)} %fusion.2), channel_id=1, source_target_pairs={{0,128},{1,129},{2,130},{3,131},{4,132},{5,133},{6,134},{7,135},{8... | collective-permute-start | bytes 196616 | tf_op jit(solution)/shard_map/ppermute | solution.py:214
  6.8 15.9 %collective-permute-start.7 = (bf16[2,128,512]{2,1,0:T(8,128)(2,1)S(1)}, bf16[2,128,512]{2,1,0:T(8,128)(2,1)S(1)}, u32[]{:S(2)}, u32[]{:S(2)}) collective-permute-start(bf16[2,128,512]{2,1,0:T(8,128)(2,1)S(1)} %stack.123), channel_id=1, source_target_pairs={{0,64},{1,193},{2,66},{3,195},{4,68},{5,197},{6,70},{7,199},{8,72}... | collective-permute-start | bytes 786440 | tf_op jit(solution)/shard_map/ppermute | solution.py:214
  14.3 10.0 %collective-permute-start.5 = (bf16[2,128,256]{2,1,0:T(8,128)(2,1)S(1)}, bf16[2,128,256]{2,1,0:T(8,128)(2,1)S(1)}, u32[]{:S(2)}, u32[]{:S(2)}) collective-permute-start(bf16[2,128,256]{2,1,0:T(8,128)(2,1)S(1)} %maximum_select_fusion.refs_0_.refs_1_), channel_id=1, source_target_pairs={{4,0},{61,1},{6,2},{63,3},{8,4},{1,5},{10,6},{3,7},{12,8},{5,9},{1... | collective-permute-start | bytes 393224 | tf_op jit(solution)/shard_map/ppermute | solution.py:277
  16.6 9.9 %collective-permute-start.4 = (bf16[2,128,256]{2,1,0:T(8,128)(2,1)S(1)}, bf16[2,128,256]{2,1,0:T(8,128)(2,1)S(1)}, u32[]{:S(2)}, u32[]{:S(2)}) collective-permute-start(bf16[2,128,256]{2,1,0:T(8,128)(2,1)S(1)} %maximum_select_fusion.refs_0_.refs_1_), channel_id=1, source_target_pairs={{2,0},{63,1},{4,2},{1,3},{6,4},{3,5},{8,6},{5,7},{10,8},{7,9},{12,... | collective-permute-start | bytes 393224 | tf_op jit(solution)/shard_map/ppermute | solution.py:278
  27.9 5.5 %collective-permute-start.8 = (bf16[2,128,512]{2,1,0:T(8,128)(2,1)S(1)}, bf16[2,128,512]{2,1,0:T(8,128)(2,1)S(1)}, u32[]{:S(2)}, u32[]{:S(2)}) collective-permute-start(bf16[2,128,512]{2,1,0:T(8,128)(2,1)S(1)} %pad_maximum_fusion.2), channel_id=1, source_target_pairs={{0,192},{1,65},{2,194},{3,67},{4,196},{5,69},{6,198},{7,71},{8,200... | collective-permute-start | bytes 786440 | tf_op jit(solution)/shard_map/ppermute | solution.py:214
  34.6 7.4 %collective-permute-start.9 = (bf16[128,256]{1,0:T(8,128)(2,1)S(1)}, bf16[128,256]{1,0:T(8,128)(2,1)S(1)}, u32[]{:S(2)}, u32[]{:S(2)}) collective-permute-start(bf16[128,256]{1,0:T(8,128)(2,1)S(1)} %get-tuple-element.160), channel_id=1, source_target_pairs={{0,128},{1,129},{2,130},{3,131},{4,132},{5,133},{6,134},{7,135},{8... | collective-permute-start | bytes 196616 | tf_op jit(solution)/shard_map/ppermute | solution.py:214
  38.1 3.9 %collective-permute-start.11 = (bf16[128,256]{1,0:T(8,128)(2,1)S(1)}, bf16[128,256]{1,0:T(8,128)(2,1)S(1)}, u32[]{:S(2)}, u32[]{:S(2)}) collective-permute-start(bf16[128,256]{1,0:T(8,128)(2,1)S(1)} %get-tuple-element.162), channel_id=1, source_target_pairs={{0,192},{1,65},{2,194},{3,67},{4,196},{5,69},{6,198},{7,71},{8,200... | collective-permute-start | bytes 196616 | tf_op jit(solution)/shard_map/ppermute | solution.py:214
  38.1 4.5 %collective-permute-start.10 = (bf16[128,256]{1,0:T(8,128)(2,1)S(1)}, bf16[128,256]{1,0:T(8,128)(2,1)S(1)}, u32[]{:S(2)}, u32[]{:S(2)}) collective-permute-start(bf16[128,256]{1,0:T(8,128)(2,1)S(1)} %get-tuple-element.161), channel_id=1, source_target_pairs={{0,64},{1,193},{2,66},{3,195},{4,68},{5,197},{6,70},{7,199},{8,72}... | collective-permute-start | bytes 196616 | tf_op jit(solution)/shard_map/ppermute | solution.py:214
  45.0 14.9 %collective-permute-start.16 = (bf16[5,128,512]{2,1,0:T(8,128)(2,1)S(1)}, bf16[5,128,512]{2,1,0:T(8,128)(2,1)S(1)}, u32[]{:S(2)}, u32[]{:S(2)}) collective-permute-start(bf16[5,128,512]{2,1,0:T(8,128)(2,1)S(1)} %pad_maximum_fusion.1), channel_id=1, source_target_pairs={{0,192},{1,65},{2,194},{3,67},{4,196},{5,69},{6,198},{7,71},{8,200... | collective-permute-start | bytes 1966088 | tf_op jit(solution)/shard_map/ppermute | solution.py:214
  45.8 8.2 %collective-permute-start.14 = (bf16[2,128,256]{2,1,0:T(8,128)(2,1)S(1)}, bf16[2,128,256]{2,1,0:T(8,128)(2,1)S(1)}, u32[]{:S(2)}, u32[]{:S(2)}) collective-permute-start(bf16[2,128,256]{2,1,0:T(8,128)(2,1)S(1)} %maximum_select_fusion.1.refs_0_.refs_4_), channel_id=1, source_target_pairs={{4,0},{61,1},{6,2},{63,3},{8,4},{1,5},{10,6},{3,7},{12,8},{5,9},{1... | collective-permute-start | bytes 393224 | tf_op jit(solution)/shard_map/ppermute | solution.py:277
  47.4 9.1 %collective-permute-start.13 = (bf16[2,128,256]{2,1,0:T(8,128)(2,1)S(1)}, bf16[2,128,256]{2,1,0:T(8,128)(2,1)S(1)}, u32[]{:S(2)}, u32[]{:S(2)}) collective-permute-start(bf16[2,128,256]{2,1,0:T(8,128)(2,1)S(1)} %maximum_select_fusion.1.refs_0_.refs_4_), channel_id=1, source_target_pairs={{2,0},{63,1},{4,2},{1,3},{6,4},{3,5},{8,6},{5,7},{10,8},{7,9},{12,... | collective-permute-start | bytes 393224 | tf_op jit(solution)/shard_map/ppermute | solution.py:278
  61.0 5.1 %collective-permute-start.17 = (bf16[128,256]{1,0:T(8,128)(2,1)S(1)}, bf16[128,256]{1,0:T(8,128)(2,1)S(1)}, u32[]{:S(2)}, u32[]{:S(2)}) collective-permute-start(bf16[128,256]{1,0:T(8,128)(2,1)S(1)} %get-tuple-element.182), channel_id=1, source_target_pairs={{0,128},{1,129},{2,130},{3,131},{4,132},{5,133},{6,134},{7,135},{8... | collective-permute-start | bytes 196616 | tf_op jit(solution)/shard_map/ppermute | solution.py:214
  62.7 4.7 %collective-permute-start.18 = (bf16[128,256]{1,0:T(8,128)(2,1)S(1)}, bf16[128,256]{1,0:T(8,128)(2,1)S(1)}, u32[]{:S(2)}, u32[]{:S(2)}) collective-permute-start(bf16[128,256]{1,0:T(8,128)(2,1)S(1)} %get-tuple-element.183), channel_id=1, source_target_pairs={{0,64},{1,193},{2,66},{3,195},{4,68},{5,197},{6,70},{7,199},{8,72}... | collective-permute-start | bytes 196616 | tf_op jit(solution)/shard_map/ppermute | solution.py:214
  67.4 3.4 %collective-permute-start.20 = (bf16[128,256]{1,0:T(8,128)(2,1)S(1)}, bf16[128,256]{1,0:T(8,128)(2,1)S(1)}, u32[]{:S(2)}, u32[]{:S(2)}) collective-permute-start(bf16[128,256]{1,0:T(8,128)(2,1)S(1)} %get-tuple-element.278), channel_id=1, source_target_pairs={{0,1},{1,0},{2,3},{3,2},{4,5},{5,4},{6,7},{7,6},{8,9},{9,8},{10,11... | collective-permute-start | bytes 196616 | tf_op jit(solution)/shard_map/ppermute | solution.py:217
  69.4 13.2 %collective-permute-start.24 = (bf16[6,128,512]{2,1,0:T(8,128)(2,1)S(1)}, bf16[6,128,512]{2,1,0:T(8,128)(2,1)S(1)}, u32[]{:S(2)}, u32[]{:S(2)}) collective-permute-start(bf16[6,128,512]{2,1,0:T(8,128)(2,1)S(1)} %pad_maximum_fusion), channel_id=1, source_target_pairs={{0,64},{1,193},{2,66},{3,195},{4,68},{5,197},{6,70},{7,199},{8,72}... | collective-permute-start | bytes 2359304 | tf_op jit(solution)/shard_map/ppermute | solution.py:214
  70.9 9.7 %collective-permute-start.22 = (bf16[2,128,256]{2,1,0:T(8,128)(2,1)S(1)}, bf16[2,128,256]{2,1,0:T(8,128)(2,1)S(1)}, u32[]{:S(2)}, u32[]{:S(2)}) collective-permute-start(bf16[2,128,256]{2,1,0:T(8,128)(2,1)S(1)} %maximum_select_fusion.2.refs_0_.refs_7_), channel_id=1, source_target_pairs={{4,0},{61,1},{6,2},{63,3},{8,4},{1,5},{10,6},{3,7},{12,8},{5,9},{1... | collective-permute-start | bytes 393224 | tf_op jit(solution)/shard_map/ppermute | solution.py:277
  71.0 9.9 %collective-permute-start.21 = (bf16[2,128,256]{2,1,0:T(8,128)(2,1)S(1)}, bf16[2,128,256]{2,1,0:T(8,128)(2,1)S(1)}, u32[]{:S(2)}, u32[]{:S(2)}) collective-permute-start(bf16[2,128,256]{2,1,0:T(8,128)(2,1)S(1)} %maximum_select_fusion.2.refs_0_.refs_7_), channel_id=1, source_target_pairs={{2,0},{63,1},{4,2},{1,3},{6,4},{3,5},{8,6},{5,7},{10,8},{7,9},{12,... | collective-permute-start | bytes 393224 | tf_op jit(solution)/shard_map/ppermute | solution.py:278
  83.7 5.0 %collective-permute-start.25 = (bf16[128,256]{1,0:T(8,128)(2,1)S(1)}, bf16[128,256]{1,0:T(8,128)(2,1)S(1)}, u32[]{:S(2)}, u32[]{:S(2)}) collective-permute-start(bf16[128,256]{1,0:T(8,128)(2,1)S(1)} %get-tuple-element.209), channel_id=1, source_target_pairs={{0,128},{1,129},{2,130},{3,131},{4,132},{5,133},{6,134},{7,135},{8... | collective-permute-start | bytes 196616 | tf_op jit(solution)/shard_map/ppermute | solution.py:214
  85.6 3.7 %collective-permute-start.27 = (bf16[128,256]{1,0:T(8,128)(2,1)S(1)}, bf16[128,256]{1,0:T(8,128)(2,1)S(1)}, u32[]{:S(2)}, u32[]{:S(2)}) collective-permute-start(bf16[128,256]{1,0:T(8,128)(2,1)S(1)} %get-tuple-element.211), channel_id=1, source_target_pairs={{0,192},{1,65},{2,194},{3,67},{4,196},{5,69},{6,198},{7,71},{8,200... | collective-permute-start | bytes 196616 | tf_op jit(solution)/shard_map/ppermute | solution.py:214
  85.8 4.4 %collective-permute-start.26 = (bf16[128,256]{1,0:T(8,128)(2,1)S(1)}, bf16[128,256]{1,0:T(8,128)(2,1)S(1)}, u32[]{:S(2)}, u32[]{:S(2)}) collective-permute-start(bf16[128,256]{1,0:T(8,128)(2,1)S(1)} %get-tuple-element.210), channel_id=1, source_target_pairs={{0,64},{1,193},{2,66},{3,195},{4,68},{5,197},{6,70},{7,199},{8,72}... | collective-permute-start | bytes 196616 | tf_op jit(solution)/shard_map/ppermute | solution.py:214
  93.1 9.8 %collective-permute-start.30 = (bf16[2,128,256]{2,1,0:T(8,128)(2,1)S(1)}, bf16[2,128,256]{2,1,0:T(8,128)(2,1)S(1)}, u32[]{:S(2)}, u32[]{:S(2)}) collective-permute-start(bf16[2,128,256]{2,1,0:T(8,128)(2,1)S(1)} %maximum_select_fusion.3.refs_0_.refs_10_), channel_id=1, source_target_pairs={{4,0},{61,1},{6,2},{63,3},{8,4},{1,5},{10,6},{3,7},{12,8},{5,9},{1... | collective-permute-start | bytes 393224 | tf_op jit(solution)/shard_map/ppermute | solution.py:277
  93.4 9.9 %collective-permute-start.29 = (bf16[2,128,256]{2,1,0:T(8,128)(2,1)S(1)}, bf16[2,128,256]{2,1,0:T(8,128)(2,1)S(1)}, u32[]{:S(2)}, u32[]{:S(2)}) collective-permute-start(bf16[2,128,256]{2,1,0:T(8,128)(2,1)S(1)} %maximum_select_fusion.3.refs_0_.refs_10_), channel_id=1, source_target_pairs={{2,0},{63,1},{4,2},{1,3},{6,4},{3,5},{8,6},{5,7},{10,8},{7,9},{12,... | collective-permute-start | bytes 393224 | tf_op jit(solution)/shard_map/ppermute | solution.py:278
  106.1 5.1 %collective-permute-start.32 = (bf16[128,256]{1,0:T(8,128)(2,1)S(1)}, bf16[128,256]{1,0:T(8,128)(2,1)S(1)}, u32[]{:S(2)}, u32[]{:S(2)}) collective-permute-start(bf16[128,256]{1,0:T(8,128)(2,1)S(1)} %get-tuple-element.238), channel_id=1, source_target_pairs={{0,128},{1,129},{2,130},{3,131},{4,132},{5,133},{6,134},{7,135},{8... | collective-permute-start | bytes 196616 | tf_op jit(solution)/shard_map/ppermute | solution.py:214
  107.1 4.5 %collective-permute-start.34 = (bf16[128,256]{1,0:T(8,128)(2,1)S(1)}, bf16[128,256]{1,0:T(8,128)(2,1)S(1)}, u32[]{:S(2)}, u32[]{:S(2)}) collective-permute-start(bf16[128,256]{1,0:T(8,128)(2,1)S(1)} %get-tuple-element.240), channel_id=1, source_target_pairs={{0,192},{1,65},{2,194},{3,67},{4,196},{5,69},{6,198},{7,71},{8,200... | collective-permute-start | bytes 196616 | tf_op jit(solution)/shard_map/ppermute | solution.py:214
  108.2 5.3 %collective-permute-start.33 = (bf16[128,256]{1,0:T(8,128)(2,1)S(1)}, bf16[128,256]{1,0:T(8,128)(2,1)S(1)}, u32[]{:S(2)}, u32[]{:S(2)}) collective-permute-start(bf16[128,256]{1,0:T(8,128)(2,1)S(1)} %get-tuple-element.239), channel_id=1, source_target_pairs={{0,64},{1,193},{2,66},{3,195},{4,68},{5,197},{6,70},{7,199},{8,72}... | collective-permute-start | bytes 196616 | tf_op jit(solution)/shard_map/ppermute | solution.py:214
  114.9 9.6 %collective-permute-start.37 = (bf16[2,128,256]{2,1,0:T(8,128)(2,1)S(1)}, bf16[2,128,256]{2,1,0:T(8,128)(2,1)S(1)}, u32[]{:S(2)}, u32[]{:S(2)}) collective-permute-start(bf16[2,128,256]{2,1,0:T(8,128)(2,1)S(1)} %maximum_select_fusion.4.refs_0_), channel_id=1, source_target_pairs={{4,0},{61,1},{6,2},{63,3},{8,4},{1,5},{10,6},{3,7},{12,8},{5,9},{1... | collective-permute-start | bytes 393224 | tf_op jit(solution)/shard_map/ppermute | solution.py:277
  115.0 10.1 %collective-permute-start.36 = (bf16[2,128,256]{2,1,0:T(8,128)(2,1)S(1)}, bf16[2,128,256]{2,1,0:T(8,128)(2,1)S(1)}, u32[]{:S(2)}, u32[]{:S(2)}) collective-permute-start(bf16[2,128,256]{2,1,0:T(8,128)(2,1)S(1)} %maximum_select_fusion.4.refs_0_), channel_id=1, source_target_pairs={{2,0},{63,1},{4,2},{1,3},{6,4},{3,5},{8,6},{5,7},{10,8},{7,9},{12,... | collective-permute-start | bytes 393224 | tf_op jit(solution)/shard_map/ppermute | solution.py:278
  127.8 4.7 %collective-permute-start.39 = (bf16[128,256]{1,0:T(8,128)(2,1)S(1)}, bf16[128,256]{1,0:T(8,128)(2,1)S(1)}, u32[]{:S(2)}, u32[]{:S(2)}) collective-permute-start(bf16[128,256]{1,0:T(8,128)(2,1)S(1)} %get-tuple-element.270), channel_id=1, source_target_pairs={{0,128},{1,129},{2,130},{3,131},{4,132},{5,133},{6,134},{7,135},{8... | collective-permute-start | bytes 196616 | tf_op jit(solution)/shard_map/ppermute | solution.py:214
  129.0 5.0 %collective-permute-start.40 = (bf16[128,256]{1,0:T(8,128)(2,1)S(1)}, bf16[128,256]{1,0:T(8,128)(2,1)S(1)}, u32[]{:S(2)}, u32[]{:S(2)}) collective-permute-start(bf16[128,256]{1,0:T(8,128)(2,1)S(1)} %get-tuple-element.271), channel_id=1, source_target_pairs={{0,64},{1,193},{2,66},{3,195},{4,68},{5,197},{6,70},{7,199},{8,72}... | collective-permute-start | bytes 196616 | tf_op jit(solution)/shard_map/ppermute | solution.py:214
  130.3 3.8 %collective-permute-start.41 = (bf16[128,256]{1,0:T(8,128)(2,1)S(1)}, bf16[128,256]{1,0:T(8,128)(2,1)S(1)}, u32[]{:S(2)}, u32[]{:S(2)}) collective-permute-start(bf16[128,256]{1,0:T(8,128)(2,1)S(1)} %get-tuple-element.272), channel_id=1, source_target_pairs={{0,192},{1,65},{2,194},{3,67},{4,196},{5,69},{6,198},{7,71},{8,200... | collective-permute-start | bytes 196616 | tf_op jit(solution)/shard_map/ppermute | solution.py:214
  (16 other events, 133.6 us)
